TPU v7x, 32 devices: a whole 2x2x4 slice. The times are simulated.
32 devices in a mesh: group: 2 (over x), tensor: 16 (over z, y, core).
Axes of the slice: x: 2, y: 2, z: 4, core: 2. Of those that a mesh axis runs over, the one named last changes fastest.
Arguments:
- three_center: bfloat16 [32, 8, 4096, 128], P(('group', 'tensor')), parts along dimension 0, may hold values from -0.1875 to 0.1875
- occ_green: bfloat16 [16, 512, 512], P('tensor'), may hold values from -0.25 to 0.25
- virt_green: bfloat16 [16, 512, 512], P('tensor'), may hold values from -0.25 to 0.25
- neighbors: int32 [16, 8], replicated, may hold values from -1 to 15, as said below
Outputs:
- polarization: float32 [256, 128], P(('group', 'tensor')), parts along dimension 0
There are 2 independent parts, one for each index of `group`. A program takes and returns all parts, laid end to end along the dimension named above; an argument that names none is the same for every part. Nothing has to cross between parts.
Inputs may be any that keep to these rules, and one draw needn't show every extreme that they name: neighbors[a, k] is either -1 (an empty slot) or the molecule a XOR k; neighbors[a, 0] = a; whenever neighbors[a, k] = b >= 0, also neighbors[b, k] = a; some molecule has all 8 slots filled.
All inputs are finite; a program needn't handle non-finite values.
Results may differ from a plain program's by a relative error of at most 0.0041.
Values may be sent and summed in bfloat16 or wider, within the bound.
No kernel may reach another device: no remote copies, remote signals or barrier semaphores. Data moves between devices by JAX's collectives and lax.ppermute only.
A program may use at most 128 MiB of HBM per device.

v0:
```python
import jax
import jax.numpy as jnp
from jax import lax
from jax.sharding import PartitionSpec as P


def spread_return(block_rows, neighbors):
    spread = lax.all_to_all(block_rows, "tensor", split_axis=2, concat_axis=0, tiled=True)
    molecules, slot_count = neighbors.shape
    live_all = neighbors >= 0
    source = (
        jnp.where(live_all, neighbors, 0) * slot_count
        + jnp.arange(slot_count, dtype=jnp.int32)[None, :]
    )
    flat_rows = spread.reshape(molecules * slot_count, spread.shape[2], spread.shape[3])
    permuted = jnp.take(flat_rows, source.reshape(-1), axis=0)
    permuted = jnp.where(
        live_all.reshape(-1)[:, None, None], permuted, jnp.zeros((), permuted.dtype)
    )
    permuted = permuted.reshape(molecules, slot_count, spread.shape[2], spread.shape[3])
    return lax.all_to_all(permuted, "tensor", split_axis=0, concat_axis=2, tiled=True)


def relayout(block_rows, neighbors):
    return spread_return(block_rows, neighbors)


def virtual_side(blocks, virt_grid, flat_shape):
    products = jnp.einsum(
        "amilp,amlkj->akijp", blocks, virt_grid, preferred_element_type=jnp.float32
    )
    return products.astype(jnp.bfloat16).reshape(flat_shape)


def occupied_side(blocks, occ_grid, flat_shape):
    projected = jnp.einsum(
        "amxny,anzyq->amxzq", occ_grid, blocks, preferred_element_type=jnp.float32
    )
    return projected.astype(jnp.bfloat16).reshape(flat_shape)


def local(three_center, occ_green, virt_green, neighbors):
    own_count, slot_count, pair_count, ri_count = three_center.shape
    block_width = occ_green.shape[1] // slot_count
    offset_row = lax.axis_index("tensor") * own_count
    own_neighbors = lax.dynamic_slice_in_dim(neighbors, offset_row, own_count, 0)
    own_live = own_neighbors >= 0
    masked = jnp.where(own_live[:, :, None, None], three_center, jnp.zeros((), three_center.dtype))
    blocks = masked.reshape(own_count, slot_count, block_width, block_width, ri_count)
    grid_shape = (own_count, slot_count, block_width, slot_count, block_width)
    occ_grid = occ_green.reshape(grid_shape)
    virt_grid = virt_green.reshape(grid_shape)
    product_side = relayout(virtual_side(blocks, virt_grid, three_center.shape), neighbors)
    project_side = occupied_side(blocks, occ_grid, three_center.shape)
    product_rows = product_side.reshape(-1, ri_count)
    project_rows = project_side.reshape(-1, ri_count)
    return lax.psum_scatter(
        jnp.einsum("rp,rq->pq", product_rows, project_rows, preferred_element_type=jnp.float32),
        "tensor",
        scatter_dimension=0,
        tiled=True,
    )


def solution(mesh):
    in_specs = (
        P(("group", "tensor"), None, None, None),
        P("tensor", None, None),
        P("tensor", None, None),
        P(),
    )
    out_specs = P(("group", "tensor"), None)
    return jax.shard_map(local, mesh=mesh, in_specs=in_specs, out_specs=out_specs, check_vma=False)
```

profile of v0, /device:TPU:0, one launch (start us, length us, event | category | flops | bytes accessed | tf_op | source)
XLA Modules:
  0.0 566.0 jit_solution(13452020094126954196)
XLA Ops:
  6.5 1.6 reshape.80
  8.2 0.9 copy.35
  9.1 0.9 fusion.11
  9.9 7.2 %broadcast_select_fusion = bf16[1,8,4096,128]{3,2,1,0:T(8,128)(2,1)} fusion(bf16[1,8,4096,128]{3,2,1,0:T(8,128)(2,1)} %param.4, pred[8]{0:T(512)(128)(4,1)S(1)} %fusion.11), kind=kLoop, calls=%fused_computation.4 | loop fusion | flops 4194304 | bytes 16777224 | tf_op jit(solution)/shard_map/jit(_where)/select_n | solution.py:48
  17.2 9.4 %fusion.2 = bf16[1,8,64,64,128]{4,3,1,2,0:T(8,128)(2,1)} fusion(bf16[8,64,64,128,1]{3,2,1,0,4:T(8,128)(2,1)} %bitcast.51, bf16[8,64,8,64]{1,3,0,2:T(8,128)(2,1)S(1)} %copy.35), kind=kOutput, calls=%fused_computation.7 | convolution fusion | flops 4299161600 | bytes 17301504 | tf_op jit(solution)/shard_map/amilp,amlkj->akijp/dot_general | solution.py:29
  26.6 9.5 %copy.36 = bf16[1,8,64,64,128]{4,3,2,1,0:T(8,128)(2,1)} copy(bf16[1,8,64,64,128]{4,3,1,2,0:T(8,128)(2,1)} %fusion.2) | data formatting | bytes 16777216 | tf_op jit(solution)/shard_map/convert_element_type | solution.py:32
  36.0 10.4 %copy.37 = bf16[1,8,4096,128]{3,1,0,2:T(8,128)(2,1)} copy(bf16[1,8,4096,128]{3,2,1,0:T(8,128)(2,1)} %bitcast.49) | data formatting | bytes 16777216 | tf_op jit(solution)/shard_map/reshape | solution.py:32
  46.4 7.6 %all-to-all-start = ((bf16[1,8,4096,128]{3,1,0,2:T(8,128)(2,1)}), bf16[1,8,4096,128]{3,1,0,2:T(8,128)(2,1)}, u32[]{:S(2)}, u32[]{:S(2)}) async-start(bf16[1,8,4096,128]{3,1,0,2:T(8,128)(2,1)} %copy.37), calls=%async_computation | async-start | bytes 16777216 | tf_op jit(solution)/shard_map/all_to_all | solution.py:8
  54.0 0.0 copy-done.1
  54.0 0.1 copy.40
  54.1 0.1 reshape.83
  54.2 0.1 copy.32
  54.3 0.1 copy.33
  54.4 150.3 %all-to-all-done = bf16[1,8,4096,128]{3,1,0,2:T(8,128)(2,1)} async-done(((bf16[1,8,4096,128]{3,1,0,2:T(8,128)(2,1)}), bf16[1,8,4096,128]{3,1,0,2:T(8,128)(2,1)}, u32[]{:S(2)}, u32[]{:S(2)}) %all-to-all-start) | async-done | bytes 8388640 | tf_op jit(solution)/shard_map/all_to_all | solution.py:8
  204.7 7.7 %copy.38 = bf16[1,8,4096,128]{3,2,1,0:T(8,128)(2,1)} copy(bf16[1,8,4096,128]{3,1,0,2:T(8,128)(2,1)} %all-to-all-done) | data formatting | bytes 16777216 | tf_op jit(solution)/shard_map/all_to_all | solution.py:8
  212.4 7.7 %copy.39 = bf16[16,1,8,256,128]{4,3,2,0,1:T(8,128)(2,1)} copy(bf16[16,1,8,256,128]{4,3,0,2,1:T(8,128)(2,1)} %bitcast.50) | data formatting | bytes 16777216 | tf_op jit(solution)/shard_map/all_to_all | solution.py:8
  220.1 9.9 %gather_fusion = bf16[128,256,128]{2,1,0:T(8,128)(2,1)} fusion(bf16[128,256,128]{2,1,0:T(8,128)(2,1)} %bitcast.48, s32[1024]{0:T(1024)S(1)} %pad_clamp_fusion), kind=kCustom, calls=%fused_computation | custom fusion | bytes 16777728 | tf_op jit(solution)/shard_map/jit(_take)/gather | solution.py:16
  230.0 7.4 %select_select_fusion = bf16[16,8,256,128]{3,2,1,0:T(8,128)(2,1)} fusion(bf16[16,8,256,128]{3,2,1,0:T(8,128)(2,1)} %bitcast.47, pred[16,8]{1,0:T(8,128)(4,1)S(1)} %copy.33, pred[16,8]{1,0:T(8,128)(4,1)S(1)} %copy.32), kind=kLoop, calls=%fused_computation.3 | loop fusion | flops 8388608 | bytes 16777472 | tf_op jit(solution)/shard_map/jit(_where)/select_n | solution.py:17
  237.4 36.7 %all-to-all-start.1 = ((bf16[16,8,256,128]{3,2,1,0:T(8,128)(2,1)}), bf16[16,8,256,128]{3,2,1,0:T(8,128)(2,1)}, u32[]{:S(2)}, u32[]{:S(2)}) async-start(bf16[16,8,256,128]{3,2,1,0:T(8,128)(2,1)} %select_select_fusion), calls=%async_computation.1 | async-start | bytes 16777216 | tf_op jit(solution)/shard_map/all_to_all | solution.py:21
  274.1 0.2 all-reduce.3.cloned.1.call-start
  274.4 0.0 copy-done
  274.4 0.5 reshape.85
  274.9 9.4 %fusion.5 = bf16[8,64,64,128]{3,1,0,2:T(8,128)(2,1)} fusion(bf16[8,64,64,128,1]{3,2,1,0,4:T(8,128)(2,1)} %bitcast.52, bf16[8,64,8,64]{3,2,1,0:T(8,128)(2,1)S(1)} %reshape.85), kind=kOutput, calls=%fused_computation.8 | convolution fusion | flops 4299161600 | bytes 17301504 | tf_op jit(solution)/shard_map/amxny,anzyq->amxzq/dot_general | solution.py:36
  284.3 12.0 %copy.44 = bf16[8,64,64,128]{3,2,1,0:T(8,128)(2,1)} copy(bf16[8,64,64,128]{3,1,0,2:T(8,128)(2,1)} %fusion.5) | data formatting | bytes 16777216 | tf_op jit(solution)/shard_map/convert_element_type | solution.py:39
  296.3 128.5 %all-to-all-done.1 = bf16[16,8,256,128]{3,2,1,0:T(8,128)(2,1)} async-done(((bf16[16,8,256,128]{3,2,1,0:T(8,128)(2,1)}), bf16[16,8,256,128]{3,2,1,0:T(8,128)(2,1)}, u32[]{:S(2)}, u32[]{:S(2)}) %all-to-all-start.1) | async-done | bytes 8388640 | tf_op jit(solution)/shard_map/all_to_all | solution.py:21
  424.8 7.7 %copy.41 = bf16[16,8,256,128]{3,2,0,1:T(8,128)(2,1)} copy(bf16[16,8,256,128]{3,2,1,0:T(8,128)(2,1)} %all-to-all-done.1) | data formatting | bytes 16777216 | tf_op jit(solution)/shard_map/all_to_all | solution.py:21
  432.6 8.8 %fusion.13 = f32[128,128]{1,0:T(8,128)} fusion(bf16[32768,128]{1,0:T(8,128)(2,1)} %bitcast.46, bf16[32768,128]{1,0:T(8,128)(2,1)} %bitcast.45), kind=kOutput, calls=%fused_computation.22 | convolution fusion | flops 1073741824 | bytes 16842752 | tf_op jit(solution)/shard_map/rp,rq->pq/dot_general | solution.py:58
  441.3 0.0 all-reduce.3.cloned.1.call-update
  441.4 0.0 copy-done.2
  441.4 0.6 dynamic-slice
  442.6 115.2 %all-reduce.3.cloned.1.call-done = f32[128,128]{1,0:T(8,128)} async-done(((f32[128,128]{1,0:T(8,128)}), f32[128,128]{1,0:T(8,128)}) %all-reduce.3.cloned.1.call-update) | async-done | bytes 65552
  557.8 1.3 constant_dynamic-slice_fusion
  (7 shorter events, 0.0 us)
Async XLA Ops:
  46.4 7.6 %copy-start.1 = (s32[16,8]{0,1:T(8,128)S(1)}, s32[16,8]{0,1:T(8,128)}, u32[]{:S(2)}) copy-start(s32[16,8]{0,1:T(8,128)} %param.7) | copy-start | bytes 1540
  46.4 158.3 %all-to-all-start = ((bf16[1,8,4096,128]{3,1,0,2:T(8,128)(2,1)}), bf16[1,8,4096,128]{3,1,0,2:T(8,128)(2,1)}, u32[]{:S(2)}, u32[]{:S(2)}) async-start(bf16[1,8,4096,128]{3,1,0,2:T(8,128)(2,1)} %copy.37), calls=%async_computation | async-start | bytes 16777216 | tf_op jit(solution)/shard_map/all_to_all | solution.py:8
  237.4 36.9 %copy-start = (bf16[1,512,512]{2,1,0:T(8,128)(2,1)S(1)}, bf16[1,512,512]{2,1,0:T(8,128)(2,1)}, u32[]{:S(2)}) copy-start(bf16[1,512,512]{2,1,0:T(8,128)(2,1)} %param.5) | copy-start | bytes 1572868
  237.4 187.4 %all-to-all-start.1 = ((bf16[16,8,256,128]{3,2,1,0:T(8,128)(2,1)}), bf16[16,8,256,128]{3,2,1,0:T(8,128)(2,1)}, u32[]{:S(2)}, u32[]{:S(2)}) async-start(bf16[16,8,256,128]{3,2,1,0:T(8,128)(2,1)} %select_select_fusion), calls=%async_computation.1 | async-start | bytes 16777216 | tf_op jit(solution)/shard_map/all_to_all | solution.py:21
  274.1 283.7 %all-reduce.3.cloned.1.call-start = ((), (), s32[]{:S(2)}) async-start(), calls=%async_computation.2 | async-start | bytes 131072
  432.6 8.8 %copy-start.2 = (u32[32]{0:T(128)S(1)}, u32[32]{0:T(128)}, u32[]{:S(2)}) copy-start(u32[32]{0:T(128)} %constant.34) | copy-start | bytes 388
Sparse Core Ops, SparseCore 0:
  441.5 116.2 all-reduce.2
where the time goes:
time: 568 us; the launch traced here: 566 us
  waiting for transfers between devices  394 us (69%)
  local copies, waits for them, and re-layouts  70.2 us (12%)
  starting transfers between devices  44.5 us (8%)
  matrix products  27.5 us (5%)
  other arithmetic  15.6 us (3%)
  between operations  14.1 us (2%)
    all_to_all x1, waiting for transfers between devices, spread_return(): lax.all_to_all(block_rows, 'tensor', split_axis=2, concat_axis=0, tiled=T...  150 us
    all_to_all x1, waiting for transfers between devices, spread_return(): lax.all_to_all(permuted, 'tensor', split_axis=0, concat_axis=2, tiled=True)  129 us
    unnamed x2, waiting for transfers between devices  115 us
    all_to_all x1, starting transfers between devices, spread_return(): lax.all_to_all(permuted, 'tensor', split_axis=0, concat_axis=2, tiled=True)  36.7 us
    all_to_all x2, local copies, waits for them, and re-layouts, spread_return(): lax.all_to_all(block_rows, 'tensor', split_axis=2, concat_axis=0, tiled=T...  15.4 us
    convert_element_type x1, local copies, waits for them, and re-layouts, occupied_side(): return projected.astype(jnp.bfloat16).reshape(flat_shape)  12 us
  transfers between devices with their start and end apart: 3, of which 3 were waited for; matrix products, arithmetic and copies ran while one was open for 4% of the time, Pallas kernels for 0%

commit v1 on v0

v1 whole, which is shorter than its diff:
```python
import functools

import jax
import jax.numpy as jnp
from jax import lax
from jax.experimental import pallas as pl
from jax.experimental.pallas import tpu as pltpu
from jax.sharding import PartitionSpec as P

SLOTS = 8
BF = jnp.bfloat16
F32 = jnp.float32


def gathered_rows(block_ref, first, count, width):
    columns = []
    for step in range(count):
        at = (first + step) * width
        columns.append(jnp.concatenate([block_ref[0, m, at : at + width, :] for m in range(SLOTS)], axis=0))
    return jnp.concatenate(columns, axis=1)


def product_kernel(slots, width, rows, me_ref, neighbors_ref, virt_ref, block_ref, *refs):
    outs, virt_t = refs[:-1], refs[-1]
    me = me_ref[0]
    low, count = slots[0], len(slots)

    @pl.when(pl.program_id(0) == 0)
    def _():
        parts = []
        for m in range(SLOTS):
            part = virt_ref[0, m * width : (m + 1) * width, low * width : (low + count) * width].astype(F32)
            parts.append(jnp.where(neighbors_ref[me, m] >= 0, part, 0.0))
        turned = jnp.concatenate(parts, axis=0).T
        for at, k in enumerate(slots):
            live = neighbors_ref[me, k] >= 0
            virt_t[at * width : (at + 1) * width, :] = jnp.where(
                live, turned[at * width : (at + 1) * width, :], 0.0
            ).astype(BF)

    ri = block_ref.shape[-1]
    for pair in range(rows // 2):
        right = gathered_rows(block_ref, 2 * pair, 2, width)
        both = jnp.dot(virt_t[...], right, preferred_element_type=F32).astype(BF)
        for at in range(count):
            for half in range(2):
                row = (2 * pair + half) * width
                outs[at][row : row + width, :] = both[at * width : (at + 1) * width, half * ri : (half + 1) * ri]


def products(slots, me, neighbors, virt, blocks, rows=8):
    pairs, ri = blocks.shape[2:]
    wide = virt.shape[1]
    width = wide // SLOTS
    steps = width // rows
    chunk = rows * width
    return pl.pallas_call(
        functools.partial(product_kernel, slots, width, rows),
        grid=(steps,),
        in_specs=[
            pl.BlockSpec(memory_space=pltpu.SMEM),
            pl.BlockSpec(memory_space=pltpu.SMEM),
            pl.BlockSpec((1, wide, wide), lambda s: (0, 0, 0)),
            pl.BlockSpec((1, SLOTS, chunk, ri), lambda s: (0, 0, s, 0)),
        ],
        out_specs=[pl.BlockSpec((chunk, ri), lambda s: (s, 0))] * len(slots),
        out_shape=[jax.ShapeDtypeStruct((pairs, ri), BF)] * len(slots),
        scratch_shapes=[pltpu.VMEM((len(slots) * width, wide), BF)],
        compiler_params=pltpu.CompilerParams(vmem_limit_bytes=32 << 20),
        cost_estimate=pl.CostEstimate(
            flops=2 * len(slots) * width * wide * width * ri,
            bytes_accessed=2 * (SLOTS + len(slots)) * pairs * ri,
            transcendentals=0,
        ),
        name="products",
    )(me, neighbors, virt, blocks)


def project_kernel(width, rows, me_ref, neighbors_ref, occ_ref, block_ref, *refs):
    outs, occ, turn = refs[:-2], refs[-2], refs[-1]
    me = me_ref[0]
    wide = SLOTS * width

    @pl.when(pl.program_id(0) == 0)
    def _():
        lane = lax.broadcasted_iota(jnp.int32, (1, wide), 1) // width
        keep = jnp.zeros((1, wide), F32)
        for n in range(SLOTS):
            keep = jnp.where((lane == n) & (neighbors_ref[me, n] >= 0), 1.0, keep)
        occ[...] = (occ_ref[0].astype(F32) * keep).astype(BF)

    ri = block_ref.shape[-1]
    for pair in range(rows // 2):
        right = gathered_rows(block_ref, 2 * pair, 2, width)
        both = jnp.dot(occ[...], right, preferred_element_type=F32)
        for half in range(2):
            turn[pl.ds(2 * pair + half, wide, stride=rows), :] = both[:, half * ri : (half + 1) * ri]
    for m in range(SLOTS):
        piece = turn[m * width * rows : (m + 1) * width * rows, :]
        outs[m][...] = piece.astype(BF).reshape(width, rows, ri)


def projections(me, neighbors, occ, blocks, rows=16):
    pairs, ri = blocks.shape[2:]
    wide = occ.shape[1]
    width = wide // SLOTS
    steps = width // rows
    chunk = rows * width
    out = pl.pallas_call(
        functools.partial(project_kernel, width, rows),
        grid=(steps,),
        in_specs=[
            pl.BlockSpec(memory_space=pltpu.SMEM),
            pl.BlockSpec(memory_space=pltpu.SMEM),
            pl.BlockSpec((1, wide, wide), lambda s: (0, 0, 0)),
            pl.BlockSpec((1, SLOTS, chunk, ri), lambda s: (0, 0, s, 0)),
        ],
        out_specs=[pl.BlockSpec((width, rows, ri), lambda s: (0, s, 0))] * SLOTS,
        out_shape=[jax.ShapeDtypeStruct((width, width, ri), BF)] * SLOTS,
        scratch_shapes=[pltpu.VMEM((wide, wide), BF), pltpu.VMEM((wide * rows, ri), F32)],
        compiler_params=pltpu.CompilerParams(vmem_limit_bytes=40 << 20),
        cost_estimate=pl.CostEstimate(
            flops=2 * wide * wide * width * ri, bytes_accessed=4 * SLOTS * pairs * ri, transcendentals=0
        ),
        name="projections",
    )(me, neighbors, occ, blocks)
    return [each.reshape(pairs, ri) for each in out]


def contract_kernel(count, has_start, *refs):
    lefts, rights = refs[:count], refs[count : 2 * count]
    out = refs[-1]

    @pl.when(pl.program_id(0) == 0)
    def _():
        out[...] = refs[2 * count][...] if has_start else jnp.zeros_like(out)

    total = out[...]
    for left, right in zip(lefts, rights):
        total += lax.dot_general(
            left[...], right[...], (((0,), (0,)), ((), ())), preferred_element_type=F32
        )
    out[...] = total


def contract(lefts, rights, start=None, chunk=1024):
    pairs, ri = lefts[0].shape
    count = len(lefts)
    starts = [] if start is None else [start]
    whole = pl.BlockSpec((ri, ri), lambda s: (0, 0))
    return pl.pallas_call(
        functools.partial(contract_kernel, count, start is not None),
        grid=(pairs // chunk,),
        in_specs=[pl.BlockSpec((chunk, ri), lambda s: (s, 0))] * (2 * count) + [whole] * len(starts),
        out_specs=whole,
        out_shape=jax.ShapeDtypeStruct((ri, ri), F32),
        compiler_params=pltpu.CompilerParams(vmem_limit_bytes=32 << 20),
        cost_estimate=pl.CostEstimate(
            flops=2 * count * pairs * ri * ri, bytes_accessed=4 * count * pairs * ri, transcendentals=0
        ),
        name="contract",
    )(*lefts, *rights, *starts)


def exchange(value, k, devices):
    return lax.ppermute(value, "tensor", [(i, i ^ k) for i in range(devices)])


def reduce_rows(total, devices, order):
    index = lax.axis_index("tensor")
    bits = [1 << b for b in reversed(range(devices.bit_length() - 1))]
    value = total.reshape((2,) * len(bits) + (total.shape[0] // devices, total.shape[1]))
    left = list(bits)
    for k in order:
        at = left.index(k)
        left.pop(at)
        low = lax.index_in_dim(value, 0, at, keepdims=False)
        high = lax.index_in_dim(value, 1, at, keepdims=False)
        upper = (index // k) % 2 == 1
        value = jnp.where(upper, high, low) + exchange(jnp.where(upper, low, high), k, devices)
    return value


def local(devices, three_center, occ_green, virt_green, neighbors):
    me = lax.axis_index("tensor").astype(jnp.int32).reshape(1)
    sides = {}
    sides[6], sides[7] = products((6, 7), me, neighbors, virt_green, three_center)
    arrived = {k: exchange(sides[k], k, devices) for k in (6, 7)}
    early = (0, 1, 2, 3, 4, 5)
    for k, value in zip(early, products(early, me, neighbors, virt_green, three_center)):
        sides[k] = value
    for k in (2, 4, 3, 5, 1):
        arrived[k] = exchange(sides[k], k, devices)
    arrived[0] = sides[0]
    project = projections(me, neighbors, occ_green, three_center)
    order = (0, 1, 6, 7, 2, 4, 3, 5)
    groups = ((0, 1), (6, 7), (2, 4), (3, 5))
    total = None
    for group in groups:
        total = contract([arrived[k] for k in group], [project[k] for k in group], total)
    bits = [1 << b for b in reversed(range(devices.bit_length() - 1))]
    return reduce_rows(total, devices, bits)


def solution(mesh):
    devices = mesh.shape["tensor"]
    in_specs = (
        P(("group", "tensor"), None, None, None),
        P("tensor", None, None),
        P("tensor", None, None),
        P(),
    )
    out_specs = P(("group", "tensor"), None)
    return jax.shard_map(
        functools.partial(local, devices), mesh=mesh, in_specs=in_specs, out_specs=out_specs, check_vma=False
    )
```

time: 568 us -> 130 us (0.23)
  waiting for transfers between devices: 394 us -> 72.4 us
  local copies, waits for them, and re-layouts: 70.2 us -> 8.29 us
  Pallas kernels: 0 us -> 33.9 us
  starting transfers between devices: 44.5 us -> 14.7 us
  matrix products: 27.5 us -> 0 us
  other arithmetic: 15.6 us -> 0.64 us
  between operations: 14.1 us -> 0.09 us
    all_to_all x2 -> x0, waiting for transfers between devices: 279 us -> none  [the longest x1 150 us: spread_return(): lax.all_to_all(block_rows, 'tensor', split_axis=2, concat_axis=0, tiled=T...]
    unnamed x2 -> x0, waiting for transfers between devices: 115 us -> none
    ppermute x0 -> x11, waiting for transfers between devices: none -> 72.4 us  [exchange(): return lax.ppermute(value, 'tensor', [(i, i ^ k) for i in range(devices)])]
    all_to_all x2 -> x0, starting transfers between devices: 44.2 us -> none  [the longest x1 36.7 us: spread_return(): lax.all_to_all(permuted, 'tensor', split_axis=0, concat_axis=2, tiled=True)]
    pallas_call x0 -> x7, Pallas kernels: none -> 33.9 us  [the longest x2 12.4 us: products(): pl.pallas_call(functools.partial(product_kernel, slots, width, rows), gri...]
    dot_general x3 -> x0, matrix products: 27.5 us -> none  [the longest x1 9.38 us: virtual_side(): jnp.einsum('amilp,amlkj->akijp', blocks, virt_grid, preferred_element_typ...]
    all_to_all x3 -> x0, local copies, waits for them, and re-layouts: 23.1 us -> none  [the longest x2 15.4 us: spread_return(): lax.all_to_all(block_rows, 'tensor', split_axis=2, concat_axis=0, tiled=T...]
    convert_element_type x2 -> x0, local copies, waits for them, and re-layouts: 21.5 us -> none  [the longest x1 12 us: occupied_side(): return projected.astype(jnp.bfloat16).reshape(flat_shape)]
  transfers between devices with their start and end apart: 3 -> 11, of which waited for: 3 -> 9; matrix products, arithmetic and copies ran while one was open for 4% -> 0% of each run, Pallas kernels for 0% -> 18%
where the time goes in v1:
time: 130 us
  waiting for transfers between devices  72.4 us (56%)
  Pallas kernels  33.9 us (26%)
  starting transfers between devices  14.7 us (11%)
  local copies, waits for them, and re-layouts  8.29 us (6%)
    ppermute x11, waiting for transfers between devices, exchange(): return lax.ppermute(value, 'tensor', [(i, i ^ k) for i in range(devices)])  72.4 us
    ppermute x11, starting transfers between devices, exchange(): return lax.ppermute(value, 'tensor', [(i, i ^ k) for i in range(devices)])  14.7 us
    pallas_call x2, Pallas kernels, products(): pl.pallas_call(functools.partial(product_kernel, slots, width, rows), gri...  12.4 us
    pallas_call x1, Pallas kernels, projections(): pl.pallas_call(functools.partial(project_kernel, width, rows), grid=(step...  11.1 us
    pallas_call x4, Pallas kernels, contract(): pl.pallas_call(functools.partial(contract_kernel, count, start is not Non...  10.3 us
    unnamed x15, local copies, waits for them, and re-layouts  8.29 us
  transfers between devices with their start and end apart: 11, of which 9 were waited for; matrix products, arithmetic and copies ran while one was open for 0% of the time, Pallas kernels for 18%

profile of v1, /device:TPU:0, one launch (start us, length us, event | category | flops | bytes accessed | tf_op | source)
XLA Modules:
  0.0 130.0 jit_solution(9327532679693354781)
XLA Ops:
  0.0 0.8 copy.5.neighbors_ref
  0.8 3.4 %copy-done = bf16[1,8,4096,128]{3,2,1,0:T(8,128)(2,1)S(1)} copy-done((bf16[1,8,4096,128]{3,2,1,0:T(8,128)(2,1)S(1)}, bf16[1,8,4096,128]{3,2,1,0:T(8,128)(2,1)}, u32[]{:S(2)}) %copy-start) | copy-done | bytes 8388632
  4.1 1.0 copy-done.5
  5.2 7.1 %products.2 = (bf16[4096,128]{1,0:T(8,128)(2,1)S(1)}, bf16[4096,128]{1,0:T(8,128)(2,1)S(1)}, bf16[4096,128]{1,0:T(8,128)(2,1)}, bf16[4096,128]{1,0:T(8,128)(2,1)...) custom-call(s32[1]{0:T(128)} %bitcast.me_ref, s32[16,8]{1,0:T(8,128)S(1)} %copy.5.neighbors_ref, ...), custom_call_target="tpu_custom_call" | custom-call | flops 3221225472 | bytes 14680064 | tf_op jit(solution)/shard_map/products/pallas_call | solution.py:57
  12.3 0.5 collective-permute-start.6
  12.8 5.3 %products.3 = (bf16[4096,128]{1,0:T(8,128)(2,1)S(1)}, bf16[4096,128]{1,0:T(8,128)(2,1)}) custom-call(s32[1]{0:T(128)} %bitcast.me_ref, s32[16,8]{1,0:T(8,128)S(1)} %copy.5.neighbors_ref, bf16[1,512,512]{2,1,0:T(8,128)(2,1)S(1)} %copy-done.5, bf16[1,8,4096,128]{3,2,1,0:T(8,128)(2,1)S(1)} %copy-done), custom_call_target="tpu_custom_call" | custom-call | flops 1073741824 | bytes 10485760 | tf_op jit(solution)/shard_map/products/pallas_call | solution.py:57
  18.1 3.5 %collective-permute-start.4 = (bf16[4096,128]{1,0:T(8,128)(2,1)S(1)}, bf16[4096,128]{1,0:T(8,128)(2,1)S(1)}, u32[]{:S(2)}, u32[]{:S(2)}) collective-permute-start(bf16[4096,128]{1,0:T(8,128)(2,1)S(1)} %get-tuple-element.29), channel_id=1, source_target_pairs={{0,6},{1,7},{2,4},{3,5},{4,2},{5,3},{6,0},{7,1},{8,14},{9,15},{10,... | collective-permute-start | bytes 3145736 | tf_op jit(solution)/shard_map/ppermute | solution.py:166
  21.6 0.1 collective-permute-start.5
  21.7 1.6 %collective-permute-start.2 = (bf16[4096,128]{1,0:T(8,128)(2,1)}, bf16[4096,128]{1,0:T(8,128)(2,1)S(1)}, u32[]{:S(2)}, u32[]{:S(2)}) collective-permute-start(bf16[4096,128]{1,0:T(8,128)(2,1)} %get-tuple-element.25), channel_id=1, source_target_pairs={{0,2},{1,3},{2,0},{3,1},{4,6},{5,7},{6,4},{7,5},{8,10},{9,11},{10,... | collective-permute-start | bytes 3145736 | tf_op jit(solution)/shard_map/ppermute | solution.py:166
  23.4 1.6 %collective-permute-start.3 = (bf16[4096,128]{1,0:T(8,128)(2,1)}, bf16[4096,128]{1,0:T(8,128)(2,1)}, u32[]{:S(2)}, u32[]{:S(2)}) collective-permute-start(bf16[4096,128]{1,0:T(8,128)(2,1)} %get-tuple-element.26), channel_id=1, source_target_pairs={{0,4},{1,5},{2,6},{3,7},{4,0},{5,1},{6,2},{7,3},{8,12},{9,13},{10,... | collective-permute-start | bytes 3145736 | tf_op jit(solution)/shard_map/ppermute | solution.py:166
  24.9 1.0 copy-done.3
  25.9 19.8 %collective-permute-done.4.refs_0_ = bf16[4096,128]{1,0:T(8,128)(2,1)S(1)} collective-permute-done((bf16[4096,128]{1,0:T(8,128)(2,1)S(1)}, bf16[4096,128]{1,0:T(8,128)(2,1)S(1)}, u32[]{:S(2)}, u32[]{:S(2)}) %collective-permute-start.4) | collective-permute-done | bytes 1048608 | tf_op jit(solution)/shard_map/ppermute | solution.py:166
  45.7 1.1 copy-done.1
  46.8 0.8 collective-permute-start.1
  47.6 1.0 copy-done.6
  48.6 11.1 %projections.1 = (bf16[64,64,128]{2,1,0:T(8,128)(2,1)S(1)}, bf16[64,64,128]{2,1,0:T(8,128)(2,1)S(1)}, bf16[64,64,128]{2,1,0:T(8,128)(2,1)S(1)}, bf16[64,64,128]{...) custom-call(s32[1]{0:T(128)} %bitcast.me_ref, ...), custom_call_target="tpu_custom_call" | custom-call | flops 4294967296 | bytes 16777216 | tf_op jit(solution)/shard_map/projections/pallas_call | solution.py:109
  59.7 1.4 %contract.4.refs_4_ = f32[128,128]{1,0:T(8,128)S(1)} custom-call(bf16[4096,128]{1,0:T(8,128)(2,1)S(1)} %get-tuple-element.33.refs_0_, bf16[4096,128]{1,0:T(8,128)(2,1)S(1)} %copy-done.4, bf16[4096,128]{1,0:T(8,128)(2,1)S(1)} %bitcast.29, bf16[4096,128]{1,0:T(8,128)(2,1)S(1)} %bitcast.30), custom_call_target="tpu_custom_call" | custom-call | flops 268435456 | bytes 4194304 | tf_op jit(solution)/shard_map/contract/pallas_call | solution.py:151
  61.2 6.7 %collective-permute-done.5.refs_1_ = bf16[4096,128]{1,0:T(8,128)(2,1)} collective-permute-done((bf16[4096,128]{1,0:T(8,128)(2,1)}, bf16[4096,128]{1,0:T(8,128)(2,1)}, u32[]{:S(2)}, u32[]{:S(2)}) %collective-permute-start.5) | collective-permute-done | bytes 1048608 | tf_op jit(solution)/shard_map/ppermute | solution.py:166
  67.9 3.0 %contract.5.refs_4_ = f32[128,128]{1,0:T(8,128)S(1)} custom-call(bf16[4096,128]{1,0:T(8,128)(2,1)S(1)} %copy-done.2, bf16[4096,128]{1,0:T(8,128)(2,1)} %collective-permute-done.5.refs_1_, bf16[4096,128]{1,0:T(8,128)(2,1)S(1)} %bitcast.27, bf16[4096,128]{1,0:T(8,128)(2,1)S(1)} %bitcast.28, f32[128,128]{1,0:T(8,128)S(1)} %contract.4.refs_4_), custom_call_target="tpu_custom_call" | custom-call | flops 268435456 | bytes 4194304 | tf_op jit(solution)/shard_map/contract/pallas_call | solution.py:151
  70.9 19.6 %collective-permute-done.2.refs_0_ = bf16[4096,128]{1,0:T(8,128)(2,1)S(1)} collective-permute-done((bf16[4096,128]{1,0:T(8,128)(2,1)}, bf16[4096,128]{1,0:T(8,128)(2,1)S(1)}, u32[]{:S(2)}, u32[]{:S(2)}) %collective-permute-start.2) | collective-permute-done | bytes 1048608 | tf_op jit(solution)/shard_map/ppermute | solution.py:166
  90.4 0.6 collective-permute-done.3.refs_1_
  91.1 3.0 %contract.6.refs_4_ = f32[128,128]{1,0:T(8,128)S(1)} custom-call(bf16[4096,128]{1,0:T(8,128)(2,1)S(1)} %collective-permute-done.2.refs_0_, bf16[4096,128]{1,0:T(8,128)(2,1)} %collective-permute-done.3.refs_1_, bf16[4096,128]{1,0:T(8,128)(2,1)S(1)} %bitcast.25, bf16[4096,128]{1,0:T(8,128)(2,1)S(1)} %bitcast.26, f32[128,128]{1,0:T(8,128)S(1)} %contract.5.refs_4_), custom_call_target="tpu_custom_call" | custom-call | flops 268435456 | bytes 4194304 | tf_op jit(solution)/shard_map/contract/pallas_call | solution.py:151
  94.1 18.7 %collective-permute-done.refs_0_ = bf16[4096,128]{1,0:T(8,128)(2,1)S(1)} collective-permute-done((bf16[4096,128]{1,0:T(8,128)(2,1)}, bf16[4096,128]{1,0:T(8,128)(2,1)S(1)}, u32[]{:S(2)}, u32[]{:S(2)}) %collective-permute-start) | collective-permute-done | bytes 1048608 | tf_op jit(solution)/shard_map/ppermute | solution.py:166
  112.8 3.0 %contract.7 = f32[128,128]{1,0:T(8,128)S(1)} custom-call(bf16[4096,128]{1,0:T(8,128)(2,1)S(1)} %collective-permute-done.refs_0_, bf16[4096,128]{1,0:T(8,128)(2,1)} %collective-permute-done.1.refs_1_, bf16[4096,128]{1,0:T(8,128)(2,1)S(1)} %bitcast.23, bf16[4096,128]{1,0:T(8,128)(2,1)S(1)} %bitcast.24, f32[128,128]{1,0:T(8,128)S(1)} %contract.6.refs_4_), custom_call_target="tpu_custom_call" | custom-call | flops 268435456 | bytes 4194304 | tf_op jit(solution)/shard_map/contract/pallas_call | solution.py:151
  115.8 2.8 %collective-permute-start.7 = (f32[2,2,2,8,128]{4,3,2,1,0:T(8,128)S(1)}, f32[2,2,2,8,128]{4,3,2,1,0:T(8,128)S(1)}, u32[]{:S(2)}, u32[]{:S(2)}) collective-permute-start(f32[2,2,2,8,128]{4,3,2,1,0:T(8,128)S(1)} %bitcast.32), channel_id=1, source_target_pairs={{0,8},{1,9},{2,10},{3,11},{4,12},{5,13},{6,14},{7,15},{8,0},{9,1},... | collective-permute-start | bytes 98312 | tf_op jit(solution)/shard_map/ppermute | solution.py:166
  118.6 2.1 %collective-permute-done.7 = f32[2,2,2,8,128]{4,3,2,1,0:T(8,128)S(1)} collective-permute-done((f32[2,2,2,8,128]{4,3,2,1,0:T(8,128)S(1)}, f32[2,2,2,8,128]{4,3,2,1,0:T(8,128)S(1)}, u32[]{:S(2)}, u32[]{:S(2)}) %collective-permute-start.7) | collective-permute-done | bytes 32800 | tf_op jit(solution)/shard_map/ppermute | solution.py:166
  120.7 1.8 %collective-permute-start.8 = (f32[2,2,8,128]{3,2,1,0:T(8,128)S(1)}, f32[2,2,8,128]{3,2,1,0:T(8,128)S(1)}, u32[]{:S(2)}, u32[]{:S(2)}) collective-permute-start(f32[2,2,8,128]{3,2,1,0:T(8,128)S(1)} %select_bitcast_fusion), channel_id=1, source_target_pairs={{0,4},{1,5},{2,6},{3,7},{4,0},{5,1},{6,2},{7,3},{8,12},{9,13},{10,... | collective-permute-start | bytes 49160 | tf_op jit(solution)/shard_map/ppermute | solution.py:166
  122.4 2.1 %collective-permute-done.8 = f32[2,2,8,128]{3,2,1,0:T(8,128)S(1)} collective-permute-done((f32[2,2,8,128]{3,2,1,0:T(8,128)S(1)}, f32[2,2,8,128]{3,2,1,0:T(8,128)S(1)}, u32[]{:S(2)}, u32[]{:S(2)}) %collective-permute-start.8) | collective-permute-done | bytes 16416 | tf_op jit(solution)/shard_map/ppermute | solution.py:166
  124.5 2.0 %collective-permute-start.9 = (f32[2,8,128]{2,1,0:T(8,128)S(1)}, f32[2,8,128]{2,1,0:T(8,128)S(1)}, u32[]{:S(2)}, u32[]{:S(2)}) collective-permute-start(f32[2,8,128]{2,1,0:T(8,128)S(1)} %select_bitcast_fusion.1), channel_id=1, source_target_pairs={{0,2},{1,3},{2,0},{3,1},{4,6},{5,7},{6,4},{7,5},{8,10},{9,11},{10,... | collective-permute-start | bytes 24584 | tf_op jit(solution)/shard_map/ppermute | solution.py:166
  126.5 1.7 %collective-permute-done.9 = f32[2,8,128]{2,1,0:T(8,128)S(1)} collective-permute-done((f32[2,8,128]{2,1,0:T(8,128)S(1)}, f32[2,8,128]{2,1,0:T(8,128)S(1)}, u32[]{:S(2)}, u32[]{:S(2)}) %collective-permute-start.9) | collective-permute-done | bytes 8224 | tf_op jit(solution)/shard_map/ppermute | solution.py:166
  128.3 1.2 collective-permute-done.10
  129.5 0.6 bitcast_add_fusion.2
  (20 shorter events, 0.1 us)
Async XLA Ops:
  0.8 3.4 %copy-start = (bf16[1,8,4096,128]{3,2,1,0:T(8,128)(2,1)S(1)}, bf16[1,8,4096,128]{3,2,1,0:T(8,128)(2,1)}, u32[]{:S(2)}) copy-start(bf16[1,8,4096,128]{3,2,1,0:T(8,128)(2,1)} %block_ref.5) | copy-start | bytes 25165828
  4.1 1.0 copy-start.5
  12.3 12.6 %collective-permute-start.6 = (bf16[4096,128]{1,0:T(8,128)(2,1)S(1)}, bf16[4096,128]{1,0:T(8,128)(2,1)S(1)}, u32[]{:S(2)}, u32[]{:S(2)}) collective-permute-start(bf16[4096,128]{1,0:T(8,128)(2,1)S(1)} %get-tuple-element.34), channel_id=1, source_target_pairs={{0,1},{1,0},{2,3},{3,2},{4,5},{5,4},{6,7},{7,6},{8,9},{9,8},{10,11... | collective-permute-start | bytes 3145736 | tf_op jit(solution)/shard_map/ppermute | solution.py:166
  18.1 27.7 %collective-permute-start.4 = (bf16[4096,128]{1,0:T(8,128)(2,1)S(1)}, bf16[4096,128]{1,0:T(8,128)(2,1)S(1)}, u32[]{:S(2)}, u32[]{:S(2)}) collective-permute-start(bf16[4096,128]{1,0:T(8,128)(2,1)S(1)} %get-tuple-element.29), channel_id=1, source_target_pairs={{0,6},{1,7},{2,4},{3,5},{4,2},{5,3},{6,0},{7,1},{8,14},{9,15},{10,... | collective-permute-start | bytes 3145736 | tf_op jit(solution)/shard_map/ppermute | solution.py:166
  21.6 46.3 %collective-permute-start.5 = (bf16[4096,128]{1,0:T(8,128)(2,1)}, bf16[4096,128]{1,0:T(8,128)(2,1)}, u32[]{:S(2)}, u32[]{:S(2)}) collective-permute-start(bf16[4096,128]{1,0:T(8,128)(2,1)} %get-tuple-element.30), channel_id=1, source_target_pairs={{0,7},{1,6},{2,5},{3,4},{4,3},{5,2},{6,1},{7,0},{8,15},{9,14},{10,... | collective-permute-start | bytes 3145736 | tf_op jit(solution)/shard_map/ppermute | solution.py:166
  21.7 68.7 %collective-permute-start.2 = (bf16[4096,128]{1,0:T(8,128)(2,1)}, bf16[4096,128]{1,0:T(8,128)(2,1)S(1)}, u32[]{:S(2)}, u32[]{:S(2)}) collective-permute-start(bf16[4096,128]{1,0:T(8,128)(2,1)} %get-tuple-element.25), channel_id=1, source_target_pairs={{0,2},{1,3},{2,0},{3,1},{4,6},{5,7},{6,4},{7,5},{8,10},{9,11},{10,... | collective-permute-start | bytes 3145736 | tf_op jit(solution)/shard_map/ppermute | solution.py:166
  23.4 67.7 %collective-permute-start.3 = (bf16[4096,128]{1,0:T(8,128)(2,1)}, bf16[4096,128]{1,0:T(8,128)(2,1)}, u32[]{:S(2)}, u32[]{:S(2)}) collective-permute-start(bf16[4096,128]{1,0:T(8,128)(2,1)} %get-tuple-element.26), channel_id=1, source_target_pairs={{0,4},{1,5},{2,6},{3,7},{4,0},{5,1},{6,2},{7,3},{8,12},{9,13},{10,... | collective-permute-start | bytes 3145736 | tf_op jit(solution)/shard_map/ppermute | solution.py:166
  24.9 1.0 copy-start.3
  25.9 86.8 %collective-permute-start = (bf16[4096,128]{1,0:T(8,128)(2,1)}, bf16[4096,128]{1,0:T(8,128)(2,1)S(1)}, u32[]{:S(2)}, u32[]{:S(2)}) collective-permute-start(bf16[4096,128]{1,0:T(8,128)(2,1)} %get-tuple-element.21), channel_id=1, source_target_pairs={{0,3},{1,2},{2,1},{3,0},{4,7},{5,6},{6,5},{7,4},{8,11},{9,10},{10,... | collective-permute-start | bytes 3145736 | tf_op jit(solution)/shard_map/ppermute | solution.py:166
  45.7 1.1 copy-start.1
  46.8 66.0 %collective-permute-start.1 = (bf16[4096,128]{1,0:T(8,128)(2,1)}, bf16[4096,128]{1,0:T(8,128)(2,1)}, u32[]{:S(2)}, u32[]{:S(2)}) collective-permute-start(bf16[4096,128]{1,0:T(8,128)(2,1)} %get-tuple-element.22), channel_id=1, source_target_pairs={{0,5},{1,4},{2,7},{3,6},{4,1},{5,0},{6,3},{7,2},{8,13},{9,12},{10,... | collective-permute-start | bytes 3145736 | tf_op jit(solution)/shard_map/ppermute | solution.py:166
  47.6 1.0 copy-start.6
  48.6 11.1 %copy-start.4 = (bf16[4096,128]{1,0:T(8,128)(2,1)S(1)}, bf16[4096,128]{1,0:T(8,128)(2,1)}, u32[]{:S(2)}) copy-start(bf16[4096,128]{1,0:T(8,128)(2,1)} %copy-done.3) | copy-start | bytes 3145732
  48.6 19.3 %copy-start.2 = (bf16[4096,128]{1,0:T(8,128)(2,1)S(1)}, bf16[4096,128]{1,0:T(8,128)(2,1)}, u32[]{:S(2)}) copy-start(bf16[4096,128]{1,0:T(8,128)(2,1)} %copy-done.1) | copy-start | bytes 3145732
  115.8 4.9 %collective-permute-start.7 = (f32[2,2,2,8,128]{4,3,2,1,0:T(8,128)S(1)}, f32[2,2,2,8,128]{4,3,2,1,0:T(8,128)S(1)}, u32[]{:S(2)}, u32[]{:S(2)}) collective-permute-start(f32[2,2,2,8,128]{4,3,2,1,0:T(8,128)S(1)} %bitcast.32), channel_id=1, source_target_pairs={{0,8},{1,9},{2,10},{3,11},{4,12},{5,13},{6,14},{7,15},{8,0},{9,1},... | collective-permute-start | bytes 98312 | tf_op jit(solution)/shard_map/ppermute | solution.py:166
  120.7 3.8 %collective-permute-start.8 = (f32[2,2,8,128]{3,2,1,0:T(8,128)S(1)}, f32[2,2,8,128]{3,2,1,0:T(8,128)S(1)}, u32[]{:S(2)}, u32[]{:S(2)}) collective-permute-start(f32[2,2,8,128]{3,2,1,0:T(8,128)S(1)} %select_bitcast_fusion), channel_id=1, source_target_pairs={{0,4},{1,5},{2,6},{3,7},{4,0},{5,1},{6,2},{7,3},{8,12},{9,13},{10,... | collective-permute-start | bytes 49160 | tf_op jit(solution)/shard_map/ppermute | solution.py:166
  124.5 3.7 %collective-permute-start.9 = (f32[2,8,128]{2,1,0:T(8,128)S(1)}, f32[2,8,128]{2,1,0:T(8,128)S(1)}, u32[]{:S(2)}, u32[]{:S(2)}) collective-permute-start(f32[2,8,128]{2,1,0:T(8,128)S(1)} %select_bitcast_fusion.1), channel_id=1, source_target_pairs={{0,2},{1,3},{2,0},{3,1},{4,6},{5,7},{6,4},{7,5},{8,10},{9,11},{10,... | collective-permute-start | bytes 24584 | tf_op jit(solution)/shard_map/ppermute | solution.py:166
  128.2 1.2 collective-permute-start.10

commit v2 on v1

v2 whole, which is shorter than its diff:
```python
import functools

import jax
import jax.numpy as jnp
from jax import lax
from jax.experimental import pallas as pl
from jax.experimental.pallas import tpu as pltpu
from jax.sharding import PartitionSpec as P

SLOTS = 8
BF = jnp.bfloat16
F32 = jnp.float32


def gathered_rows(block, first, count, width):
    columns = []
    for step in range(count):
        rows = pl.ds(pl.multiple_of(first + step * width, width), width)
        columns.append(jnp.concatenate([block[m, rows, :] for m in range(SLOTS)], axis=0))
    return jnp.concatenate(columns, axis=1)


def product_kernel(slots, width, chunks, me_ref, neighbors_ref, virt_hbm, block_hbm, *refs):
    outs = refs[-5 - len(slots) : -5]
    virt, virt_t, block, virt_sem, sems = refs[-5:]
    me = me_ref[0]
    low, count = slots[0], len(slots)
    ri = block.shape[-1]
    size = block.shape[1] // chunks

    def block_copy(c):
        rows = pl.ds(pl.multiple_of(c * size, size), size)
        return pltpu.make_async_copy(block_hbm.at[0, :, rows, :], block.at[:, rows, :], sems.at[c])

    virt_copy = pltpu.make_async_copy(
        virt_hbm.at[0, :, pl.ds(low * width, count * width)], virt, virt_sem
    )
    virt_copy.start()
    for c in range(chunks):
        block_copy(c).start()
    virt_copy.wait()
    parts = [
        jnp.where(neighbors_ref[m, me] >= 0, virt[m * width : (m + 1) * width, :].astype(F32), 0.0)
        for m in range(SLOTS)
    ]
    turned = jnp.concatenate(parts, axis=0).T
    for at, k in enumerate(slots):
        live = neighbors_ref[k, me] >= 0
        virt_t[at * width : (at + 1) * width, :] = jnp.where(
            live, turned[at * width : (at + 1) * width, :], 0.0
        ).astype(BF)

    @pl.loop(0, chunks)
    def _(c):
        block_copy(c).wait()
        for pair in range(size // width // 2):
            base = c * size + 2 * pair * width
            right = gathered_rows(block, base, 2, width)
            both = jnp.dot(virt_t[...], right, preferred_element_type=F32).astype(BF)
            for at in range(count):
                for half in range(2):
                    rows = pl.ds(pl.multiple_of(base + half * width, width), width)
                    outs[at][rows, :] = both[at * width : (at + 1) * width, half * ri : (half + 1) * ri]


def products(slots, me, neighbors, virt, blocks, chunks, after=None, near=False):
    pairs, ri = blocks.shape[2:]
    wide = virt.shape[1]
    width = wide // SLOTS
    count = len(slots)
    smem = pl.BlockSpec(memory_space=pltpu.SMEM)
    hbm = pl.BlockSpec(memory_space=pltpu.HBM)
    after = [] if after is None else [after]
    return pl.pallas_call(
        functools.partial(product_kernel, slots, width, chunks),
        in_specs=[smem, smem, hbm, hbm] + [pl.BlockSpec(memory_space=pl.ANY)] * len(after),
        out_specs=[pl.BlockSpec(memory_space=pltpu.VMEM)] * count,
        out_shape=[pltpu.VMEM((pairs, ri), BF) if near else pltpu.HBM((pairs, ri), BF)] * count,
        scratch_shapes=[
            pltpu.VMEM((wide, count * width), BF),
            pltpu.VMEM((count * width, wide), BF),
            pltpu.VMEM((SLOTS, pairs, ri), BF),
            pltpu.SemaphoreType.DMA,
            pltpu.SemaphoreType.DMA((chunks,)),
        ],
        compiler_params=pltpu.CompilerParams(vmem_limit_bytes=24 << 20),
        cost_estimate=pl.CostEstimate(flops=1, bytes_accessed=1, transcendentals=0),
        name="products",
    )(me, neighbors, virt, blocks, *after)


def project_kernel(width, rows, me_ref, neighbors_ref, occ_ref, block_ref, *refs):
    outs, occ, turn = refs[:-2], refs[-2], refs[-1]
    me = me_ref[0]
    wide = SLOTS * width

    @pl.when(pl.program_id(0) == 0)
    def _():
        slot = lax.broadcasted_iota(jnp.int32, (1, wide), 1) // width
        keep = jnp.zeros((1, wide), F32)
        for n in range(SLOTS):
            keep = jnp.where((slot == n) & (neighbors_ref[n, me] >= 0), 1.0, keep)
        occ[...] = (occ_ref[0].astype(F32) * keep).astype(BF)

    ri = block_ref.shape[-1]
    for pair in range(rows // 2):
        right = gathered_rows(block_ref.at[0], 2 * pair * width, 2, width)
        both = jnp.dot(occ[...], right, preferred_element_type=F32)
        for half in range(2):
            turn[pl.ds(2 * pair + half, wide, stride=rows), :] = both[:, half * ri : (half + 1) * ri]
    for m in range(SLOTS):
        piece = turn[m * width * rows : (m + 1) * width * rows, :]
        outs[m][...] = piece.astype(BF).reshape(width, rows, ri)


def projections(me, neighbors, occ, blocks, rows=16):
    pairs, ri = blocks.shape[2:]
    wide = occ.shape[1]
    width = wide // SLOTS
    steps = width // rows
    chunk = rows * width
    smem = pl.BlockSpec(memory_space=pltpu.SMEM)
    out = pl.pallas_call(
        functools.partial(project_kernel, width, rows),
        grid=(steps,),
        in_specs=[
            smem,
            smem,
            pl.BlockSpec((1, wide, wide), lambda s: (0, 0, 0)),
            pl.BlockSpec((1, SLOTS, chunk, ri), lambda s: (0, 0, s, 0)),
        ],
        out_specs=[pl.BlockSpec((width, rows, ri), lambda s: (0, s, 0))] * SLOTS,
        out_shape=[pltpu.HBM((width, width, ri), BF)] * SLOTS,
        scratch_shapes=[pltpu.VMEM((wide, wide), BF), pltpu.VMEM((wide * rows, ri), F32)],
        compiler_params=pltpu.CompilerParams(vmem_limit_bytes=20 << 20),
        cost_estimate=pl.CostEstimate(flops=1, bytes_accessed=1, transcendentals=0),
        name="projections",
    )(me, neighbors, occ, blocks)
    return [each.reshape(pairs, ri) for each in out]


def turn_kernel(count, *refs):
    span = refs[0].shape[1]
    for source, out in zip(refs[:count], refs[count:]):

        @pl.loop(0, source.shape[0] // span)
        def _(c):
            at = pl.ds(pl.multiple_of(c * span, span), span)
            out[:, at] = source[at, :].T


def turned(values):
    pairs, ri = values[0].shape
    vmem = pl.BlockSpec(memory_space=pltpu.VMEM)
    return pl.pallas_call(
        functools.partial(turn_kernel, len(values)),
        in_specs=[vmem] * len(values),
        out_specs=[vmem] * len(values),
        out_shape=[pltpu.VMEM((ri, pairs), BF)] * len(values),
        compiler_params=pltpu.CompilerParams(vmem_limit_bytes=12 << 20),
        cost_estimate=pl.CostEstimate(flops=1, bytes_accessed=1, transcendentals=0),
        name="turn",
    )(*values)


def contract_kernel(count, has_start, last, *refs):
    lefts, rights = refs[:count], refs[count : 2 * count]
    out = refs[-1]
    total = refs[2 * count][...] if has_start else None
    for left, right in zip(lefts, rights):
        dims = (((1 if last else 0,), (0,)), ((), ()))
        term = lax.dot_general(left[...], right[...], dims, preferred_element_type=F32)
        total = term if total is None else total + term
    out[...] = total.T if last else total


def contract(lefts, rights, start=None, last=False):
    ri = rights[0].shape[1]
    count = len(lefts)
    starts = [] if start is None else [start]
    vmem = pl.BlockSpec(memory_space=pltpu.VMEM)
    return pl.pallas_call(
        functools.partial(contract_kernel, count, start is not None, last),
        in_specs=[vmem] * (2 * count + len(starts)),
        out_specs=vmem,
        out_shape=pltpu.VMEM((ri, ri), F32),
        compiler_params=pltpu.CompilerParams(vmem_limit_bytes=12 << 20),
        cost_estimate=pl.CostEstimate(flops=1, bytes_accessed=1, transcendentals=0),
        name="contract",
    )(*lefts, *rights, *starts)


def exchange(value, k, devices):
    return lax.ppermute(value, "tensor", [(i, i ^ k) for i in range(devices)])


def reduce_rows(total, devices, order):
    index = lax.axis_index("tensor")
    bits = [1 << b for b in reversed(range(devices.bit_length() - 1))]
    value = total.reshape((2,) * len(bits) + (total.shape[0] // devices, total.shape[1]))
    left = list(bits)
    for k in order:
        at = left.index(k)
        left.pop(at)
        low = lax.index_in_dim(value, 0, at, keepdims=False)
        high = lax.index_in_dim(value, 1, at, keepdims=False)
        upper = (index & k) != 0
        value = jnp.where(upper, high, low) + exchange(jnp.where(upper, low, high), k, devices)
    return value


def local(devices, three_center, occ_green, virt_green, neighbors):
    me = lax.axis_index("tensor").astype(jnp.int32).reshape(1)
    by_slot = pltpu.with_memory_space_constraint(neighbors.T, pltpu.HBM)
    three_center = pltpu.with_memory_space_constraint(three_center, pltpu.HBM)
    occ_green = pltpu.with_memory_space_constraint(occ_green, pltpu.HBM)
    virt_green = pltpu.with_memory_space_constraint(virt_green, pltpu.HBM)
    sides = dict(zip((6, 7), products((6, 7), me, by_slot, virt_green, three_center, 2, near=True)))
    arrived = {k: exchange(sides[k], k, devices) for k in (6, 7)}
    middle = (2, 3, 4, 5)
    sides.update(zip(middle, products(middle, me, by_slot, virt_green, three_center, 4, sides[6])))
    for k in (2, 4, 3, 5):
        arrived[k] = exchange(sides[k], k, devices)
    sides.update(zip((0, 1), products((0, 1), me, by_slot, virt_green, three_center, 2, arrived[6])))
    arrived[0] = sides[0]
    arrived[1] = exchange(sides[1], 1, devices)
    project = projections(me, by_slot, occ_green, three_center)
    project[3], project[5] = turned((project[3], project[5]))
    groups = ((6,), (0, 7), (1, 2, 4), (3, 5))
    total = None
    for group in groups:
        total = contract(
            [project[k] for k in group], [arrived[k] for k in group], total, group is groups[-1]
        )
    bits = [1 << b for b in reversed(range(devices.bit_length() - 1))]
    return reduce_rows(total, devices, bits)


def solution(mesh):
    devices = mesh.shape["tensor"]
    in_specs = (
        P(("group", "tensor"), None, None, None),
        P("tensor", None, None),
        P("tensor", None, None),
        P(),
    )
    out_specs = P(("group", "tensor"), None)
    return jax.shard_map(
        functools.partial(local, devices), mesh=mesh, in_specs=in_specs, out_specs=out_specs, check_vma=False
    )
```

time: 130 us -> 117 us (0.900)
  waiting for transfers between devices: 72.4 us -> 41.7 us
  Pallas kernels: 33.9 us -> 42 us
  local copies, waits for them, and re-layouts: 8.29 us -> 14.4 us
  starting transfers between devices: 14.7 us -> 17.5 us
    ppermute x11, waiting for transfers between devices: 72.4 us -> 41.7 us  [exchange(): return lax.ppermute(value, 'tensor', [(i, i ^ k) for i in range(devices)])]
    pallas_call x2 -> x4, Pallas kernels: 12.4 us -> 24.5 us  [the longest x3 20 us: products(): pl.pallas_call(functools.partial(product_kernel, slots, width, chunks), i...]
    unnamed x15 -> x30, local copies, waits for them, and re-layouts: 8.29 us -> 14.4 us
    pallas_call x4, Pallas kernels: 10.3 us -> 5.77 us  [contract(): pl.pallas_call(functools.partial(contract_kernel, count, start is not Non...]
    ppermute x11, starting transfers between devices: 14.7 us -> 17.5 us  [exchange(): return lax.ppermute(value, 'tensor', [(i, i ^ k) for i in range(devices)])]
  transfers between devices with their start and end apart: 11 -> 11, of which waited for: 9 -> 7; matrix products, arithmetic and copies ran while one was open for 0% -> 0% of each run, Pallas kernels for 18% -> 30%
where the time goes in v2:
time: 117 us; the launch traced here: 116 us
  Pallas kernels  42 us (36%)
  waiting for transfers between devices  41.7 us (36%)
  starting transfers between devices  17.5 us (15%)
  local copies, waits for them, and re-layouts  14.4 us (12%)
    ppermute x11, waiting for transfers between devices, exchange(): return lax.ppermute(value, 'tensor', [(i, i ^ k) for i in range(devices)])  41.7 us
    pallas_call x3, Pallas kernels, products(): pl.pallas_call(functools.partial(product_kernel, slots, width, chunks), i...  20 us
    ppermute x11, starting transfers between devices, exchange(): return lax.ppermute(value, 'tensor', [(i, i ^ k) for i in range(devices)])  17.5 us
    unnamed x30, local copies, waits for them, and re-layouts  14.4 us
    pallas_call x1, Pallas kernels, projections(): pl.pallas_call(functools.partial(project_kernel, width, rows), grid=(step...  11.7 us
    pallas_call x4, Pallas kernels, contract(): pl.pallas_call(functools.partial(contract_kernel, count, start is not Non...  5.77 us
    pallas_call x1, Pallas kernels, turned(): pl.pallas_call(functools.partial(turn_kernel, len(values)), in_specs=[vme...  4.51 us
  transfers between devices with their start and end apart: 11, of which 7 were waited for; matrix products, arithmetic and copies ran while one was open for 0% of the time, Pallas kernels for 30%

profile of v2, /device:TPU:0, one launch (start us, length us, event | category | flops | bytes accessed | tf_op | source)
XLA Modules:
  0.0 116.4 jit_solution(3192744482854380216)
XLA Ops:
  0.0 5.1 %products.3 = (bf16[4096,128]{1,0:T(8,128)(2,1)S(1)}, bf16[4096,128]{1,0:T(8,128)(2,1)S(1)}) custom-call(s32[1]{0:T(128)} %bitcast.me_ref, s32[8,16]{1,0:T(8,128)} %bitcast.33, bf16[1,512,512]{2,1,0:T(8,128)(2,1)} %virt_hbm.5, bf16[1,8,4096,128]{3,2,1,0:T(8,128)(2,1)} %block_hbm.5), custom_call_target="tpu_custom_call" | custom-call | flops 1 | bytes 1 | tf_op jit(solution)/shard_map/products/pallas_call | solution.py:74
  5.1 4.0 %collective-permute-start.2 = (bf16[4096,128]{1,0:T(8,128)(2,1)S(1)}, bf16[4096,128]{1,0:T(8,128)(2,1)S(1)}, u32[]{:S(2)}, u32[]{:S(2)}) collective-permute-start(bf16[4096,128]{1,0:T(8,128)(2,1)S(1)} %get-tuple-element.27.refs_0_), channel_id=1, source_target_pairs={{0,6},{1,7},{2,4},{3,5},{4,2},{5,3},{6,0},{7,1},{8,14},{9,15},{10,... | collective-permute-start | bytes 3145736 | tf_op jit(solution)/shard_map/ppermute | solution.py:194
  9.1 8.5 %products.4 = (bf16[4096,128]{1,0:T(8,128)(2,1)}, bf16[4096,128]{1,0:T(8,128)(2,1)}, bf16[4096,128]{1,0:T(8,128)(2,1)}, bf16[4096,128]{1,0:T(8,128)(2,1)}) custom-call(s32[1]{0:T(128)} %bitcast.me_ref, s32[8,16]{1,0:T(8,128)} %bitcast.34, bf16[1,512,512]{2,1,0:T(8,128)(2,1)} %virt_hbm.5, bf16[1,8,4096,128]{3,2,1,0:T(8,128)(2,1)} %block_hbm.5, ...), custom_call_target="tpu_custom_call" | custom-call | flops 1 | bytes 1 | tf_op jit(solution)/shard_map/products/pallas_call | solution.py:74
  17.6 1.1 collective-permute-start.4
  18.8 1.6 %collective-permute-start.5 = (bf16[4096,128]{1,0:T(8,128)(2,1)}, bf16[4096,128]{1,0:T(8,128)(2,1)S(1)}, u32[]{:S(2)}, u32[]{:S(2)}) collective-permute-start(bf16[4096,128]{1,0:T(8,128)(2,1)} %get-tuple-element.35), channel_id=1, source_target_pairs={{0,4},{1,5},{2,6},{3,7},{4,0},{5,1},{6,2},{7,3},{8,12},{9,13},{10,... | collective-permute-start | bytes 3145736 | tf_op jit(solution)/shard_map/ppermute | solution.py:194
  20.3 12.9 %collective-permute-done.2.refs_0_.refs_1_ = bf16[4096,128]{1,0:T(8,128)(2,1)S(1)} collective-permute-done((bf16[4096,128]{1,0:T(8,128)(2,1)S(1)}, bf16[4096,128]{1,0:T(8,128)(2,1)S(1)}, u32[]{:S(2)}, u32[]{:S(2)}) %collective-permute-start.2) | collective-permute-done | bytes 1048608 | tf_op jit(solution)/shard_map/ppermute | solution.py:194
  33.2 6.5 %products.5 = (bf16[4096,128]{1,0:T(8,128)(2,1)}, bf16[4096,128]{1,0:T(8,128)(2,1)}) custom-call(s32[1]{0:T(128)} %bitcast.me_ref, s32[8,16]{1,0:T(8,128)} %bitcast.35, bf16[1,512,512]{2,1,0:T(8,128)(2,1)} %virt_hbm.5, bf16[1,8,4096,128]{3,2,1,0:T(8,128)(2,1)} %block_hbm.5, bf16[4096,128]{1,0:T(8,128)(2,1)S(1)} %collective-permute-done.2.refs_0_.refs_1_), custom_call_target="tpu_custom_call" | custom-call | flops 1 | bytes 1 | tf_op jit(solution)/shard_map/products/pallas_call | solution.py:74
  39.8 2.1 %collective-permute-start = (bf16[4096,128]{1,0:T(8,128)(2,1)}, bf16[4096,128]{1,0:T(8,128)(2,1)}, u32[]{:S(2)}, u32[]{:S(2)}) collective-permute-start(bf16[4096,128]{1,0:T(8,128)(2,1)} %get-tuple-element.28), channel_id=1, source_target_pairs={{0,3},{1,2},{2,1},{3,0},{4,7},{5,6},{6,5},{7,4},{8,11},{9,10},{10,... | collective-permute-start | bytes 3145736 | tf_op jit(solution)/shard_map/ppermute | solution.py:194
  41.8 13.4 %collective-permute-done.6.refs_3_ = bf16[4096,128]{1,0:T(8,128)(2,1)S(1)} collective-permute-done((bf16[4096,128]{1,0:T(8,128)(2,1)S(1)}, bf16[4096,128]{1,0:T(8,128)(2,1)S(1)}, u32[]{:S(2)}, u32[]{:S(2)}) %collective-permute-start.6) | collective-permute-done | bytes 1048608 | tf_op jit(solution)/shard_map/ppermute | solution.py:194
  55.2 1.8 %collective-permute-start.1 = (bf16[4096,128]{1,0:T(8,128)(2,1)}, bf16[4096,128]{1,0:T(8,128)(2,1)}, u32[]{:S(2)}, u32[]{:S(2)}) collective-permute-start(bf16[4096,128]{1,0:T(8,128)(2,1)} %get-tuple-element.29), channel_id=1, source_target_pairs={{0,5},{1,4},{2,7},{3,6},{4,1},{5,0},{6,3},{7,2},{8,13},{9,12},{10,... | collective-permute-start | bytes 3145736 | tf_op jit(solution)/shard_map/ppermute | solution.py:194
  57.1 11.7 %projections.1 = (bf16[64,64,128]{2,1,0:T(8,128)(2,1)}, bf16[64,64,128]{2,1,0:T(8,128)(2,1)}, bf16[64,64,128]{2,1,0:T(8,128)(2,1)}, bf16[64,64,128]{2,1,0:T(8,12...) custom-call(s32[1]{0:T(128)} %bitcast.me_ref, ...), custom_call_target="tpu_custom_call" | custom-call | flops 1 | bytes 1 | tf_op jit(solution)/shard_map/projections/pallas_call | solution.py:123
  68.8 1.2 %copy-done.4 = bf16[64,64,128]{2,1,0:T(8,128)(2,1)S(1)} copy-done((bf16[64,64,128]{2,1,0:T(8,128)(2,1)S(1)}, bf16[64,64,128]{2,1,0:T(8,128)(2,1)}, u32[]{:S(2)}) %copy-start.4) | copy-done | bytes 1048600
  70.0 1.2 %copy-done.5 = bf16[64,64,128]{2,1,0:T(8,128)(2,1)S(1)} copy-done((bf16[64,64,128]{2,1,0:T(8,128)(2,1)S(1)}, bf16[64,64,128]{2,1,0:T(8,128)(2,1)}, u32[]{:S(2)}) %copy-start.5) | copy-done | bytes 1048600
  71.2 4.5 %turn.1 = (bf16[128,4096]{1,0:T(8,128)(2,1)S(1)}, bf16[128,4096]{1,0:T(8,128)(2,1)S(1)}) custom-call(bf16[4096,128]{1,0:T(8,128)(2,1)S(1)} %bitcast.28, bf16[4096,128]{1,0:T(8,128)(2,1)S(1)} %bitcast.29), custom_call_target="tpu_custom_call" | custom-call | flops 1 | bytes 1 | tf_op jit(solution)/shard_map/turn/pallas_call | solution.py:155
  77.7 1.2 %copy-done.3 = bf16[64,64,128]{2,1,0:T(8,128)(2,1)S(1)} copy-done((bf16[64,64,128]{2,1,0:T(8,128)(2,1)S(1)}, bf16[64,64,128]{2,1,0:T(8,128)(2,1)}, u32[]{:S(2)}) %copy-start.3) | copy-done | bytes 1048600
  79.4 1.4 %copy-done.7 = bf16[4096,128]{1,0:T(8,128)(2,1)S(1)} copy-done((bf16[4096,128]{1,0:T(8,128)(2,1)S(1)}, bf16[4096,128]{1,0:T(8,128)(2,1)}, u32[]{:S(2)}) %copy-start.7) | copy-done | bytes 1048600
  80.8 1.2 %copy-done.12 = bf16[4096,128]{1,0:T(8,128)(2,1)S(1)} copy-done((bf16[4096,128]{1,0:T(8,128)(2,1)S(1)}, bf16[4096,128]{1,0:T(8,128)(2,1)}, u32[]{:S(2)}) %copy-start.12) | copy-done | bytes 1048600
  82.0 1.2 %copy-done.13 = bf16[64,64,128]{2,1,0:T(8,128)(2,1)S(1)} copy-done((bf16[64,64,128]{2,1,0:T(8,128)(2,1)S(1)}, bf16[64,64,128]{2,1,0:T(8,128)(2,1)}, u32[]{:S(2)}) %copy-start.13) | copy-done | bytes 1048600
  83.3 1.2 %copy-done.14 = bf16[64,64,128]{2,1,0:T(8,128)(2,1)S(1)} copy-done((bf16[64,64,128]{2,1,0:T(8,128)(2,1)S(1)}, bf16[64,64,128]{2,1,0:T(8,128)(2,1)}, u32[]{:S(2)}) %copy-start.14) | copy-done | bytes 1048600
  85.3 1.2 %copy-done = bf16[64,64,128]{2,1,0:T(8,128)(2,1)S(1)} copy-done((bf16[64,64,128]{2,1,0:T(8,128)(2,1)S(1)}, bf16[64,64,128]{2,1,0:T(8,128)(2,1)}, u32[]{:S(2)}) %copy-start) | copy-done | bytes 1048600
  86.5 1.2 %copy-done.1 = bf16[64,64,128]{2,1,0:T(8,128)(2,1)S(1)} copy-done((bf16[64,64,128]{2,1,0:T(8,128)(2,1)S(1)}, bf16[64,64,128]{2,1,0:T(8,128)(2,1)}, u32[]{:S(2)}) %copy-start.1) | copy-done | bytes 1048600
  87.7 1.2 %copy-done.2 = bf16[64,64,128]{2,1,0:T(8,128)(2,1)S(1)} copy-done((bf16[64,64,128]{2,1,0:T(8,128)(2,1)S(1)}, bf16[64,64,128]{2,1,0:T(8,128)(2,1)}, u32[]{:S(2)}) %copy-start.2) | copy-done | bytes 1048600
  88.9 2.2 %contract.6.refs_4_ = f32[128,128]{1,0:T(8,128)S(1)} custom-call(bf16[4096,128]{1,0:T(8,128)(2,1)S(1)} %bitcast.24, bf16[4096,128]{1,0:T(8,128)(2,1)S(1)} %bitcast.25, bf16[4096,128]{1,0:T(8,128)(2,1)S(1)} %bitcast.26, bf16[4096,128]{1,0:T(8,128)(2,1)} %collective-permute-done.3.refs_3_, bf16[4096,128]{1,0:T(8,128)(2,1)S(1)} %collective-permute-done.4.refs_4_, ...), custom_call_target="tpu_custom_call" | custom-call | flops 1 | bytes 1 | tf_op jit(solution)/shard_map/contract/pallas_call | solution.py:182
  91.2 8.5 %collective-permute-done.refs_2_ = bf16[4096,128]{1,0:T(8,128)(2,1)} collective-permute-done((bf16[4096,128]{1,0:T(8,128)(2,1)}, bf16[4096,128]{1,0:T(8,128)(2,1)}, u32[]{:S(2)}, u32[]{:S(2)}) %collective-permute-start) | collective-permute-done | bytes 1048608 | tf_op jit(solution)/shard_map/ppermute | solution.py:194
  99.8 2.3 %contract.7 = f32[128,128]{1,0:T(8,128)S(1)} custom-call(bf16[128,4096]{1,0:T(8,128)(2,1)S(1)} %copy-done.9, bf16[128,4096]{1,0:T(8,128)(2,1)S(1)} %copy-done.11, bf16[4096,128]{1,0:T(8,128)(2,1)} %collective-permute-done.refs_2_, bf16[4096,128]{1,0:T(8,128)(2,1)} %collective-permute-done.1.refs_3_, f32[128,128]{1,0:T(8,128)S(1)} %contract.6.refs_4_), custom_call_target="tpu_custom_call" | custom-call | flops 1 | bytes 1 | tf_op jit(solution)/shard_map/contract/pallas_call | solution.py:182
  102.1 2.8 %collective-permute-start.7 = (f32[2,2,2,8,128]{4,3,2,1,0:T(8,128)S(1)}, f32[2,2,2,8,128]{4,3,2,1,0:T(8,128)S(1)}, u32[]{:S(2)}, u32[]{:S(2)}) collective-permute-start(f32[2,2,2,8,128]{4,3,2,1,0:T(8,128)S(1)} %bitcast.37), channel_id=1, source_target_pairs={{0,8},{1,9},{2,10},{3,11},{4,12},{5,13},{6,14},{7,15},{8,0},{9,1},... | collective-permute-start | bytes 98312 | tf_op jit(solution)/shard_map/ppermute | solution.py:194
  104.9 2.1 %collective-permute-done.7 = f32[2,2,2,8,128]{4,3,2,1,0:T(8,128)S(1)} collective-permute-done((f32[2,2,2,8,128]{4,3,2,1,0:T(8,128)S(1)}, f32[2,2,2,8,128]{4,3,2,1,0:T(8,128)S(1)}, u32[]{:S(2)}, u32[]{:S(2)}) %collective-permute-start.7) | collective-permute-done | bytes 32800 | tf_op jit(solution)/shard_map/ppermute | solution.py:194
  107.0 1.8 %collective-permute-start.8 = (f32[2,2,8,128]{3,2,1,0:T(8,128)S(1)}, f32[2,2,8,128]{3,2,1,0:T(8,128)S(1)}, u32[]{:S(2)}, u32[]{:S(2)}) collective-permute-start(f32[2,2,8,128]{3,2,1,0:T(8,128)S(1)} %select_bitcast_fusion), channel_id=1, source_target_pairs={{0,4},{1,5},{2,6},{3,7},{4,0},{5,1},{6,2},{7,3},{8,12},{9,13},{10,... | collective-permute-start | bytes 49160 | tf_op jit(solution)/shard_map/ppermute | solution.py:194
  108.8 2.0 %collective-permute-done.8 = f32[2,2,8,128]{3,2,1,0:T(8,128)S(1)} collective-permute-done((f32[2,2,8,128]{3,2,1,0:T(8,128)S(1)}, f32[2,2,8,128]{3,2,1,0:T(8,128)S(1)}, u32[]{:S(2)}, u32[]{:S(2)}) %collective-permute-start.8) | collective-permute-done | bytes 16416 | tf_op jit(solution)/shard_map/ppermute | solution.py:194
  110.8 2.1 %collective-permute-start.9 = (f32[2,8,128]{2,1,0:T(8,128)S(1)}, f32[2,8,128]{2,1,0:T(8,128)S(1)}, u32[]{:S(2)}, u32[]{:S(2)}) collective-permute-start(f32[2,8,128]{2,1,0:T(8,128)S(1)} %select_bitcast_fusion.1), channel_id=1, source_target_pairs={{0,2},{1,3},{2,0},{3,1},{4,6},{5,7},{6,4},{7,5},{8,10},{9,11},{10,... | collective-permute-start | bytes 24584 | tf_op jit(solution)/shard_map/ppermute | solution.py:194
  112.9 1.6 %collective-permute-done.9 = f32[2,8,128]{2,1,0:T(8,128)S(1)} collective-permute-done((f32[2,8,128]{2,1,0:T(8,128)S(1)}, f32[2,8,128]{2,1,0:T(8,128)S(1)}, u32[]{:S(2)}, u32[]{:S(2)}) %collective-permute-start.9) | collective-permute-done | bytes 8224 | tf_op jit(solution)/shard_map/ppermute | solution.py:194
  114.6 1.2 collective-permute-done.10
  (37 shorter events, 4.0 us)
Async XLA Ops:
  5.1 28.1 %collective-permute-start.2 = (bf16[4096,128]{1,0:T(8,128)(2,1)S(1)}, bf16[4096,128]{1,0:T(8,128)(2,1)S(1)}, u32[]{:S(2)}, u32[]{:S(2)}) collective-permute-start(bf16[4096,128]{1,0:T(8,128)(2,1)S(1)} %get-tuple-element.27.refs_0_), channel_id=1, source_target_pairs={{0,6},{1,7},{2,4},{3,5},{4,2},{5,3},{6,0},{7,1},{8,14},{9,15},{10,... | collective-permute-start | bytes 3145736 | tf_op jit(solution)/shard_map/ppermute | solution.py:194
  9.1 46.1 %collective-permute-start.6 = (bf16[4096,128]{1,0:T(8,128)(2,1)S(1)}, bf16[4096,128]{1,0:T(8,128)(2,1)S(1)}, u32[]{:S(2)}, u32[]{:S(2)}) collective-permute-start(bf16[4096,128]{1,0:T(8,128)(2,1)S(1)} %get-tuple-element.39), channel_id=1, source_target_pairs={{0,7},{1,6},{2,5},{3,4},{4,3},{5,2},{6,1},{7,0},{8,15},{9,14},{10,... | collective-permute-start | bytes 3145736 | tf_op jit(solution)/shard_map/ppermute | solution.py:194
  17.6 67.6 %collective-permute-start.4 = (bf16[4096,128]{1,0:T(8,128)(2,1)}, bf16[4096,128]{1,0:T(8,128)(2,1)S(1)}, u32[]{:S(2)}, u32[]{:S(2)}) collective-permute-start(bf16[4096,128]{1,0:T(8,128)(2,1)} %get-tuple-element.34), channel_id=1, source_target_pairs={{0,2},{1,3},{2,0},{3,1},{4,6},{5,7},{6,4},{7,5},{8,10},{9,11},{10,... | collective-permute-start | bytes 3145736 | tf_op jit(solution)/shard_map/ppermute | solution.py:194
  18.8 66.5 %collective-permute-start.5 = (bf16[4096,128]{1,0:T(8,128)(2,1)}, bf16[4096,128]{1,0:T(8,128)(2,1)S(1)}, u32[]{:S(2)}, u32[]{:S(2)}) collective-permute-start(bf16[4096,128]{1,0:T(8,128)(2,1)} %get-tuple-element.35), channel_id=1, source_target_pairs={{0,4},{1,5},{2,6},{3,7},{4,0},{5,1},{6,2},{7,3},{8,12},{9,13},{10,... | collective-permute-start | bytes 3145736 | tf_op jit(solution)/shard_map/ppermute | solution.py:194
  39.7 45.6 %collective-permute-start.3 = (bf16[4096,128]{1,0:T(8,128)(2,1)}, bf16[4096,128]{1,0:T(8,128)(2,1)}, u32[]{:S(2)}, u32[]{:S(2)}) collective-permute-start(bf16[4096,128]{1,0:T(8,128)(2,1)} %get-tuple-element.33), channel_id=1, source_target_pairs={{0,1},{1,0},{2,3},{3,2},{4,5},{5,4},{6,7},{7,6},{8,9},{9,8},{10,11... | collective-permute-start | bytes 3145736 | tf_op jit(solution)/shard_map/ppermute | solution.py:194
  39.8 60.0 %collective-permute-start = (bf16[4096,128]{1,0:T(8,128)(2,1)}, bf16[4096,128]{1,0:T(8,128)(2,1)}, u32[]{:S(2)}, u32[]{:S(2)}) collective-permute-start(bf16[4096,128]{1,0:T(8,128)(2,1)} %get-tuple-element.28), channel_id=1, source_target_pairs={{0,3},{1,2},{2,1},{3,0},{4,7},{5,6},{6,5},{7,4},{8,11},{9,10},{10,... | collective-permute-start | bytes 3145736 | tf_op jit(solution)/shard_map/ppermute | solution.py:194
  55.2 13.6 %copy-start.6 = (bf16[4096,128]{1,0:T(8,128)(2,1)}, bf16[4096,128]{1,0:T(8,128)(2,1)S(1)}, u32[]{:S(2)}) copy-start(bf16[4096,128]{1,0:T(8,128)(2,1)S(1)} %collective-permute-done.6.refs_3_) | copy-start | bytes 3145732
  55.2 44.5 %collective-permute-start.1 = (bf16[4096,128]{1,0:T(8,128)(2,1)}, bf16[4096,128]{1,0:T(8,128)(2,1)}, u32[]{:S(2)}, u32[]{:S(2)}) collective-permute-start(bf16[4096,128]{1,0:T(8,128)(2,1)} %get-tuple-element.29), channel_id=1, source_target_pairs={{0,5},{1,4},{2,7},{3,6},{4,1},{5,0},{6,3},{7,2},{8,13},{9,12},{10,... | collective-permute-start | bytes 3145736 | tf_op jit(solution)/shard_map/ppermute | solution.py:194
  68.8 1.2 %copy-start.4 = (bf16[64,64,128]{2,1,0:T(8,128)(2,1)S(1)}, bf16[64,64,128]{2,1,0:T(8,128)(2,1)}, u32[]{:S(2)}) copy-start(bf16[64,64,128]{2,1,0:T(8,128)(2,1)} %get-tuple-element.23) | copy-start | bytes 3145732
  70.0 1.2 %copy-start.5 = (bf16[64,64,128]{2,1,0:T(8,128)(2,1)S(1)}, bf16[64,64,128]{2,1,0:T(8,128)(2,1)}, u32[]{:S(2)}) copy-start(bf16[64,64,128]{2,1,0:T(8,128)(2,1)} %get-tuple-element.24) | copy-start | bytes 3145732
  75.7 1.0 copy-start.8
  76.8 1.0 copy-start.10
  77.7 1.2 %copy-start.3 = (bf16[64,64,128]{2,1,0:T(8,128)(2,1)S(1)}, bf16[64,64,128]{2,1,0:T(8,128)(2,1)}, u32[]{:S(2)}) copy-start(bf16[64,64,128]{2,1,0:T(8,128)(2,1)} %get-tuple-element.40) | copy-start | bytes 3145732
  79.0 20.8 %copy-start.9 = (bf16[128,4096]{1,0:T(8,128)(2,1)S(1)}, bf16[128,4096]{1,0:T(8,128)(2,1)}, u32[]{:S(2)}) copy-start(bf16[128,4096]{1,0:T(8,128)(2,1)} %copy-done.8) | copy-start | bytes 3145732
  79.0 20.8 %copy-start.11 = (bf16[128,4096]{1,0:T(8,128)(2,1)S(1)}, bf16[128,4096]{1,0:T(8,128)(2,1)}, u32[]{:S(2)}) copy-start(bf16[128,4096]{1,0:T(8,128)(2,1)} %copy-done.10) | copy-start | bytes 3145732
  79.4 1.4 %copy-start.7 = (bf16[4096,128]{1,0:T(8,128)(2,1)S(1)}, bf16[4096,128]{1,0:T(8,128)(2,1)}, u32[]{:S(2)}) copy-start(bf16[4096,128]{1,0:T(8,128)(2,1)} %copy-done.6) | copy-start | bytes 3145732
  80.8 1.2 %copy-start.12 = (bf16[4096,128]{1,0:T(8,128)(2,1)S(1)}, bf16[4096,128]{1,0:T(8,128)(2,1)}, u32[]{:S(2)}) copy-start(bf16[4096,128]{1,0:T(8,128)(2,1)} %get-tuple-element.38.refs_2_) | copy-start | bytes 3145732
  82.0 1.2 %copy-start.13 = (bf16[64,64,128]{2,1,0:T(8,128)(2,1)S(1)}, bf16[64,64,128]{2,1,0:T(8,128)(2,1)}, u32[]{:S(2)}) copy-start(bf16[64,64,128]{2,1,0:T(8,128)(2,1)} %get-tuple-element.36) | copy-start | bytes 3145732
  83.3 1.2 %copy-start.14 = (bf16[64,64,128]{2,1,0:T(8,128)(2,1)S(1)}, bf16[64,64,128]{2,1,0:T(8,128)(2,1)}, u32[]{:S(2)}) copy-start(bf16[64,64,128]{2,1,0:T(8,128)(2,1)} %get-tuple-element.37) | copy-start | bytes 3145732
  85.3 1.2 %copy-start = (bf16[64,64,128]{2,1,0:T(8,128)(2,1)S(1)}, bf16[64,64,128]{2,1,0:T(8,128)(2,1)}, u32[]{:S(2)}) copy-start(bf16[64,64,128]{2,1,0:T(8,128)(2,1)} %get-tuple-element.30) | copy-start | bytes 3145732
  86.5 1.2 %copy-start.1 = (bf16[64,64,128]{2,1,0:T(8,128)(2,1)S(1)}, bf16[64,64,128]{2,1,0:T(8,128)(2,1)}, u32[]{:S(2)}) copy-start(bf16[64,64,128]{2,1,0:T(8,128)(2,1)} %get-tuple-element.31) | copy-start | bytes 3145732
  87.7 1.2 %copy-start.2 = (bf16[64,64,128]{2,1,0:T(8,128)(2,1)S(1)}, bf16[64,64,128]{2,1,0:T(8,128)(2,1)}, u32[]{:S(2)}) copy-start(bf16[64,64,128]{2,1,0:T(8,128)(2,1)} %get-tuple-element.32) | copy-start | bytes 3145732
  102.1 4.9 %collective-permute-start.7 = (f32[2,2,2,8,128]{4,3,2,1,0:T(8,128)S(1)}, f32[2,2,2,8,128]{4,3,2,1,0:T(8,128)S(1)}, u32[]{:S(2)}, u32[]{:S(2)}) collective-permute-start(f32[2,2,2,8,128]{4,3,2,1,0:T(8,128)S(1)} %bitcast.37), channel_id=1, source_target_pairs={{0,8},{1,9},{2,10},{3,11},{4,12},{5,13},{6,14},{7,15},{8,0},{9,1},... | collective-permute-start | bytes 98312 | tf_op jit(solution)/shard_map/ppermute | solution.py:194
  107.0 3.8 %collective-permute-start.8 = (f32[2,2,8,128]{3,2,1,0:T(8,128)S(1)}, f32[2,2,8,128]{3,2,1,0:T(8,128)S(1)}, u32[]{:S(2)}, u32[]{:S(2)}) collective-permute-start(f32[2,2,8,128]{3,2,1,0:T(8,128)S(1)} %select_bitcast_fusion), channel_id=1, source_target_pairs={{0,4},{1,5},{2,6},{3,7},{4,0},{5,1},{6,2},{7,3},{8,12},{9,13},{10,... | collective-permute-start | bytes 49160 | tf_op jit(solution)/shard_map/ppermute | solution.py:194
  110.8 3.7 %collective-permute-start.9 = (f32[2,8,128]{2,1,0:T(8,128)S(1)}, f32[2,8,128]{2,1,0:T(8,128)S(1)}, u32[]{:S(2)}, u32[]{:S(2)}) collective-permute-start(f32[2,8,128]{2,1,0:T(8,128)S(1)} %select_bitcast_fusion.1), channel_id=1, source_target_pairs={{0,2},{1,3},{2,0},{3,1},{4,6},{5,7},{6,4},{7,5},{8,10},{9,11},{10,... | collective-permute-start | bytes 24584 | tf_op jit(solution)/shard_map/ppermute | solution.py:194
  114.5 1.2 %collective-permute-start.10 = (f32[8,128]{1,0:T(8,128)S(1)}, f32[8,128]{1,0:T(8,128)S(1)}, u32[]{:S(2)}, u32[]{:S(2)}) collective-permute-start(f32[8,128]{1,0:T(8,128)S(1)} %select_bitcast_fusion.2), channel_id=1, source_target_pairs={{0,1},{1,0},{2,3},{3,2},{4,5},{5,4},{6,7},{7,6},{8,9},{9,8},{10,11... | collective-permute-start | bytes 12296 | tf_op jit(solution)/shard_map/ppermute | solution.py:194

commit v3 on v2

--- a/solution.py
+++ b/solution.py
@@ -20,25 +20,7 @@
     return jnp.concatenate(columns, axis=1)
 
 
-def product_kernel(slots, width, chunks, me_ref, neighbors_ref, virt_hbm, block_hbm, *refs):
-    outs = refs[-5 - len(slots) : -5]
-    virt, virt_t, block, virt_sem, sems = refs[-5:]
-    me = me_ref[0]
-    low, count = slots[0], len(slots)
-    ri = block.shape[-1]
-    size = block.shape[1] // chunks
-
-    def block_copy(c):
-        rows = pl.ds(pl.multiple_of(c * size, size), size)
-        return pltpu.make_async_copy(block_hbm.at[0, :, rows, :], block.at[:, rows, :], sems.at[c])
-
-    virt_copy = pltpu.make_async_copy(
-        virt_hbm.at[0, :, pl.ds(low * width, count * width)], virt, virt_sem
-    )
-    virt_copy.start()
-    for c in range(chunks):
-        block_copy(c).start()
-    virt_copy.wait()
+def masked_turned(slots, width, me, neighbors_ref, virt, virt_t):
     parts = [
         jnp.where(neighbors_ref[m, me] >= 0, virt[m * width : (m + 1) * width, :].astype(F32), 0.0)
         for m in range(SLOTS)
@@ -49,6 +31,28 @@
         virt_t[at * width : (at + 1) * width, :] = jnp.where(
             live, turned[at * width : (at + 1) * width, :], 0.0
         ).astype(BF)
+
+
+def product_kernel(slots, width, chunks, me_ref, neighbors_ref, virt_hbm, block_hbm, *refs):
+    outs = refs[-5 - len(slots) : -5]
+    virt, virt_t, block, virt_sem, sems = refs[-5:]
+    me = me_ref[0]
+    low, count = slots[0], len(slots)
+    ri = block.shape[-1]
+    size = block.shape[1] // chunks
+
+    def block_copy(c):
+        rows = pl.ds(pl.multiple_of(c * size, size), size)
+        return pltpu.make_async_copy(block_hbm.at[0, :, rows, :], block.at[:, rows, :], sems.at[c])
+
+    virt_copy = pltpu.make_async_copy(
+        virt_hbm.at[0, :, pl.ds(low * width, count * width)], virt, virt_sem
+    )
+    virt_copy.start()
+    for c in range(chunks):
+        block_copy(c).start()
+    virt_copy.wait()
+    masked_turned(slots, width, me, neighbors_ref, virt, virt_t)
 
     @pl.loop(0, chunks)
     def _(c):
@@ -89,7 +93,87 @@
     )(me, neighbors, virt, blocks, *after)
 
 
-def project_kernel(width, rows, me_ref, neighbors_ref, occ_ref, block_ref, *refs):
+def turned_product_kernel(slots, width, chunks, slab, cuts, me_ref, neighbors_ref, virt_hbm, block_hbm, *refs):
+    count = len(slots)
+    outs = refs[-7 - sum(len(each) for each in cuts) : -7]
+    virt, virt_t, block, sides, virt_sem, sems, out_sems = refs[-7:]
+    me = me_ref[0]
+    low = slots[0]
+    ri = block.shape[-1]
+    size = block.shape[1] // chunks
+
+    def block_copy(c):
+        rows = pl.ds(pl.multiple_of(c * size, size), size)
+        return pltpu.make_async_copy(block_hbm.at[0, :, rows, :], block.at[:, rows, :], sems.at[c])
+
+    virt_copy = pltpu.make_async_copy(
+        virt_hbm.at[0, :, pl.ds(low * width, count * width)], virt, virt_sem
+    )
+    virt_copy.start()
+    for c in range(chunks):
+        block_copy(c).start()
+    virt_copy.wait()
+    masked_turned(slots, width, me, neighbors_ref, virt, virt_t)
+
+    @pl.loop(0, chunks)
+    def _(c):
+        block_copy(c).wait()
+        for pair in range(size // width // 2):
+            base = c * size + 2 * pair * width
+            right = gathered_rows(block, base, 2, width)
+            both = jnp.dot(virt_t[...], right, preferred_element_type=F32).astype(BF)
+            lanes = pl.ds(pl.multiple_of(base, 2 * width), 2 * width)
+            for at in range(count):
+                mine = both[at * width : (at + 1) * width, :]
+                rows = jnp.concatenate([mine[:, :ri], mine[:, ri:]], axis=0)
+                sides[at, :, lanes] = rows.T
+
+    copies = []
+    outs = list(outs)
+    for at, k in enumerate(slots):
+        chip = (me ^ k) >> 1
+        for first, last in cuts[at]:
+            out = outs.pop(0)
+            for g in range(first, last):
+                source = pl.ds(pl.multiple_of((chip ^ g) * slab, slab), slab)
+                target = out.at[pl.ds((g - first) * slab, slab), :]
+                copies.append(pltpu.make_async_copy(sides.at[at, source, :], target, out_sems.at[len(copies)]))
+    for copy in copies:
+        copy.start()
+    for copy in copies:
+        copy.wait()
+
+
+def turned_products(slots, me, neighbors, virt, blocks, chunks, slab, cuts, after):
+    pairs, ri = blocks.shape[2:]
+    wide = virt.shape[1]
+    width = wide // SLOTS
+    count = len(slots)
+    smem = pl.BlockSpec(memory_space=pltpu.SMEM)
+    hbm = pl.BlockSpec(memory_space=pltpu.HBM)
+    out = pl.pallas_call(
+        functools.partial(turned_product_kernel, slots, width, chunks, slab, cuts),
+        in_specs=[smem, smem, hbm, hbm, pl.BlockSpec(memory_space=pl.ANY)],
+        out_specs=[hbm] * sum(len(each) for each in cuts),
+        out_shape=[pltpu.HBM(((last - first) * slab, pairs), BF) for each in cuts for first, last in each],
+        scratch_shapes=[
+            pltpu.VMEM((wide, count * width), BF),
+            pltpu.VMEM((count * width, wide), BF),
+            pltpu.VMEM((SLOTS, pairs, ri), BF),
+            pltpu.VMEM((count, ri, pairs), BF),
+            pltpu.SemaphoreType.DMA,
+            pltpu.SemaphoreType.DMA((chunks,)),
+            pltpu.SemaphoreType.DMA((count * ri // slab,)),
+        ],
+        compiler_params=pltpu.CompilerParams(vmem_limit_bytes=24 << 20),
+        cost_estimate=pl.CostEstimate(flops=1, bytes_accessed=1, transcendentals=0),
+        name="turned_products",
+    )(me, neighbors, virt, blocks, after)
+    out = list(out)
+    return {k: [out.pop(0) for _ in cuts[at]] for at, k in enumerate(slots)}
+
+
+def project_kernel(width, rows, me_ref, neighbors_ref, occ_ref, block_ref, after_ref, *refs):
     outs, occ, turn = refs[:-2], refs[-2], refs[-1]
     me = me_ref[0]
     wide = SLOTS * width
@@ -113,7 +197,7 @@
         outs[m][...] = piece.astype(BF).reshape(width, rows, ri)
 
 
-def projections(me, neighbors, occ, blocks, rows=16):
+def projections(me, neighbors, occ, blocks, after, rows=16):
     pairs, ri = blocks.shape[2:]
     wide = occ.shape[1]
     width = wide // SLOTS
@@ -128,66 +212,88 @@
             smem,
             pl.BlockSpec((1, wide, wide), lambda s: (0, 0, 0)),
             pl.BlockSpec((1, SLOTS, chunk, ri), lambda s: (0, 0, s, 0)),
+            pl.BlockSpec(memory_space=pl.ANY),
         ],
         out_specs=[pl.BlockSpec((width, rows, ri), lambda s: (0, s, 0))] * SLOTS,
-        out_shape=[pltpu.HBM((width, width, ri), BF)] * SLOTS,
+        out_shape=[(pltpu.VMEM if m in (3, 5) else pltpu.HBM)((width, width, ri), BF) for m in range(SLOTS)],
         scratch_shapes=[pltpu.VMEM((wide, wide), BF), pltpu.VMEM((wide * rows, ri), F32)],
-        compiler_params=pltpu.CompilerParams(vmem_limit_bytes=20 << 20),
+        compiler_params=pltpu.CompilerParams(vmem_limit_bytes=17 << 20),
         cost_estimate=pl.CostEstimate(flops=1, bytes_accessed=1, transcendentals=0),
         name="projections",
-    )(me, neighbors, occ, blocks)
+    )(me, neighbors, occ, blocks, after)
     return [each.reshape(pairs, ri) for each in out]
 
 
-def turn_kernel(count, *refs):
-    span = refs[0].shape[1]
-    for source, out in zip(refs[:count], refs[count:]):
-
-        @pl.loop(0, source.shape[0] // span)
-        def _(c):
-            at = pl.ds(pl.multiple_of(c * span, span), span)
-            out[:, at] = source[at, :].T
-
-
-def turned(values):
-    pairs, ri = values[0].shape
-    vmem = pl.BlockSpec(memory_space=pltpu.VMEM)
-    return pl.pallas_call(
-        functools.partial(turn_kernel, len(values)),
-        in_specs=[vmem] * len(values),
-        out_specs=[vmem] * len(values),
-        out_shape=[pltpu.VMEM((ri, pairs), BF)] * len(values),
-        compiler_params=pltpu.CompilerParams(vmem_limit_bytes=12 << 20),
-        cost_estimate=pl.CostEstimate(flops=1, bytes_accessed=1, transcendentals=0),
-        name="turn",
-    )(*values)
-
-
-def contract_kernel(count, has_start, last, *refs):
-    lefts, rights = refs[:count], refs[count : 2 * count]
-    out = refs[-1]
+def contract_kernel(count, has_start, *refs):
+    out = refs[2 * count + has_start + (len(refs) - 2 * count - has_start - 1) // 2]
     total = refs[2 * count][...] if has_start else None
-    for left, right in zip(lefts, rights):
-        dims = (((1 if last else 0,), (0,)), ((), ()))
-        term = lax.dot_general(left[...], right[...], dims, preferred_element_type=F32)
+    for left, right in zip(refs[:count], refs[count : 2 * count]):
+        term = lax.dot_general(left[...], right[...], (((0,), (0,)), ((), ())), preferred_element_type=F32)
         total = term if total is None else total + term
-    out[...] = total.T if last else total
-
-
-def contract(lefts, rights, start=None, last=False):
-    ri = rights[0].shape[1]
+    out[...] = total
+
+
+def contract(lefts, rights, start=None, passed=()):
+    pairs, ri = rights[0].shape
     count = len(lefts)
     starts = [] if start is None else [start]
     vmem = pl.BlockSpec(memory_space=pltpu.VMEM)
+    anywhere = pl.BlockSpec(memory_space=pl.ANY)
     return pl.pallas_call(
-        functools.partial(contract_kernel, count, start is not None, last),
-        in_specs=[vmem] * (2 * count + len(starts)),
-        out_specs=vmem,
-        out_shape=pltpu.VMEM((ri, ri), F32),
-        compiler_params=pltpu.CompilerParams(vmem_limit_bytes=12 << 20),
+        functools.partial(contract_kernel, count, len(starts)),
+        in_specs=[vmem] * (2 * count + len(starts)) + [anywhere] * len(passed),
+        out_specs=[vmem] + [anywhere] * len(passed),
+        out_shape=[pltpu.VMEM((ri, ri), F32)] + [pltpu.HBM(each.shape, each.dtype) for each in passed],
+        input_output_aliases={2 * count + len(starts) + at: 1 + at for at in range(len(passed))},
+        compiler_params=pltpu.CompilerParams(vmem_limit_bytes=8 << 20),
         cost_estimate=pl.CostEstimate(flops=1, bytes_accessed=1, transcendentals=0),
         name="contract",
-    )(*lefts, *rights, *starts)
+    )(*lefts, *rights, *starts, *passed)
+
+
+def rows_kernel(count, rows, slab, bases, me_ref, *refs):
+    lefts, rights = refs[:count], refs[count : 2 * count]
+    rest = refs[2 * count : 2 * count + len(bases)]
+    passed = (len(refs) - 2 * count - len(bases) - len(rows)) // 2
+    outs = refs[2 * count + len(bases) + passed :][: len(rows)]
+    chip = me_ref[0] >> 1
+    height = sum(rows)
+    total = jnp.zeros((height, rights[0].shape[1]), F32)
+    for left, right in zip(lefts, rights):
+        total += jnp.dot(left[...], right[...], preferred_element_type=F32)
+    for base, (kind, first) in zip(rest, bases):
+        if kind == "all":
+            pieces = []
+            for g in range(first, first + height // slab):
+                pieces.append(base[pl.ds(pl.multiple_of((chip ^ g) * slab, slab), slab), :])
+            total += jnp.concatenate(pieces, axis=0) if len(pieces) > 1 else pieces[0]
+        else:
+            total += base[...]
+    at = 0
+    for out, each in zip(outs, rows):
+        out[...] = total[at : at + each, :]
+        at += each
+
+
+def contract_rows(me, lefts, rights, rows, slab, bases=(), passed=()):
+    ri = rights[0].shape[1]
+    count = len(lefts)
+    vmem = pl.BlockSpec(memory_space=pltpu.VMEM)
+    anywhere = pl.BlockSpec(memory_space=pl.ANY)
+    kinds = tuple((kind, first) for kind, first, _ in bases)
+    return pl.pallas_call(
+        functools.partial(rows_kernel, count, rows, slab, kinds),
+        in_specs=[pl.BlockSpec(memory_space=pltpu.SMEM)]
+        + [vmem] * (2 * count + len(bases))
+        + [anywhere] * len(passed),
+        out_specs=[vmem] * len(rows) + [anywhere] * len(passed),
+        out_shape=[pltpu.VMEM((each, ri), F32) for each in rows]
+        + [pltpu.HBM(each.shape, each.dtype) for each in passed],
+        input_output_aliases={1 + 2 * count + len(bases) + at: len(rows) + at for at in range(len(passed))},
+        compiler_params=pltpu.CompilerParams(vmem_limit_bytes=8 << 20),
+        cost_estimate=pl.CostEstimate(flops=20_000_000_000, bytes_accessed=1, transcendentals=0),
+        name="contract_rows",
+    )(me, *lefts, *rights, *[array for _, _, array in bases], *passed)
 
 
 def exchange(value, k, devices):
@@ -218,22 +324,67 @@
     sides = dict(zip((6, 7), products((6, 7), me, by_slot, virt_green, three_center, 2, near=True)))
     arrived = {k: exchange(sides[k], k, devices) for k in (6, 7)}
     middle = (2, 3, 4, 5)
-    sides.update(zip(middle, products(middle, me, by_slot, virt_green, three_center, 4, sides[6])))
-    for k in (2, 4, 3, 5):
-        arrived[k] = exchange(sides[k], k, devices)
-    sides.update(zip((0, 1), products((0, 1), me, by_slot, virt_green, three_center, 2, arrived[6])))
+    slab = 2 * three_center.shape[-1] // devices
+    by_owner = devices == 16 and slab == 16
+    if by_owner:
+        cuts = (((4, 8), (0, 4)), ((4, 8), (1, 4), (0, 1)), ((4, 8), (0, 4)), ((4, 8), (1, 4), (0, 1)))
+        pieces = turned_products(
+            middle, me, by_slot, virt_green, three_center, 4, slab, cuts, sides[6]
+        )
+        latest = pieces[5][0]
+    else:
+        sides.update(zip(middle, products(middle, me, by_slot, virt_green, three_center, 4, sides[6])))
+        for k in middle:
+            arrived[k] = exchange(sides[k], k, devices)
+        latest = sides[5]
+    sides.update(zip((0, 1), products((0, 1), me, by_slot, virt_green, three_center, 2, latest)))
+    project = projections(me, by_slot, occ_green, three_center, sides[0])
     arrived[0] = sides[0]
     arrived[1] = exchange(sides[1], 1, devices)
-    project = projections(me, by_slot, occ_green, three_center)
-    project[3], project[5] = turned((project[3], project[5]))
-    groups = ((6,), (0, 7), (1, 2, 4), (3, 5))
-    total = None
-    for group in groups:
-        total = contract(
-            [project[k] for k in group], [arrived[k] for k in group], total, group is groups[-1]
-        )
-    bits = [1 << b for b in reversed(range(devices.bit_length() - 1))]
-    return reduce_rows(total, devices, bits)
+    first, second = (2, 4), (3, 5)
+    passed = [pieces[k][0] for k in second] if by_owner else []
+    total, *passed = contract([arrived[k] for k in (6, 0)], [project[k] for k in (6, 0)], None, passed)
+    if not by_owner:
+        for group in ((7, 1), first, second):
+            (total,) = contract([arrived[k] for k in group], [project[k] for k in group], total)
+        bits = [1 << b for b in reversed(range(devices.bit_length() - 1))]
+        return reduce_rows(total, devices, bits)
+
+    def send(values, slots):
+        return [exchange(value, k, devices) for k, value in zip(slots, values)]
+
+    first_rights = [project[k] for k in first]
+    second_rights = [project[k] for k in second]
+    first_far = send([pieces[k][0] for k in first], first)
+    second_far = send(passed, second)
+    (total,) = contract([arrived[k] for k in (7, 1)], [project[k] for k in (7, 1)], total)
+    outer, *passed = contract_rows(
+        me, first_far, first_rights, (4 * slab,), slab, [("all", 4, total)], [pieces[k][1] for k in first]
+    )
+    first_own = send(passed, first)
+    outer, *passed = contract_rows(
+        me, second_far, second_rights, (4 * slab,), slab, [("own", 0, outer)], [pieces[k][1] for k in second]
+    )
+    inner = exchange(outer, 8, devices)
+    second_mid = send(passed, second)
+    chip, rest, *passed = contract_rows(
+        me,
+        first_own,
+        first_rights,
+        (slab, 3 * slab),
+        slab,
+        [("all", 0, total), ("own", 0, inner)],
+        [pieces[k][2] for k in second],
+    )
+    second_near = send(passed, second)
+    square = contract_rows(me, second_mid, second_rights, (slab,) * 3, slab, [("own", 0, rest)])
+    square = [exchange(value, 2 * (at + 1), devices) for at, value in enumerate(square)]
+    (chip,) = contract_rows(me, second_near, second_rights, (slab,), slab, [("own", 0, chip)])
+    chip = chip + square[0] + square[1] + square[2]
+    half = slab // 2
+    upper = (lax.axis_index("tensor") & 1) != 0
+    keep = jnp.where(upper, chip[half:], chip[:half])
+    return keep + exchange(jnp.where(upper, chip[:half], chip[half:]), 1, devices)
 
 
 def solution(mesh):

time: 117 us -> 107 us (0.915)
  local copies, waits for them, and re-layouts: 14.4 us -> 8.39 us
  Pallas kernels: 42 us -> 37.5 us
  starting transfers between devices: 17.5 us -> 21.6 us
  waiting for transfers between devices: 41.7 us -> 38.7 us
    pallas_call x3 -> x2, Pallas kernels: 20 us -> 11.6 us  [products(): pl.pallas_call(functools.partial(product_kernel, slots, width, chunks), i...]
    unnamed x30 -> x22, local copies, waits for them, and re-layouts: 14.4 us -> 8.39 us
    pallas_call x5 -> x8, Pallas kernels: 10.3 us -> 14.5 us  [the longest x1 9.58 us: turned_products(): pl.pallas_call(functools.partial(turned_product_kernel, slots, width, chu...]
    ppermute x11 -> x18, starting transfers between devices: 17.5 us -> 21.6 us  [exchange(): return lax.ppermute(value, 'tensor', [(i, i ^ k) for i in range(devices)])]
    ppermute x11 -> x18, waiting for transfers between devices: 41.7 us -> 38.7 us  [exchange(): return lax.ppermute(value, 'tensor', [(i, i ^ k) for i in range(devices)])]
  transfers between devices with their start and end apart: 11 -> 18, of which waited for: 7 -> 12; matrix products, arithmetic and copies ran while one was open for 0% -> 0% of each run, Pallas kernels for 30% -> 30%
where the time goes in v3:
time: 107 us
  waiting for transfers between devices  38.7 us (36%)
  Pallas kernels  37.5 us (35%)
  starting transfers between devices  21.6 us (20%)
  local copies, waits for them, and re-layouts  8.39 us (8%)
    ppermute x18, waiting for transfers between devices, exchange(): return lax.ppermute(value, 'tensor', [(i, i ^ k) for i in range(devices)])  38.7 us
    ppermute x18, starting transfers between devices, exchange(): return lax.ppermute(value, 'tensor', [(i, i ^ k) for i in range(devices)])  21.6 us
    pallas_call x2, Pallas kernels, products(): pl.pallas_call(functools.partial(product_kernel, slots, width, chunks), i...  11.6 us
    pallas_call x1, Pallas kernels, projections(): pl.pallas_call(functools.partial(project_kernel, width, rows), grid=(step...  11.4 us
    pallas_call x1, Pallas kernels, turned_products(): pl.pallas_call(functools.partial(turned_product_kernel, slots, width, chu...  9.58 us
    unnamed x22, local copies, waits for them, and re-layouts  8.39 us
    pallas_call x5, Pallas kernels, contract_rows(): pl.pallas_call(functools.partial(rows_kernel, count, rows, slab, kinds),...  3.43 us
  transfers between devices with their start and end apart: 18, of which 12 were waited for; matrix products, arithmetic and copies ran while one was open for 0% of the time, Pallas kernels for 30%

profile of v3, /device:TPU:0, one launch (start us, length us, event | category | flops | bytes accessed | tf_op | source)
XLA Modules:
  0.0 106.9 jit_solution(8275819821176623262)
XLA Ops:
  0.0 5.1 %products.2 = (bf16[4096,128]{1,0:T(8,128)(2,1)S(1)}, bf16[4096,128]{1,0:T(8,128)(2,1)S(1)}) custom-call(s32[1]{0:T(128)} %bitcast.me_ref, s32[8,16]{1,0:T(8,128)} %bitcast.24, bf16[1,512,512]{2,1,0:T(8,128)(2,1)} %virt_hbm.5, bf16[1,8,4096,128]{3,2,1,0:T(8,128)(2,1)} %block_ref.1), custom_call_target="tpu_custom_call" | custom-call | flops 1 | bytes 1 | tf_op jit(solution)/shard_map/products/pallas_call | solution.py:78
  5.1 4.0 %collective-permute-start.4 = (bf16[4096,128]{1,0:T(8,128)(2,1)S(1)}, bf16[4096,128]{1,0:T(8,128)(2,1)S(1)}, u32[]{:S(2)}, u32[]{:S(2)}) collective-permute-start(bf16[4096,128]{1,0:T(8,128)(2,1)S(1)} %get-tuple-element.43.refs_0_), channel_id=1, source_target_pairs={{0,6},{1,7},{2,4},{3,5},{4,2},{5,3},{6,0},{7,1},{8,14},{9,15},{10,... | collective-permute-start | bytes 3145736 | tf_op jit(solution)/shard_map/ppermute | solution.py:300
  9.1 9.6 %turned_products.1 = (bf16[64,4096]{1,0:T(8,128)(2,1)}, bf16[64,4096]{1,0:T(8,128)(2,1)}, bf16[64,4096]{1,0:T(8,128)(2,1)}, bf16[48,4096]{1,0:T(8,128)(2,1)}, bf...) custom-call(s32[1]{0:T(128)} %bitcast.me_ref, ...), custom_call_target="tpu_custom_call" | custom-call | flops 1 | bytes 1 | tf_op jit(solution)/shard_map/turned_products/pallas_call | solution.py:154
  18.7 1.0 copy-done.1
  19.8 6.5 %products.3 = (bf16[4096,128]{1,0:T(8,128)(2,1)}, bf16[4096,128]{1,0:T(8,128)(2,1)}) custom-call(s32[1]{0:T(128)} %bitcast.me_ref, s32[8,16]{1,0:T(8,128)} %bitcast.26, bf16[1,512,512]{2,1,0:T(8,128)(2,1)} %virt_hbm.5, bf16[1,8,4096,128]{3,2,1,0:T(8,128)(2,1)} %block_ref.1, bf16[64,4096]{1,0:T(8,128)(2,1)S(1)} %copy-done.1), custom_call_target="tpu_custom_call" | custom-call | flops 1 | bytes 1 | tf_op jit(solution)/shard_map/products/pallas_call | solution.py:78
  26.5 1.9 %collective-permute-start = (bf16[64,4096]{1,0:T(8,128)(2,1)S(1)}, bf16[64,4096]{1,0:T(8,128)(2,1)S(1)}, u32[]{:S(2)}, u32[]{:S(2)}) collective-permute-start(bf16[64,4096]{1,0:T(8,128)(2,1)S(1)} %copy-done.10), channel_id=1, source_target_pairs={{0,2},{1,3},{2,0},{3,1},{4,6},{5,7},{6,4},{7,5},{8,10},{9,11},{10,... | collective-permute-start | bytes 1572872 | tf_op jit(solution)/shard_map/ppermute | solution.py:300
  28.4 1.6 %collective-permute-start.1 = (bf16[64,4096]{1,0:T(8,128)(2,1)S(1)}, bf16[64,4096]{1,0:T(8,128)(2,1)S(1)}, u32[]{:S(2)}, u32[]{:S(2)}) collective-permute-start(bf16[64,4096]{1,0:T(8,128)(2,1)S(1)} %copy-done.9), channel_id=1, source_target_pairs={{0,4},{1,5},{2,6},{3,7},{4,0},{5,1},{6,2},{7,3},{8,12},{9,13},{10,... | collective-permute-start | bytes 1572872 | tf_op jit(solution)/shard_map/ppermute | solution.py:300
  30.0 1.2 %copy-done = bf16[4096,128]{1,0:T(8,128)(2,1)S(1)} copy-done((bf16[4096,128]{1,0:T(8,128)(2,1)S(1)}, bf16[4096,128]{1,0:T(8,128)(2,1)}, u32[]{:S(2)}) %copy-start) | copy-done | bytes 1048600
  31.2 11.4 %projections.1 = (bf16[64,64,128]{2,1,0:T(8,128)(2,1)}, bf16[64,64,128]{2,1,0:T(8,128)(2,1)}, bf16[64,64,128]{2,1,0:T(8,128)(2,1)}, bf16[64,64,128]{2,1,0:T(8,12...) custom-call(s32[1]{0:T(128)} %bitcast.me_ref, ...), custom_call_target="tpu_custom_call" | custom-call | flops 1 | bytes 1 | tf_op jit(solution)/shard_map/projections/pallas_call | solution.py:207
  42.6 1.2 %copy-done.2 = bf16[64,64,128]{2,1,0:T(8,128)(2,1)S(1)} copy-done((bf16[64,64,128]{2,1,0:T(8,128)(2,1)S(1)}, bf16[64,64,128]{2,1,0:T(8,128)(2,1)}, u32[]{:S(2)}) %copy-start.2) | copy-done | bytes 1048600
  43.8 1.2 %copy-done.3 = bf16[64,64,128]{2,1,0:T(8,128)(2,1)S(1)} copy-done((bf16[64,64,128]{2,1,0:T(8,128)(2,1)S(1)}, bf16[64,64,128]{2,1,0:T(8,128)(2,1)}, u32[]{:S(2)}) %copy-start.3) | copy-done | bytes 1048600
  46.2 9.0 %collective-permute-done.2.refs_0_ = bf16[4096,128]{1,0:T(8,128)(2,1)S(1)} collective-permute-done((bf16[4096,128]{1,0:T(8,128)(2,1)S(1)}, bf16[4096,128]{1,0:T(8,128)(2,1)S(1)}, u32[]{:S(2)}, u32[]{:S(2)}) %collective-permute-start.2) | collective-permute-done | bytes 1048608 | tf_op jit(solution)/shard_map/ppermute | solution.py:300
  55.2 1.2 %copy-done.4 = bf16[64,64,128]{2,1,0:T(8,128)(2,1)S(1)} copy-done((bf16[64,64,128]{2,1,0:T(8,128)(2,1)S(1)}, bf16[64,64,128]{2,1,0:T(8,128)(2,1)}, u32[]{:S(2)}) %copy-start.4) | copy-done | bytes 1048600
  56.4 1.2 %copy-done.5 = bf16[64,64,128]{2,1,0:T(8,128)(2,1)S(1)} copy-done((bf16[64,64,128]{2,1,0:T(8,128)(2,1)S(1)}, bf16[64,64,128]{2,1,0:T(8,128)(2,1)}, u32[]{:S(2)}) %copy-start.5) | copy-done | bytes 1048600
  57.7 0.7 contract.3.refs_4_
  58.4 7.6 %collective-permute-done.refs_0_ = bf16[64,4096]{1,0:T(8,128)(2,1)S(1)} collective-permute-done((bf16[64,4096]{1,0:T(8,128)(2,1)S(1)}, bf16[64,4096]{1,0:T(8,128)(2,1)S(1)}, u32[]{:S(2)}, u32[]{:S(2)}) %collective-permute-start) | collective-permute-done | bytes 524320 | tf_op jit(solution)/shard_map/ppermute | solution.py:300
  66.1 1.3 %collective-permute-done.1.refs_1_ = bf16[64,4096]{1,0:T(8,128)(2,1)S(1)} collective-permute-done((bf16[64,4096]{1,0:T(8,128)(2,1)S(1)}, bf16[64,4096]{1,0:T(8,128)(2,1)S(1)}, u32[]{:S(2)}, u32[]{:S(2)}) %collective-permute-start.1) | collective-permute-done | bytes 524320 | tf_op jit(solution)/shard_map/ppermute | solution.py:300
  68.3 1.7 %collective-permute-start.6 = (bf16[64,4096]{1,0:T(8,128)(2,1)}, bf16[64,4096]{1,0:T(8,128)(2,1)}, u32[]{:S(2)}, u32[]{:S(2)}) collective-permute-start(bf16[64,4096]{1,0:T(8,128)(2,1)} %get-tuple-element.61), channel_id=1, source_target_pairs={{0,4},{1,5},{2,6},{3,7},{4,0},{5,1},{6,2},{7,3},{8,12},{9,13},{10,... | collective-permute-start | bytes 1572872 | tf_op jit(solution)/shard_map/ppermute | solution.py:300
  70.0 7.2 %collective-permute-done.7.refs_0_ = bf16[64,4096]{1,0:T(8,128)(2,1)S(1)} collective-permute-done((bf16[64,4096]{1,0:T(8,128)(2,1)}, bf16[64,4096]{1,0:T(8,128)(2,1)S(1)}, u32[]{:S(2)}, u32[]{:S(2)}) %collective-permute-start.7) | collective-permute-done | bytes 524320 | tf_op jit(solution)/shard_map/ppermute | solution.py:300
  78.3 2.6 %collective-permute-start.9 = (f32[64,128]{1,0:T(8,128)S(1)}, f32[64,128]{1,0:T(8,128)S(1)}, u32[]{:S(2)}, u32[]{:S(2)}) collective-permute-start(f32[64,128]{1,0:T(8,128)S(1)} %get-tuple-element.69), channel_id=1, source_target_pairs={{0,8},{1,9},{2,10},{3,11},{4,12},{5,13},{6,14},{7,15},{8,0},{9,1},... | collective-permute-start | bytes 98312 | tf_op jit(solution)/shard_map/ppermute | solution.py:300
  80.9 0.9 collective-permute-start.12
  81.8 1.4 %collective-permute-start.13 = (bf16[48,4096]{1,0:T(8,128)(2,1)}, bf16[48,4096]{1,0:T(8,128)(2,1)S(1)}, u32[]{:S(2)}, u32[]{:S(2)}) collective-permute-start(bf16[48,4096]{1,0:T(8,128)(2,1)} %get-tuple-element.76), channel_id=1, source_target_pairs={{0,5},{1,4},{2,7},{3,6},{4,1},{5,0},{6,3},{7,2},{8,13},{9,12},{10,... | collective-permute-start | bytes 1179656 | tf_op jit(solution)/shard_map/ppermute | solution.py:300
  83.2 5.4 %collective-permute-done.5.refs_0_ = bf16[64,4096]{1,0:T(8,128)(2,1)} collective-permute-done((bf16[64,4096]{1,0:T(8,128)(2,1)}, bf16[64,4096]{1,0:T(8,128)(2,1)}, u32[]{:S(2)}, u32[]{:S(2)}) %collective-permute-start.5) | collective-permute-done | bytes 524320 | tf_op jit(solution)/shard_map/ppermute | solution.py:300
  88.6 2.0 %collective-permute-done.6.refs_1_ = bf16[64,4096]{1,0:T(8,128)(2,1)} collective-permute-done((bf16[64,4096]{1,0:T(8,128)(2,1)}, bf16[64,4096]{1,0:T(8,128)(2,1)}, u32[]{:S(2)}, u32[]{:S(2)}) %collective-permute-start.6) | collective-permute-done | bytes 524320 | tf_op jit(solution)/shard_map/ppermute | solution.py:300
  90.6 1.2 %copy-done.8 = bf16[64,64,128]{2,1,0:T(8,128)(2,1)S(1)} copy-done((bf16[64,64,128]{2,1,0:T(8,128)(2,1)S(1)}, bf16[64,64,128]{2,1,0:T(8,128)(2,1)}, u32[]{:S(2)}) %copy-start.8) | copy-done | bytes 1048600
  91.9 1.7 %contract_rows.7 = (f32[16,128]{1,0:T(8,128)S(1)}, f32[48,128]{1,0:T(8,128)S(1)}, bf16[16,4096]{1,0:T(8,128)(2,1)}, bf16[16,4096]{1,0:T(8,128)(2,1)}) custom-call(s32[1]{0:T(128)} %bitcast.me_ref, bf16[64,4096]{1,0:T(8,128)(2,1)} %collective-permute-done.5.refs_0_, ...), custom_call_target="tpu_custom_call", output_to_operand_aliasing={{2}: (7, {}), {3}: (8, {})} | custom-call | flops 20000000000 | bytes 1 | tf_op jit(solution)/shard_map/contract_rows/pallas_call | solution.py:284
  93.6 2.7 %collective-permute-start.11 = (bf16[16,4096]{1,0:T(8,128)(2,1)}, bf16[16,4096]{1,0:T(8,128)(2,1)S(1)}, u32[]{:S(2)}, u32[]{:S(2)}) collective-permute-start(bf16[16,4096]{1,0:T(8,128)(2,1)} %get-tuple-element.73), channel_id=1, source_target_pairs={{0,5},{1,4},{2,7},{3,6},{4,1},{5,0},{6,3},{7,2},{8,13},{9,12},{10,... | collective-permute-start | bytes 393224 | tf_op jit(solution)/shard_map/ppermute | solution.py:300
  97.5 1.5 %collective-permute-start.14 = (f32[16,128]{1,0:T(8,128)S(1)}, f32[16,128]{1,0:T(8,128)S(1)}, u32[]{:S(2)}, u32[]{:S(2)}) collective-permute-start(f32[16,128]{1,0:T(8,128)S(1)} %get-tuple-element.78), channel_id=1, source_target_pairs={{0,2},{1,3},{2,0},{3,1},{4,6},{5,7},{6,4},{7,5},{8,10},{9,11},{10,... | collective-permute-start | bytes 24584 | tf_op jit(solution)/shard_map/ppermute | solution.py:300
  99.0 1.6 %collective-permute-start.15 = (f32[16,128]{1,0:T(8,128)S(1)}, f32[16,128]{1,0:T(8,128)S(1)}, u32[]{:S(2)}, u32[]{:S(2)}) collective-permute-start(f32[16,128]{1,0:T(8,128)S(1)} %get-tuple-element.79), channel_id=1, source_target_pairs={{0,4},{1,5},{2,6},{3,7},{4,0},{5,1},{6,2},{7,3},{8,12},{9,13},{10,... | collective-permute-start | bytes 24584 | tf_op jit(solution)/shard_map/ppermute | solution.py:300
  101.4 1.2 %collective-permute-done.15 = f32[16,128]{1,0:T(8,128)S(1)} collective-permute-done((f32[16,128]{1,0:T(8,128)S(1)}, f32[16,128]{1,0:T(8,128)S(1)}, u32[]{:S(2)}, u32[]{:S(2)}) %collective-permute-start.15) | collective-permute-done | bytes 8224 | tf_op jit(solution)/shard_map/ppermute | solution.py:300
  102.6 2.5 %collective-permute-done.16 = f32[16,128]{1,0:T(8,128)S(1)} collective-permute-done((f32[16,128]{1,0:T(8,128)S(1)}, f32[16,128]{1,0:T(8,128)S(1)}, u32[]{:S(2)}, u32[]{:S(2)}) %collective-permute-start.16) | collective-permute-done | bytes 8224 | tf_op jit(solution)/shard_map/ppermute | solution.py:300
  105.2 1.2 %collective-permute-done.17 = f32[8,128]{1,0:T(8,128)S(1)} collective-permute-done((f32[8,128]{1,0:T(8,128)S(1)}, f32[8,128]{1,0:T(8,128)S(1)}, u32[]{:S(2)}, u32[]{:S(2)}) %collective-permute-start.17) | collective-permute-done | bytes 4128 | tf_op jit(solution)/shard_map/ppermute | solution.py:300
  (40 shorter events, 6.1 us)
Async XLA Ops:
  5.1 37.5 %collective-permute-start.4 = (bf16[4096,128]{1,0:T(8,128)(2,1)S(1)}, bf16[4096,128]{1,0:T(8,128)(2,1)S(1)}, u32[]{:S(2)}, u32[]{:S(2)}) collective-permute-start(bf16[4096,128]{1,0:T(8,128)(2,1)S(1)} %get-tuple-element.43.refs_0_), channel_id=1, source_target_pairs={{0,6},{1,7},{2,4},{3,5},{4,2},{5,3},{6,0},{7,1},{8,14},{9,15},{10,... | collective-permute-start | bytes 3145736 | tf_op jit(solution)/shard_map/ppermute | solution.py:300
  18.7 1.0 copy-start.1
  19.8 6.8 %copy-start.10 = (bf16[64,4096]{1,0:T(8,128)(2,1)S(1)}, bf16[64,4096]{1,0:T(8,128)(2,1)}, u32[]{:S(2)}) copy-start(bf16[64,4096]{1,0:T(8,128)(2,1)} %get-tuple-element.44) | copy-start | bytes 1572868
  19.8 8.7 %copy-start.9 = (bf16[64,4096]{1,0:T(8,128)(2,1)S(1)}, bf16[64,4096]{1,0:T(8,128)(2,1)}, u32[]{:S(2)}) copy-start(bf16[64,4096]{1,0:T(8,128)(2,1)} %get-tuple-element.45) | copy-start | bytes 1572868
  26.3 19.6 %collective-permute-start.3 = (bf16[4096,128]{1,0:T(8,128)(2,1)}, bf16[4096,128]{1,0:T(8,128)(2,1)S(1)}, u32[]{:S(2)}, u32[]{:S(2)}) collective-permute-start(bf16[4096,128]{1,0:T(8,128)(2,1)} %get-tuple-element.51), channel_id=1, source_target_pairs={{0,1},{1,0},{2,3},{3,2},{4,5},{5,4},{6,7},{7,6},{8,9},{9,8},{10,11... | collective-permute-start | bytes 3145736 | tf_op jit(solution)/shard_map/ppermute | solution.py:300
  26.4 28.8 %collective-permute-start.2 = (bf16[4096,128]{1,0:T(8,128)(2,1)S(1)}, bf16[4096,128]{1,0:T(8,128)(2,1)S(1)}, u32[]{:S(2)}, u32[]{:S(2)}) collective-permute-start(bf16[4096,128]{1,0:T(8,128)(2,1)S(1)} %get-tuple-element.50), channel_id=1, source_target_pairs={{0,7},{1,6},{2,5},{3,4},{4,3},{5,2},{6,1},{7,0},{8,15},{9,14},{10,... | collective-permute-start | bytes 3145736 | tf_op jit(solution)/shard_map/ppermute | solution.py:300
  26.5 39.5 %collective-permute-start = (bf16[64,4096]{1,0:T(8,128)(2,1)S(1)}, bf16[64,4096]{1,0:T(8,128)(2,1)S(1)}, u32[]{:S(2)}, u32[]{:S(2)}) collective-permute-start(bf16[64,4096]{1,0:T(8,128)(2,1)S(1)} %copy-done.10), channel_id=1, source_target_pairs={{0,2},{1,3},{2,0},{3,1},{4,6},{5,7},{6,4},{7,5},{8,10},{9,11},{10,... | collective-permute-start | bytes 1572872 | tf_op jit(solution)/shard_map/ppermute | solution.py:300
  28.4 38.9 %collective-permute-start.1 = (bf16[64,4096]{1,0:T(8,128)(2,1)S(1)}, bf16[64,4096]{1,0:T(8,128)(2,1)S(1)}, u32[]{:S(2)}, u32[]{:S(2)}) collective-permute-start(bf16[64,4096]{1,0:T(8,128)(2,1)S(1)} %copy-done.9), channel_id=1, source_target_pairs={{0,4},{1,5},{2,6},{3,7},{4,0},{5,1},{6,2},{7,3},{8,12},{9,13},{10,... | collective-permute-start | bytes 1572872 | tf_op jit(solution)/shard_map/ppermute | solution.py:300
  30.0 1.2 %copy-start = (bf16[4096,128]{1,0:T(8,128)(2,1)S(1)}, bf16[4096,128]{1,0:T(8,128)(2,1)}, u32[]{:S(2)}) copy-start(bf16[4096,128]{1,0:T(8,128)(2,1)} %get-tuple-element.47.after_ref.refs_1_) | copy-start | bytes 3145732
  42.6 1.2 %copy-start.2 = (bf16[64,64,128]{2,1,0:T(8,128)(2,1)S(1)}, bf16[64,64,128]{2,1,0:T(8,128)(2,1)}, u32[]{:S(2)}) copy-start(bf16[64,64,128]{2,1,0:T(8,128)(2,1)} %get-tuple-element.55) | copy-start | bytes 3145732
  43.8 1.2 %copy-start.3 = (bf16[64,64,128]{2,1,0:T(8,128)(2,1)S(1)}, bf16[64,64,128]{2,1,0:T(8,128)(2,1)}, u32[]{:S(2)}) copy-start(bf16[64,64,128]{2,1,0:T(8,128)(2,1)} %get-tuple-element.54) | copy-start | bytes 3145732
  45.1 22.3 %copy-start.6 = (bf16[64,64,128]{2,1,0:T(8,128)(2,1)S(1)}, bf16[64,64,128]{2,1,0:T(8,128)(2,1)}, u32[]{:S(2)}) copy-start(bf16[64,64,128]{2,1,0:T(8,128)(2,1)} %get-tuple-element.48) | copy-start | bytes 3145732
  45.1 22.3 %copy-start.7 = (bf16[64,64,128]{2,1,0:T(8,128)(2,1)S(1)}, bf16[64,64,128]{2,1,0:T(8,128)(2,1)}, u32[]{:S(2)}) copy-start(bf16[64,64,128]{2,1,0:T(8,128)(2,1)} %get-tuple-element.49) | copy-start | bytes 3145732
  45.8 31.4 %collective-permute-start.7 = (bf16[64,4096]{1,0:T(8,128)(2,1)}, bf16[64,4096]{1,0:T(8,128)(2,1)S(1)}, u32[]{:S(2)}, u32[]{:S(2)}) collective-permute-start(bf16[64,4096]{1,0:T(8,128)(2,1)} %get-tuple-element.62), channel_id=1, source_target_pairs={{0,3},{1,2},{2,1},{3,0},{4,7},{5,6},{6,5},{7,4},{8,11},{9,10},{10,... | collective-permute-start | bytes 1572872 | tf_op jit(solution)/shard_map/ppermute | solution.py:300
  45.9 31.9 %collective-permute-start.8 = (bf16[64,4096]{1,0:T(8,128)(2,1)}, bf16[64,4096]{1,0:T(8,128)(2,1)S(1)}, u32[]{:S(2)}, u32[]{:S(2)}) collective-permute-start(bf16[64,4096]{1,0:T(8,128)(2,1)} %get-tuple-element.63), channel_id=1, source_target_pairs={{0,5},{1,4},{2,7},{3,6},{4,1},{5,0},{6,3},{7,2},{8,13},{9,12},{10,... | collective-permute-start | bytes 1572872 | tf_op jit(solution)/shard_map/ppermute | solution.py:300
  55.2 1.2 %copy-start.4 = (bf16[64,64,128]{2,1,0:T(8,128)(2,1)S(1)}, bf16[64,64,128]{2,1,0:T(8,128)(2,1)}, u32[]{:S(2)}) copy-start(bf16[64,64,128]{2,1,0:T(8,128)(2,1)} %get-tuple-element.53) | copy-start | bytes 3145732
  56.4 1.2 %copy-start.5 = (bf16[64,64,128]{2,1,0:T(8,128)(2,1)S(1)}, bf16[64,64,128]{2,1,0:T(8,128)(2,1)}, u32[]{:S(2)}) copy-start(bf16[64,64,128]{2,1,0:T(8,128)(2,1)} %get-tuple-element.52) | copy-start | bytes 3145732
  67.8 20.8 %collective-permute-start.5 = (bf16[64,4096]{1,0:T(8,128)(2,1)}, bf16[64,4096]{1,0:T(8,128)(2,1)}, u32[]{:S(2)}, u32[]{:S(2)}) collective-permute-start(bf16[64,4096]{1,0:T(8,128)(2,1)} %get-tuple-element.60), channel_id=1, source_target_pairs={{0,2},{1,3},{2,0},{3,1},{4,6},{5,7},{6,4},{7,5},{8,10},{9,11},{10,... | collective-permute-start | bytes 1572872 | tf_op jit(solution)/shard_map/ppermute | solution.py:300
  68.3 22.4 %collective-permute-start.6 = (bf16[64,4096]{1,0:T(8,128)(2,1)}, bf16[64,4096]{1,0:T(8,128)(2,1)}, u32[]{:S(2)}, u32[]{:S(2)}) collective-permute-start(bf16[64,4096]{1,0:T(8,128)(2,1)} %get-tuple-element.61), channel_id=1, source_target_pairs={{0,4},{1,5},{2,6},{3,7},{4,0},{5,1},{6,2},{7,3},{8,12},{9,13},{10,... | collective-permute-start | bytes 1572872 | tf_op jit(solution)/shard_map/ppermute | solution.py:300
  78.3 12.4 %collective-permute-start.9 = (f32[64,128]{1,0:T(8,128)S(1)}, f32[64,128]{1,0:T(8,128)S(1)}, u32[]{:S(2)}, u32[]{:S(2)}) collective-permute-start(f32[64,128]{1,0:T(8,128)S(1)} %get-tuple-element.69), channel_id=1, source_target_pairs={{0,8},{1,9},{2,10},{3,11},{4,12},{5,13},{6,14},{7,15},{8,0},{9,1},... | collective-permute-start | bytes 98312 | tf_op jit(solution)/shard_map/ppermute | solution.py:300
  80.9 15.9 %collective-permute-start.12 = (bf16[48,4096]{1,0:T(8,128)(2,1)}, bf16[48,4096]{1,0:T(8,128)(2,1)S(1)}, u32[]{:S(2)}, u32[]{:S(2)}) collective-permute-start(bf16[48,4096]{1,0:T(8,128)(2,1)} %get-tuple-element.75), channel_id=1, source_target_pairs={{0,3},{1,2},{2,1},{3,0},{4,7},{5,6},{6,5},{7,4},{8,11},{9,10},{10,... | collective-permute-start | bytes 1179656 | tf_op jit(solution)/shard_map/ppermute | solution.py:300
  81.8 15.2 %collective-permute-start.13 = (bf16[48,4096]{1,0:T(8,128)(2,1)}, bf16[48,4096]{1,0:T(8,128)(2,1)S(1)}, u32[]{:S(2)}, u32[]{:S(2)}) collective-permute-start(bf16[48,4096]{1,0:T(8,128)(2,1)} %get-tuple-element.76), channel_id=1, source_target_pairs={{0,5},{1,4},{2,7},{3,6},{4,1},{5,0},{6,3},{7,2},{8,13},{9,12},{10,... | collective-permute-start | bytes 1179656 | tf_op jit(solution)/shard_map/ppermute | solution.py:300
  90.6 1.2 %copy-start.8 = (bf16[64,64,128]{2,1,0:T(8,128)(2,1)S(1)}, bf16[64,64,128]{2,1,0:T(8,128)(2,1)}, u32[]{:S(2)}) copy-start(bf16[64,64,128]{2,1,0:T(8,128)(2,1)} %get-tuple-element.49) | copy-start | bytes 3145732
  93.5 7.5 %collective-permute-start.10 = (bf16[16,4096]{1,0:T(8,128)(2,1)}, bf16[16,4096]{1,0:T(8,128)(2,1)S(1)}, u32[]{:S(2)}, u32[]{:S(2)}) collective-permute-start(bf16[16,4096]{1,0:T(8,128)(2,1)} %get-tuple-element.72), channel_id=1, source_target_pairs={{0,3},{1,2},{2,1},{3,0},{4,7},{5,6},{6,5},{7,4},{8,11},{9,10},{10,... | collective-permute-start | bytes 393224 | tf_op jit(solution)/shard_map/ppermute | solution.py:300
  93.6 7.4 %collective-permute-start.11 = (bf16[16,4096]{1,0:T(8,128)(2,1)}, bf16[16,4096]{1,0:T(8,128)(2,1)S(1)}, u32[]{:S(2)}, u32[]{:S(2)}) collective-permute-start(bf16[16,4096]{1,0:T(8,128)(2,1)} %get-tuple-element.73), channel_id=1, source_target_pairs={{0,5},{1,4},{2,7},{3,6},{4,1},{5,0},{6,3},{7,2},{8,13},{9,12},{10,... | collective-permute-start | bytes 393224 | tf_op jit(solution)/shard_map/ppermute | solution.py:300
  97.5 4.0 %collective-permute-start.14 = (f32[16,128]{1,0:T(8,128)S(1)}, f32[16,128]{1,0:T(8,128)S(1)}, u32[]{:S(2)}, u32[]{:S(2)}) collective-permute-start(f32[16,128]{1,0:T(8,128)S(1)} %get-tuple-element.78), channel_id=1, source_target_pairs={{0,2},{1,3},{2,0},{3,1},{4,6},{5,7},{6,4},{7,5},{8,10},{9,11},{10,... | collective-permute-start | bytes 24584 | tf_op jit(solution)/shard_map/ppermute | solution.py:300
  99.0 3.7 %collective-permute-start.15 = (f32[16,128]{1,0:T(8,128)S(1)}, f32[16,128]{1,0:T(8,128)S(1)}, u32[]{:S(2)}, u32[]{:S(2)}) collective-permute-start(f32[16,128]{1,0:T(8,128)S(1)} %get-tuple-element.79), channel_id=1, source_target_pairs={{0,4},{1,5},{2,6},{3,7},{4,0},{5,1},{6,2},{7,3},{8,12},{9,13},{10,... | collective-permute-start | bytes 24584 | tf_op jit(solution)/shard_map/ppermute | solution.py:300
  100.5 4.5 %collective-permute-start.16 = (f32[16,128]{1,0:T(8,128)S(1)}, f32[16,128]{1,0:T(8,128)S(1)}, u32[]{:S(2)}, u32[]{:S(2)}) collective-permute-start(f32[16,128]{1,0:T(8,128)S(1)} %get-tuple-element.80), channel_id=1, source_target_pairs={{0,6},{1,7},{2,4},{3,5},{4,2},{5,3},{6,0},{7,1},{8,14},{9,15},{10,... | collective-permute-start | bytes 24584 | tf_op jit(solution)/shard_map/ppermute | solution.py:300
  105.1 1.2 %collective-permute-start.17 = (f32[8,128]{1,0:T(8,128)S(1)}, f32[8,128]{1,0:T(8,128)S(1)}, u32[]{:S(2)}, u32[]{:S(2)}) collective-permute-start(f32[8,128]{1,0:T(8,128)S(1)} %slice_select_fusion), channel_id=1, source_target_pairs={{0,1},{1,0},{2,3},{3,2},{4,5},{5,4},{6,7},{7,6},{8,9},{9,8},{10,11... | collective-permute-start | bytes 12296 | tf_op jit(solution)/shard_map/ppermute | solution.py:300

commit v4 on v3

--- a/solution.py
+++ b/solution.py
@@ -33,10 +33,10 @@
         ).astype(BF)
 
 
-def product_kernel(slots, width, chunks, me_ref, neighbors_ref, virt_hbm, block_hbm, *refs):
-    outs = refs[-5 - len(slots) : -5]
-    virt, virt_t, block, virt_sem, sems = refs[-5:]
-    me = me_ref[0]
+def product_kernel(slots, width, chunks, neighbors_hbm, virt_hbm, block_hbm, *refs):
+    outs = refs[-7 - len(slots) : -7]
+    neighbors_ref, virt, virt_t, block, neighbors_sem, virt_sem, sems = refs[-7:]
+    me = lax.axis_index("tensor")
     low, count = slots[0], len(slots)
     ri = block.shape[-1]
     size = block.shape[1] // chunks
@@ -48,9 +48,12 @@
     virt_copy = pltpu.make_async_copy(
         virt_hbm.at[0, :, pl.ds(low * width, count * width)], virt, virt_sem
     )
+    neighbors_copy = pltpu.make_async_copy(neighbors_hbm, neighbors_ref, neighbors_sem)
+    neighbors_copy.start()
     virt_copy.start()
     for c in range(chunks):
         block_copy(c).start()
+    neighbors_copy.wait()
     virt_copy.wait()
     masked_turned(slots, width, me, neighbors_ref, virt, virt_t)
 
@@ -67,30 +70,31 @@
                     outs[at][rows, :] = both[at * width : (at + 1) * width, half * ri : (half + 1) * ri]
 
 
-def products(slots, me, neighbors, virt, blocks, chunks, after=None, near=False):
+def products(slots, neighbors, virt, blocks, chunks, after=None, near=False):
     pairs, ri = blocks.shape[2:]
     wide = virt.shape[1]
     width = wide // SLOTS
     count = len(slots)
-    smem = pl.BlockSpec(memory_space=pltpu.SMEM)
     hbm = pl.BlockSpec(memory_space=pltpu.HBM)
     after = [] if after is None else [after]
     return pl.pallas_call(
         functools.partial(product_kernel, slots, width, chunks),
-        in_specs=[smem, smem, hbm, hbm] + [pl.BlockSpec(memory_space=pl.ANY)] * len(after),
+        in_specs=[hbm, hbm, hbm] + [pl.BlockSpec(memory_space=pl.ANY)] * len(after),
         out_specs=[pl.BlockSpec(memory_space=pltpu.VMEM)] * count,
         out_shape=[pltpu.VMEM((pairs, ri), BF) if near else pltpu.HBM((pairs, ri), BF)] * count,
         scratch_shapes=[
+            pltpu.SMEM(neighbors.shape, jnp.int32),
             pltpu.VMEM((wide, count * width), BF),
             pltpu.VMEM((count * width, wide), BF),
             pltpu.VMEM((SLOTS, pairs, ri), BF),
+            pltpu.SemaphoreType.DMA,
             pltpu.SemaphoreType.DMA,
             pltpu.SemaphoreType.DMA((chunks,)),
         ],
         compiler_params=pltpu.CompilerParams(vmem_limit_bytes=24 << 20),
         cost_estimate=pl.CostEstimate(flops=1, bytes_accessed=1, transcendentals=0),
         name="products",
-    )(me, neighbors, virt, blocks, *after)
+    )(neighbors, virt, blocks, *after)
 
 
 def turned_product_kernel(slots, width, chunks, slab, cuts, me_ref, neighbors_ref, virt_hbm, block_hbm, *refs):
@@ -215,7 +219,7 @@
             pl.BlockSpec(memory_space=pl.ANY),
         ],
         out_specs=[pl.BlockSpec((width, rows, ri), lambda s: (0, s, 0))] * SLOTS,
-        out_shape=[(pltpu.VMEM if m in (3, 5) else pltpu.HBM)((width, width, ri), BF) for m in range(SLOTS)],
+        out_shape=[(pltpu.VMEM if m in (2, 3, 4, 5) else pltpu.HBM)((width, width, ri), BF) for m in range(SLOTS)],
         scratch_shapes=[pltpu.VMEM((wide, wide), BF), pltpu.VMEM((wide * rows, ri), F32)],
         compiler_params=pltpu.CompilerParams(vmem_limit_bytes=17 << 20),
         cost_estimate=pl.CostEstimate(flops=1, bytes_accessed=1, transcendentals=0),
@@ -251,14 +255,15 @@
     )(*lefts, *rights, *starts, *passed)
 
 
-def rows_kernel(count, rows, slab, bases, me_ref, *refs):
+def rows_kernel(count, rows, slab, bases, after, me_ref, *refs):
     lefts, rights = refs[:count], refs[count : 2 * count]
     rest = refs[2 * count : 2 * count + len(bases)]
-    passed = (len(refs) - 2 * count - len(bases) - len(rows)) // 2
-    outs = refs[2 * count + len(bases) + passed :][: len(rows)]
+    skip = 2 * count + len(bases) + after
+    skip += (len(refs) - skip - len(rows)) // 2
+    outs = refs[skip : skip + len(rows)]
     chip = me_ref[0] >> 1
     height = sum(rows)
-    total = jnp.zeros((height, rights[0].shape[1]), F32)
+    total = jnp.zeros((height, rest[0].shape[1]), F32)
     for left, right in zip(lefts, rights):
         total += jnp.dot(left[...], right[...], preferred_element_type=F32)
     for base, (kind, first) in zip(rest, bases):
@@ -268,32 +273,32 @@
                 pieces.append(base[pl.ds(pl.multiple_of((chip ^ g) * slab, slab), slab), :])
             total += jnp.concatenate(pieces, axis=0) if len(pieces) > 1 else pieces[0]
         else:
-            total += base[...]
+            total += base[first : first + height, :]
     at = 0
     for out, each in zip(outs, rows):
         out[...] = total[at : at + each, :]
         at += each
 
 
-def contract_rows(me, lefts, rights, rows, slab, bases=(), passed=()):
-    ri = rights[0].shape[1]
+def contract_rows(me, lefts, rights, rows, slab, bases=(), passed=(), after=()):
+    ri = bases[0][2].shape[1]
     count = len(lefts)
     vmem = pl.BlockSpec(memory_space=pltpu.VMEM)
     anywhere = pl.BlockSpec(memory_space=pl.ANY)
     kinds = tuple((kind, first) for kind, first, _ in bases)
     return pl.pallas_call(
-        functools.partial(rows_kernel, count, rows, slab, kinds),
+        functools.partial(rows_kernel, count, rows, slab, kinds, len(after)),
         in_specs=[pl.BlockSpec(memory_space=pltpu.SMEM)]
-        + [vmem] * (2 * count + len(bases))
+        + [vmem] * (2 * count + len(bases) + len(after))
         + [anywhere] * len(passed),
         out_specs=[vmem] * len(rows) + [anywhere] * len(passed),
         out_shape=[pltpu.VMEM((each, ri), F32) for each in rows]
         + [pltpu.HBM(each.shape, each.dtype) for each in passed],
-        input_output_aliases={1 + 2 * count + len(bases) + at: len(rows) + at for at in range(len(passed))},
+        input_output_aliases={1 + 2 * count + len(bases) + len(after) + at: len(rows) + at for at in range(len(passed))},
         compiler_params=pltpu.CompilerParams(vmem_limit_bytes=8 << 20),
         cost_estimate=pl.CostEstimate(flops=20_000_000_000, bytes_accessed=1, transcendentals=0),
         name="contract_rows",
-    )(me, *lefts, *rights, *[array for _, _, array in bases], *passed)
+    )(me, *lefts, *rights, *[array for _, _, array in bases], *after, *passed)
 
 
 def exchange(value, k, devices):
@@ -321,27 +326,27 @@
     three_center = pltpu.with_memory_space_constraint(three_center, pltpu.HBM)
     occ_green = pltpu.with_memory_space_constraint(occ_green, pltpu.HBM)
     virt_green = pltpu.with_memory_space_constraint(virt_green, pltpu.HBM)
-    sides = dict(zip((6, 7), products((6, 7), me, by_slot, virt_green, three_center, 2, near=True)))
+    sides = dict(zip((6, 7), products((6, 7), by_slot, virt_green, three_center, 2, near=True)))
     arrived = {k: exchange(sides[k], k, devices) for k in (6, 7)}
     middle = (2, 3, 4, 5)
     slab = 2 * three_center.shape[-1] // devices
     by_owner = devices == 16 and slab == 16
     if by_owner:
-        cuts = (((4, 8), (0, 4)), ((4, 8), (1, 4), (0, 1)), ((4, 8), (0, 4)), ((4, 8), (1, 4), (0, 1)))
+        cuts = (((3, 8), (0, 3)), ((3, 8), (1, 3), (0, 1))) * 2
         pieces = turned_products(
             middle, me, by_slot, virt_green, three_center, 4, slab, cuts, sides[6]
         )
         latest = pieces[5][0]
     else:
-        sides.update(zip(middle, products(middle, me, by_slot, virt_green, three_center, 4, sides[6])))
+        sides.update(zip(middle, products(middle, by_slot, virt_green, three_center, 4, sides[6])))
         for k in middle:
             arrived[k] = exchange(sides[k], k, devices)
         latest = sides[5]
-    sides.update(zip((0, 1), products((0, 1), me, by_slot, virt_green, three_center, 2, latest)))
+    sides.update(zip((0, 1), products((0, 1), by_slot, virt_green, three_center, 2, latest)))
     project = projections(me, by_slot, occ_green, three_center, sides[0])
     arrived[0] = sides[0]
     arrived[1] = exchange(sides[1], 1, devices)
-    first, second = (2, 4), (3, 5)
+    first, second = (4, 2), (5, 3)
     passed = [pieces[k][0] for k in second] if by_owner else []
     total, *passed = contract([arrived[k] for k in (6, 0)], [project[k] for k in (6, 0)], None, passed)
     if not by_owner:
@@ -359,28 +364,27 @@
     second_far = send(passed, second)
     (total,) = contract([arrived[k] for k in (7, 1)], [project[k] for k in (7, 1)], total)
     outer, *passed = contract_rows(
-        me, first_far, first_rights, (4 * slab,), slab, [("all", 4, total)], [pieces[k][1] for k in first]
+        me, first_far, first_rights, (5 * slab,), slab, [("all", 3, total)], [pieces[k][1] for k in first]
     )
     first_own = send(passed, first)
-    outer, *passed = contract_rows(
-        me, second_far, second_rights, (4 * slab,), slab, [("own", 0, outer)], [pieces[k][1] for k in second]
+    across, outer, *passed = contract_rows(
+        me, second_far, second_rights, (slab, 4 * slab), slab, [("own", 0, outer)], [pieces[k][1] for k in second]
     )
     inner = exchange(outer, 8, devices)
     second_mid = send(passed, second)
     chip, rest, *passed = contract_rows(
-        me,
-        first_own,
-        first_rights,
-        (slab, 3 * slab),
-        slab,
-        [("all", 0, total), ("own", 0, inner)],
-        [pieces[k][2] for k in second],
+        me, first_own, first_rights, (slab, 2 * slab), slab, [("all", 0, total)], [pieces[k][2] for k in second]
     )
     second_near = send(passed, second)
-    square = contract_rows(me, second_mid, second_rights, (slab,) * 3, slab, [("own", 0, rest)])
-    square = [exchange(value, 2 * (at + 1), devices) for at, value in enumerate(square)]
-    (chip,) = contract_rows(me, second_near, second_rights, (slab,), slab, [("own", 0, chip)])
-    chip = chip + square[0] + square[1] + square[2]
+    across = exchange(across + inner[3 * slab :], 6, devices)
+    square = contract_rows(
+        me, second_mid, second_rights, (slab, slab), slab, [("own", 0, rest), ("own", slab, inner)]
+    )
+    square = [exchange(square[at], 2 * (at + 1), devices) for at in (1, 0)]
+    (chip,) = contract_rows(
+        me, second_near, second_rights, (slab,), slab, [("own", 0, chip), ("own", 0, inner)]
+    )
+    chip = chip + across + square[0] + square[1]
     half = slab // 2
     upper = (lax.axis_index("tensor") & 1) != 0
     keep = jnp.where(upper, chip[half:], chip[:half])

time: 107 us -> 106 us (level)
  waiting for transfers between devices: 38.7 us -> 33.3 us
  local copies, waits for them, and re-layouts: 8.39 us -> 11.2 us
  Pallas kernels: 37.5 us -> 38.7 us
    ppermute x18, waiting for transfers between devices: 38.7 us -> 33.3 us  [exchange(): return lax.ppermute(value, 'tensor', [(i, i ^ k) for i in range(devices)])]
    unnamed x22 -> x30, local copies, waits for them, and re-layouts: 8.39 us -> 11.2 us
    pallas_call x2, Pallas kernels: 1.49 us -> 3.04 us  [contract(): pl.pallas_call(functools.partial(contract_kernel, count, len(starts)), in...]
  transfers between devices with their start and end apart: 18 -> 18, of which waited for: 12 -> 9; matrix products, arithmetic and copies ran while one was open for 0% -> 0% of each run, Pallas kernels for 30% -> 32%
where the time goes in v4:
time: 106 us; the launch traced here: 105 us
  Pallas kernels  38.7 us (37%)
  waiting for transfers between devices  33.3 us (31%)
  starting transfers between devices  21.1 us (20%)
  local copies, waits for them, and re-layouts  11.2 us (11%)
    ppermute x18, waiting for transfers between devices, exchange(): return lax.ppermute(value, 'tensor', [(i, i ^ k) for i in range(devices)])  33.3 us
    ppermute x18, starting transfers between devices, exchange(): return lax.ppermute(value, 'tensor', [(i, i ^ k) for i in range(devices)])  21.1 us
    pallas_call x1, Pallas kernels, projections(): pl.pallas_call(functools.partial(project_kernel, width, rows), grid=(step...  11.4 us
    unnamed x30, local copies, waits for them, and re-layouts  11.2 us
    pallas_call x2, Pallas kernels, products(): pl.pallas_call(functools.partial(product_kernel, slots, width, chunks), i...  11 us
    pallas_call x1, Pallas kernels, turned_products(): pl.pallas_call(functools.partial(turned_product_kernel, slots, width, chu...  9.47 us
    pallas_call x5, Pallas kernels, contract_rows(): pl.pallas_call(functools.partial(rows_kernel, count, rows, slab, kinds, l...  3.72 us
    pallas_call x2, Pallas kernels, contract(): pl.pallas_call(functools.partial(contract_kernel, count, len(starts)), in...  3.04 us
  transfers between devices with their start and end apart: 18, of which 9 were waited for; matrix products, arithmetic and copies ran while one was open for 0% of the time, Pallas kernels for 32%

profile of v4, /device:TPU:0, one launch (start us, length us, event | category | flops | bytes accessed | tf_op | source)
XLA Modules:
  0.0 105.1 jit_solution(17632053074536144299)
XLA Ops:
  0.0 5.3 %products.2 = (bf16[4096,128]{1,0:T(8,128)(2,1)S(1)}, bf16[4096,128]{1,0:T(8,128)(2,1)}) custom-call(s32[8,16]{1,0:T(8,128)} %bitcast.24, bf16[1,512,512]{2,1,0:T(8,128)(2,1)} %virt_hbm.5, bf16[1,8,4096,128]{3,2,1,0:T(8,128)(2,1)} %block_ref.1), custom_call_target="tpu_custom_call" | custom-call | flops 1 | bytes 1 | tf_op jit(solution)/shard_map/products/pallas_call | solution.py:80
  5.3 4.0 %collective-permute-start.4 = (bf16[4096,128]{1,0:T(8,128)(2,1)S(1)}, bf16[4096,128]{1,0:T(8,128)(2,1)S(1)}, u32[]{:S(2)}, u32[]{:S(2)}) collective-permute-start(bf16[4096,128]{1,0:T(8,128)(2,1)S(1)} %get-tuple-element.43.refs_0_), channel_id=1, source_target_pairs={{0,6},{1,7},{2,4},{3,5},{4,2},{5,3},{6,0},{7,1},{8,14},{9,15},{10,... | collective-permute-start | bytes 3145736 | tf_op jit(solution)/shard_map/ppermute | solution.py:305
  9.4 9.5 %turned_products.1 = (bf16[80,4096]{1,0:T(8,128)(2,1)}, bf16[48,4096]{1,0:T(8,128)(2,1)}, bf16[80,4096]{1,0:T(8,128)(2,1)}, bf16[32,4096]{1,0:T(8,128)(2,1)}, bf...) custom-call(s32[1]{0:T(128)} %bitcast.me_ref, ...), custom_call_target="tpu_custom_call" | custom-call | flops 1 | bytes 1 | tf_op jit(solution)/shard_map/turned_products/pallas_call | solution.py:158
  18.9 1.1 %copy-done.2 = bf16[80,4096]{1,0:T(8,128)(2,1)S(1)} copy-done((bf16[80,4096]{1,0:T(8,128)(2,1)S(1)}, bf16[80,4096]{1,0:T(8,128)(2,1)}, u32[]{:S(2)}) %copy-start.2) | copy-done | bytes 655384
  20.0 5.7 %products.3 = (bf16[4096,128]{1,0:T(8,128)(2,1)}, bf16[4096,128]{1,0:T(8,128)(2,1)}) custom-call(s32[8,16]{1,0:T(8,128)} %bitcast.26, bf16[1,512,512]{2,1,0:T(8,128)(2,1)} %virt_hbm.5, bf16[1,8,4096,128]{3,2,1,0:T(8,128)(2,1)} %block_ref.1, bf16[80,4096]{1,0:T(8,128)(2,1)S(1)} %copy-done.2), custom_call_target="tpu_custom_call" | custom-call | flops 1 | bytes 1 | tf_op jit(solution)/shard_map/products/pallas_call | solution.py:80
  25.9 1.9 %collective-permute-start = (bf16[80,4096]{1,0:T(8,128)(2,1)}, bf16[80,4096]{1,0:T(8,128)(2,1)}, u32[]{:S(2)}, u32[]{:S(2)}) collective-permute-start(bf16[80,4096]{1,0:T(8,128)(2,1)} %get-tuple-element.44), channel_id=1, source_target_pairs={{0,4},{1,5},{2,6},{3,7},{4,0},{5,1},{6,2},{7,3},{8,12},{9,13},{10,... | collective-permute-start | bytes 1966088 | tf_op jit(solution)/shard_map/ppermute | solution.py:305
  27.8 1.5 %collective-permute-start.1 = (bf16[80,4096]{1,0:T(8,128)(2,1)}, bf16[80,4096]{1,0:T(8,128)(2,1)}, u32[]{:S(2)}, u32[]{:S(2)}) collective-permute-start(bf16[80,4096]{1,0:T(8,128)(2,1)} %get-tuple-element.45), channel_id=1, source_target_pairs={{0,2},{1,3},{2,0},{3,1},{4,6},{5,7},{6,4},{7,5},{8,10},{9,11},{10,... | collective-permute-start | bytes 1966088 | tf_op jit(solution)/shard_map/ppermute | solution.py:305
  29.3 1.2 %copy-done = bf16[4096,128]{1,0:T(8,128)(2,1)S(1)} copy-done((bf16[4096,128]{1,0:T(8,128)(2,1)S(1)}, bf16[4096,128]{1,0:T(8,128)(2,1)}, u32[]{:S(2)}) %copy-start) | copy-done | bytes 1048600
  30.5 11.4 %projections.1 = (bf16[64,64,128]{2,1,0:T(8,128)(2,1)}, bf16[64,64,128]{2,1,0:T(8,128)(2,1)}, bf16[64,64,128]{2,1,0:T(8,128)(2,1)S(1)}, bf16[64,64,128]{2,1,0:T(...) custom-call(s32[1]{0:T(128)} %bitcast.me_ref, ...), custom_call_target="tpu_custom_call" | custom-call | flops 1 | bytes 1 | tf_op jit(solution)/shard_map/projections/pallas_call | solution.py:211
  42.0 1.0 copy-done.7
  43.0 1.0 copy-done.9
  43.9 1.1 %copy-done.11 = bf16[64,64,128]{2,1,0:T(8,128)(2,1)} copy-done((bf16[64,64,128]{2,1,0:T(8,128)(2,1)}, bf16[64,64,128]{2,1,0:T(8,128)(2,1)S(1)}, u32[]{:S(2)}) %copy-start.11) | copy-done | bytes 1048600
  45.0 1.0 copy-done.13
  46.0 1.2 %copy-done.5 = bf16[64,64,128]{2,1,0:T(8,128)(2,1)S(1)} copy-done((bf16[64,64,128]{2,1,0:T(8,128)(2,1)S(1)}, bf16[64,64,128]{2,1,0:T(8,128)(2,1)}, u32[]{:S(2)}) %copy-start.5) | copy-done | bytes 1048600
  47.2 1.2 %copy-done.6 = bf16[64,64,128]{2,1,0:T(8,128)(2,1)S(1)} copy-done((bf16[64,64,128]{2,1,0:T(8,128)(2,1)S(1)}, bf16[64,64,128]{2,1,0:T(8,128)(2,1)}, u32[]{:S(2)}) %copy-start.6) | copy-done | bytes 1048600
  49.6 6.0 %collective-permute-done.2.refs_0_ = bf16[4096,128]{1,0:T(8,128)(2,1)} collective-permute-done((bf16[4096,128]{1,0:T(8,128)(2,1)}, bf16[4096,128]{1,0:T(8,128)(2,1)}, u32[]{:S(2)}, u32[]{:S(2)}) %collective-permute-start.2) | collective-permute-done | bytes 1048608 | tf_op jit(solution)/shard_map/ppermute | solution.py:305
  55.6 1.2 %copy-done.3 = bf16[64,64,128]{2,1,0:T(8,128)(2,1)S(1)} copy-done((bf16[64,64,128]{2,1,0:T(8,128)(2,1)S(1)}, bf16[64,64,128]{2,1,0:T(8,128)(2,1)}, u32[]{:S(2)}) %copy-start.3) | copy-done | bytes 1048600
  56.8 1.2 %copy-done.4 = bf16[64,64,128]{2,1,0:T(8,128)(2,1)S(1)} copy-done((bf16[64,64,128]{2,1,0:T(8,128)(2,1)S(1)}, bf16[64,64,128]{2,1,0:T(8,128)(2,1)}, u32[]{:S(2)}) %copy-start.4) | copy-done | bytes 1048600
  58.0 2.3 %contract.3.refs_4_ = f32[128,128]{1,0:T(8,128)S(1)} custom-call(bf16[4096,128]{1,0:T(8,128)(2,1)} %collective-permute-done.2.refs_0_, bf16[4096,128]{1,0:T(8,128)(2,1)} %collective-permute-done.3.refs_1_, bf16[4096,128]{1,0:T(8,128)(2,1)S(1)} %bitcast.11, bf16[4096,128]{1,0:T(8,128)(2,1)S(1)} %bitcast.10, f32[128,128]{1,0:T(8,128)S(1)} %get-tuple-element.57.refs_4_), custom_call_target="tpu_custom_call" | custom-call | flops 1 | bytes 1 | tf_op jit(solution)/shard_map/contract/pallas_call | solution.py:246
  60.3 10.2 %collective-permute-done.refs_0_ = bf16[80,4096]{1,0:T(8,128)(2,1)} collective-permute-done((bf16[80,4096]{1,0:T(8,128)(2,1)}, bf16[80,4096]{1,0:T(8,128)(2,1)}, u32[]{:S(2)}, u32[]{:S(2)}) %collective-permute-start) | collective-permute-done | bytes 655392 | tf_op jit(solution)/shard_map/ppermute | solution.py:305
  70.6 1.9 %contract_rows.5 = (f32[80,128]{1,0:T(8,128)S(1)}, bf16[48,4096]{1,0:T(8,128)(2,1)}, bf16[48,4096]{1,0:T(8,128)(2,1)}) custom-call(s32[1]{0:T(128)} %bitcast.me_ref, bf16[80,4096]{1,0:T(8,128)(2,1)} %collective-permute-done.refs_0_, bf16[80,4096]{1,0:T(8,128)(2,1)} %collective-permute-done.1.refs_1_, ...), custom_call_target="tpu_custom_call", output_to_operand_aliasing={{1}: (6, {}), {2}: (7, {})} | custom-call | flops 20000000000 | bytes 1 | tf_op jit(solution)/shard_map/contract_rows/pallas_call | solution.py:289
  72.5 1.6 %collective-permute-start.5 = (bf16[48,4096]{1,0:T(8,128)(2,1)}, bf16[48,4096]{1,0:T(8,128)(2,1)S(1)}, u32[]{:S(2)}, u32[]{:S(2)}) collective-permute-start(bf16[48,4096]{1,0:T(8,128)(2,1)} %get-tuple-element.60), channel_id=1, source_target_pairs={{0,4},{1,5},{2,6},{3,7},{4,0},{5,1},{6,2},{7,3},{8,12},{9,13},{10,... | collective-permute-start | bytes 1179656 | tf_op jit(solution)/shard_map/ppermute | solution.py:305
  74.6 8.4 %collective-permute-done.10.refs_1_ = bf16[80,4096]{1,0:T(8,128)(2,1)S(1)} collective-permute-done((bf16[80,4096]{1,0:T(8,128)(2,1)}, bf16[80,4096]{1,0:T(8,128)(2,1)S(1)}, u32[]{:S(2)}, u32[]{:S(2)}) %collective-permute-start.10) | collective-permute-done | bytes 655392 | tf_op jit(solution)/shard_map/ppermute | solution.py:305
  84.2 2.7 %collective-permute-start.11 = (f32[64,128]{1,0:T(8,128)S(1)}, f32[64,128]{1,0:T(8,128)S(1)}, u32[]{:S(2)}, u32[]{:S(2)}) collective-permute-start(f32[64,128]{1,0:T(8,128)S(1)} %get-tuple-element.74), channel_id=1, source_target_pairs={{0,8},{1,9},{2,10},{3,11},{4,12},{5,13},{6,14},{7,15},{8,0},{9,1},... | collective-permute-start | bytes 98312 | tf_op jit(solution)/shard_map/ppermute | solution.py:305
  86.8 1.8 %collective-permute-start.13 = (bf16[32,4096]{1,0:T(8,128)(2,1)}, bf16[32,4096]{1,0:T(8,128)(2,1)S(1)}, u32[]{:S(2)}, u32[]{:S(2)}) collective-permute-start(bf16[32,4096]{1,0:T(8,128)(2,1)} %get-tuple-element.76), channel_id=1, source_target_pairs={{0,5},{1,4},{2,7},{3,6},{4,1},{5,0},{6,3},{7,2},{8,13},{9,12},{10,... | collective-permute-start | bytes 786440 | tf_op jit(solution)/shard_map/ppermute | solution.py:305
  89.1 4.5 %collective-permute-done.5.refs_0_ = bf16[48,4096]{1,0:T(8,128)(2,1)S(1)} collective-permute-done((bf16[48,4096]{1,0:T(8,128)(2,1)}, bf16[48,4096]{1,0:T(8,128)(2,1)S(1)}, u32[]{:S(2)}, u32[]{:S(2)}) %collective-permute-start.5) | collective-permute-done | bytes 393248 | tf_op jit(solution)/shard_map/ppermute | solution.py:305
  94.1 1.1 %collective-permute-start.8 = (bf16[16,4096]{1,0:T(8,128)(2,1)}, bf16[16,4096]{1,0:T(8,128)(2,1)S(1)}, u32[]{:S(2)}, u32[]{:S(2)}) collective-permute-start(bf16[16,4096]{1,0:T(8,128)(2,1)} %get-tuple-element.65), channel_id=1, source_target_pairs={{0,3},{1,2},{2,1},{3,0},{4,7},{5,6},{6,5},{7,4},{8,11},{9,10},{10,... | collective-permute-start | bytes 393224 | tf_op jit(solution)/shard_map/ppermute | solution.py:305
  95.2 2.1 %collective-permute-start.12 = (f32[16,128]{1,0:T(8,128)S(1)}, f32[16,128]{1,0:T(8,128)S(1)}, u32[]{:S(2)}, u32[]{:S(2)}) collective-permute-start(f32[16,128]{1,0:T(8,128)S(1)} %slice_add_fusion), channel_id=1, source_target_pairs={{0,6},{1,7},{2,4},{3,5},{4,2},{5,3},{6,0},{7,1},{8,14},{9,15},{10,... | collective-permute-start | bytes 24584 | tf_op jit(solution)/shard_map/ppermute | solution.py:305
  97.3 1.1 %collective-permute-done.13.refs_0_ = bf16[32,4096]{1,0:T(8,128)(2,1)S(1)} collective-permute-done((bf16[32,4096]{1,0:T(8,128)(2,1)}, bf16[32,4096]{1,0:T(8,128)(2,1)S(1)}, u32[]{:S(2)}, u32[]{:S(2)}) %collective-permute-start.13) | collective-permute-done | bytes 262176 | tf_op jit(solution)/shard_map/ppermute | solution.py:305
  99.3 1.5 %collective-permute-start.16 = (f32[16,128]{1,0:T(8,128)S(1)}, f32[16,128]{1,0:T(8,128)S(1)}, u32[]{:S(2)}, u32[]{:S(2)}) collective-permute-start(f32[16,128]{1,0:T(8,128)S(1)} %get-tuple-element.80), channel_id=1, source_target_pairs={{0,2},{1,3},{2,0},{3,1},{4,6},{5,7},{6,4},{7,5},{8,10},{9,11},{10,... | collective-permute-start | bytes 24584 | tf_op jit(solution)/shard_map/ppermute | solution.py:305
  101.2 1.4 %collective-permute-done.15 = f32[16,128]{1,0:T(8,128)S(1)} collective-permute-done((f32[16,128]{1,0:T(8,128)S(1)}, f32[16,128]{1,0:T(8,128)S(1)}, u32[]{:S(2)}, u32[]{:S(2)}) %collective-permute-start.15) | collective-permute-done | bytes 8224 | tf_op jit(solution)/shard_map/ppermute | solution.py:305
  103.7 0.8 collective-permute-done.17
  (49 shorter events, 7.0 us)
Async XLA Ops:
  5.3 40.7 %collective-permute-start.4 = (bf16[4096,128]{1,0:T(8,128)(2,1)S(1)}, bf16[4096,128]{1,0:T(8,128)(2,1)S(1)}, u32[]{:S(2)}, u32[]{:S(2)}) collective-permute-start(bf16[4096,128]{1,0:T(8,128)(2,1)S(1)} %get-tuple-element.43.refs_0_), channel_id=1, source_target_pairs={{0,6},{1,7},{2,4},{3,5},{4,2},{5,3},{6,0},{7,1},{8,14},{9,15},{10,... | collective-permute-start | bytes 3145736 | tf_op jit(solution)/shard_map/ppermute | solution.py:305
  18.9 1.1 %copy-start.2 = (bf16[80,4096]{1,0:T(8,128)(2,1)S(1)}, bf16[80,4096]{1,0:T(8,128)(2,1)}, u32[]{:S(2)}) copy-start(bf16[80,4096]{1,0:T(8,128)(2,1)} %get-tuple-element.46.refs_0_.refs_4_) | copy-start | bytes 1966084
  25.6 23.7 %collective-permute-start.3 = (bf16[4096,128]{1,0:T(8,128)(2,1)}, bf16[4096,128]{1,0:T(8,128)(2,1)}, u32[]{:S(2)}, u32[]{:S(2)}) collective-permute-start(bf16[4096,128]{1,0:T(8,128)(2,1)} %get-tuple-element.51), channel_id=1, source_target_pairs={{0,1},{1,0},{2,3},{3,2},{4,5},{5,4},{6,7},{7,6},{8,9},{9,8},{10,11... | collective-permute-start | bytes 3145736 | tf_op jit(solution)/shard_map/ppermute | solution.py:305
  25.7 29.9 %collective-permute-start.2 = (bf16[4096,128]{1,0:T(8,128)(2,1)}, bf16[4096,128]{1,0:T(8,128)(2,1)}, u32[]{:S(2)}, u32[]{:S(2)}) collective-permute-start(bf16[4096,128]{1,0:T(8,128)(2,1)} %get-tuple-element.50), channel_id=1, source_target_pairs={{0,7},{1,6},{2,5},{3,4},{4,3},{5,2},{6,1},{7,0},{8,15},{9,14},{10,... | collective-permute-start | bytes 3145736 | tf_op jit(solution)/shard_map/ppermute | solution.py:305
  25.9 44.7 %collective-permute-start = (bf16[80,4096]{1,0:T(8,128)(2,1)}, bf16[80,4096]{1,0:T(8,128)(2,1)}, u32[]{:S(2)}, u32[]{:S(2)}) collective-permute-start(bf16[80,4096]{1,0:T(8,128)(2,1)} %get-tuple-element.44), channel_id=1, source_target_pairs={{0,4},{1,5},{2,6},{3,7},{4,0},{5,1},{6,2},{7,3},{8,12},{9,13},{10,... | collective-permute-start | bytes 1966088 | tf_op jit(solution)/shard_map/ppermute | solution.py:305
  27.8 42.7 %collective-permute-start.1 = (bf16[80,4096]{1,0:T(8,128)(2,1)}, bf16[80,4096]{1,0:T(8,128)(2,1)}, u32[]{:S(2)}, u32[]{:S(2)}) collective-permute-start(bf16[80,4096]{1,0:T(8,128)(2,1)} %get-tuple-element.45), channel_id=1, source_target_pairs={{0,2},{1,3},{2,0},{3,1},{4,6},{5,7},{6,4},{7,5},{8,10},{9,11},{10,... | collective-permute-start | bytes 1966088 | tf_op jit(solution)/shard_map/ppermute | solution.py:305
  29.3 1.2 %copy-start = (bf16[4096,128]{1,0:T(8,128)(2,1)S(1)}, bf16[4096,128]{1,0:T(8,128)(2,1)}, u32[]{:S(2)}) copy-start(bf16[4096,128]{1,0:T(8,128)(2,1)} %get-tuple-element.47.after_ref.refs_1_) | copy-start | bytes 3145732
  30.5 15.5 %copy-start.1 = (bf16[4096,128]{1,0:T(8,128)(2,1)S(1)}, bf16[4096,128]{1,0:T(8,128)(2,1)}, u32[]{:S(2)}) copy-start(bf16[4096,128]{1,0:T(8,128)(2,1)} %get-tuple-element.47.after_ref.refs_1_) | copy-start | bytes 3145732
  42.0 1.0 copy-start.7
  43.9 1.1 %copy-start.11 = (bf16[64,64,128]{2,1,0:T(8,128)(2,1)}, bf16[64,64,128]{2,1,0:T(8,128)(2,1)S(1)}, u32[]{:S(2)}) copy-start(bf16[64,64,128]{2,1,0:T(8,128)(2,1)S(1)} %get-tuple-element.49) | copy-start | bytes 3145732
  45.0 1.0 copy-start.13
  46.0 1.2 %copy-start.5 = (bf16[64,64,128]{2,1,0:T(8,128)(2,1)S(1)}, bf16[64,64,128]{2,1,0:T(8,128)(2,1)}, u32[]{:S(2)}) copy-start(bf16[64,64,128]{2,1,0:T(8,128)(2,1)} %get-tuple-element.55) | copy-start | bytes 3145732
  47.2 1.2 %copy-start.6 = (bf16[64,64,128]{2,1,0:T(8,128)(2,1)S(1)}, bf16[64,64,128]{2,1,0:T(8,128)(2,1)}, u32[]{:S(2)}) copy-start(bf16[64,64,128]{2,1,0:T(8,128)(2,1)} %get-tuple-element.54) | copy-start | bytes 3145732
  48.5 22.1 %copy-start.12 = (bf16[64,64,128]{2,1,0:T(8,128)(2,1)S(1)}, bf16[64,64,128]{2,1,0:T(8,128)(2,1)}, u32[]{:S(2)}) copy-start(bf16[64,64,128]{2,1,0:T(8,128)(2,1)} %copy-done.11) | copy-start | bytes 3145732
  48.5 22.1 %copy-start.14 = (bf16[64,64,128]{2,1,0:T(8,128)(2,1)S(1)}, bf16[64,64,128]{2,1,0:T(8,128)(2,1)}, u32[]{:S(2)}) copy-start(bf16[64,64,128]{2,1,0:T(8,128)(2,1)} %copy-done.13) | copy-start | bytes 3145732
  49.2 33.8 %collective-permute-start.10 = (bf16[80,4096]{1,0:T(8,128)(2,1)}, bf16[80,4096]{1,0:T(8,128)(2,1)S(1)}, u32[]{:S(2)}, u32[]{:S(2)}) collective-permute-start(bf16[80,4096]{1,0:T(8,128)(2,1)} %get-tuple-element.70), channel_id=1, source_target_pairs={{0,3},{1,2},{2,1},{3,0},{4,7},{5,6},{6,5},{7,4},{8,11},{9,10},{10,... | collective-permute-start | bytes 1966088 | tf_op jit(solution)/shard_map/ppermute | solution.py:305
  49.3 34.4 %collective-permute-start.9 = (bf16[80,4096]{1,0:T(8,128)(2,1)}, bf16[80,4096]{1,0:T(8,128)(2,1)S(1)}, u32[]{:S(2)}, u32[]{:S(2)}) collective-permute-start(bf16[80,4096]{1,0:T(8,128)(2,1)} %get-tuple-element.69), channel_id=1, source_target_pairs={{0,5},{1,4},{2,7},{3,6},{4,1},{5,0},{6,3},{7,2},{8,13},{9,12},{10,... | collective-permute-start | bytes 1966088 | tf_op jit(solution)/shard_map/ppermute | solution.py:305
  55.6 1.2 %copy-start.3 = (bf16[64,64,128]{2,1,0:T(8,128)(2,1)S(1)}, bf16[64,64,128]{2,1,0:T(8,128)(2,1)}, u32[]{:S(2)}) copy-start(bf16[64,64,128]{2,1,0:T(8,128)(2,1)} %get-tuple-element.53) | copy-start | bytes 3145732
  56.8 1.2 %copy-start.4 = (bf16[64,64,128]{2,1,0:T(8,128)(2,1)S(1)}, bf16[64,64,128]{2,1,0:T(8,128)(2,1)}, u32[]{:S(2)}) copy-start(bf16[64,64,128]{2,1,0:T(8,128)(2,1)} %get-tuple-element.52) | copy-start | bytes 3145732
  70.5 13.1 %copy-start.8 = (bf16[64,64,128]{2,1,0:T(8,128)(2,1)S(1)}, bf16[64,64,128]{2,1,0:T(8,128)(2,1)}, u32[]{:S(2)}) copy-start(bf16[64,64,128]{2,1,0:T(8,128)(2,1)} %copy-done.7) | copy-start | bytes 3145732
  70.5 13.1 %copy-start.10 = (bf16[64,64,128]{2,1,0:T(8,128)(2,1)S(1)}, bf16[64,64,128]{2,1,0:T(8,128)(2,1)}, u32[]{:S(2)}) copy-start(bf16[64,64,128]{2,1,0:T(8,128)(2,1)} %copy-done.9) | copy-start | bytes 3145732
  72.5 21.1 %collective-permute-start.5 = (bf16[48,4096]{1,0:T(8,128)(2,1)}, bf16[48,4096]{1,0:T(8,128)(2,1)S(1)}, u32[]{:S(2)}, u32[]{:S(2)}) collective-permute-start(bf16[48,4096]{1,0:T(8,128)(2,1)} %get-tuple-element.60), channel_id=1, source_target_pairs={{0,4},{1,5},{2,6},{3,7},{4,0},{5,1},{6,2},{7,3},{8,12},{9,13},{10,... | collective-permute-start | bytes 1179656 | tf_op jit(solution)/shard_map/ppermute | solution.py:305
  74.1 19.5 %collective-permute-start.6 = (bf16[48,4096]{1,0:T(8,128)(2,1)}, bf16[48,4096]{1,0:T(8,128)(2,1)S(1)}, u32[]{:S(2)}, u32[]{:S(2)}) collective-permute-start(bf16[48,4096]{1,0:T(8,128)(2,1)} %get-tuple-element.61), channel_id=1, source_target_pairs={{0,2},{1,3},{2,0},{3,1},{4,6},{5,7},{6,4},{7,5},{8,10},{9,11},{10,... | collective-permute-start | bytes 1179656 | tf_op jit(solution)/shard_map/ppermute | solution.py:305
  84.2 11.1 %collective-permute-start.11 = (f32[64,128]{1,0:T(8,128)S(1)}, f32[64,128]{1,0:T(8,128)S(1)}, u32[]{:S(2)}, u32[]{:S(2)}) collective-permute-start(f32[64,128]{1,0:T(8,128)S(1)} %get-tuple-element.74), channel_id=1, source_target_pairs={{0,8},{1,9},{2,10},{3,11},{4,12},{5,13},{6,14},{7,15},{8,0},{9,1},... | collective-permute-start | bytes 98312 | tf_op jit(solution)/shard_map/ppermute | solution.py:305
  86.8 11.6 %collective-permute-start.13 = (bf16[32,4096]{1,0:T(8,128)(2,1)}, bf16[32,4096]{1,0:T(8,128)(2,1)S(1)}, u32[]{:S(2)}, u32[]{:S(2)}) collective-permute-start(bf16[32,4096]{1,0:T(8,128)(2,1)} %get-tuple-element.76), channel_id=1, source_target_pairs={{0,5},{1,4},{2,7},{3,6},{4,1},{5,0},{6,3},{7,2},{8,13},{9,12},{10,... | collective-permute-start | bytes 786440 | tf_op jit(solution)/shard_map/ppermute | solution.py:305
  88.7 9.8 %collective-permute-start.14 = (bf16[32,4096]{1,0:T(8,128)(2,1)}, bf16[32,4096]{1,0:T(8,128)(2,1)S(1)}, u32[]{:S(2)}, u32[]{:S(2)}) collective-permute-start(bf16[32,4096]{1,0:T(8,128)(2,1)} %get-tuple-element.77), channel_id=1, source_target_pairs={{0,3},{1,2},{2,1},{3,0},{4,7},{5,6},{6,5},{7,4},{8,11},{9,10},{10,... | collective-permute-start | bytes 786440 | tf_op jit(solution)/shard_map/ppermute | solution.py:305
  94.1 6.7 %collective-permute-start.7 = (bf16[16,4096]{1,0:T(8,128)(2,1)}, bf16[16,4096]{1,0:T(8,128)(2,1)S(1)}, u32[]{:S(2)}, u32[]{:S(2)}) collective-permute-start(bf16[16,4096]{1,0:T(8,128)(2,1)} %get-tuple-element.64), channel_id=1, source_target_pairs={{0,5},{1,4},{2,7},{3,6},{4,1},{5,0},{6,3},{7,2},{8,13},{9,12},{10,... | collective-permute-start | bytes 393224 | tf_op jit(solution)/shard_map/ppermute | solution.py:305
  94.1 6.6 %collective-permute-start.8 = (bf16[16,4096]{1,0:T(8,128)(2,1)}, bf16[16,4096]{1,0:T(8,128)(2,1)S(1)}, u32[]{:S(2)}, u32[]{:S(2)}) collective-permute-start(bf16[16,4096]{1,0:T(8,128)(2,1)} %get-tuple-element.65), channel_id=1, source_target_pairs={{0,3},{1,2},{2,1},{3,0},{4,7},{5,6},{6,5},{7,4},{8,11},{9,10},{10,... | collective-permute-start | bytes 393224 | tf_op jit(solution)/shard_map/ppermute | solution.py:305
  95.2 5.9 %collective-permute-start.12 = (f32[16,128]{1,0:T(8,128)S(1)}, f32[16,128]{1,0:T(8,128)S(1)}, u32[]{:S(2)}, u32[]{:S(2)}) collective-permute-start(f32[16,128]{1,0:T(8,128)S(1)} %slice_add_fusion), channel_id=1, source_target_pairs={{0,6},{1,7},{2,4},{3,5},{4,2},{5,3},{6,0},{7,1},{8,14},{9,15},{10,... | collective-permute-start | bytes 24584 | tf_op jit(solution)/shard_map/ppermute | solution.py:305
  98.9 3.7 %collective-permute-start.15 = (f32[16,128]{1,0:T(8,128)S(1)}, f32[16,128]{1,0:T(8,128)S(1)}, u32[]{:S(2)}, u32[]{:S(2)}) collective-permute-start(f32[16,128]{1,0:T(8,128)S(1)} %get-tuple-element.79), channel_id=1, source_target_pairs={{0,4},{1,5},{2,6},{3,7},{4,0},{5,1},{6,2},{7,3},{8,12},{9,13},{10,... | collective-permute-start | bytes 24584 | tf_op jit(solution)/shard_map/ppermute | solution.py:305
  99.3 3.7 %collective-permute-start.16 = (f32[16,128]{1,0:T(8,128)S(1)}, f32[16,128]{1,0:T(8,128)S(1)}, u32[]{:S(2)}, u32[]{:S(2)}) collective-permute-start(f32[16,128]{1,0:T(8,128)S(1)} %get-tuple-element.80), channel_id=1, source_target_pairs={{0,2},{1,3},{2,0},{3,1},{4,6},{5,7},{6,4},{7,5},{8,10},{9,11},{10,... | collective-permute-start | bytes 24584 | tf_op jit(solution)/shard_map/ppermute | solution.py:305
  102.9 1.6 %collective-permute-start.17 = (f32[8,128]{1,0:T(8,128)S(1)}, f32[8,128]{1,0:T(8,128)S(1)}, u32[]{:S(2)}, u32[]{:S(2)}) collective-permute-start(f32[8,128]{1,0:T(8,128)S(1)} %slice_select_fusion), channel_id=1, source_target_pairs={{0,1},{1,0},{2,3},{3,2},{4,5},{5,4},{6,7},{7,6},{8,9},{9,8},{10,11... | collective-permute-start | bytes 12296 | tf_op jit(solution)/shard_map/ppermute | solution.py:305
  (1 other events, 1.0 us)

commit v5 on v4

--- a/solution.py
+++ b/solution.py
@@ -21,75 +21,99 @@
 
 
 def masked_turned(slots, width, me, neighbors_ref, virt, virt_t):
-    parts = [
-        jnp.where(neighbors_ref[m, me] >= 0, virt[m * width : (m + 1) * width, :].astype(F32), 0.0)
-        for m in range(SLOTS)
+    for pair in range(len(slots) // 2):
+        parts = [
+            jnp.where(neighbors_ref[m, me] >= 0, virt[pair, m * width : (m + 1) * width, :].astype(F32), 0.0)
+            for m in range(SLOTS)
+        ]
+        turned = jnp.concatenate(parts, axis=0).T
+        for at in range(2):
+            live = neighbors_ref[slots[2 * pair + at], me] >= 0
+            virt_t[(2 * pair + at) * width : (2 * pair + at + 1) * width, :] = jnp.where(
+                live, turned[at * width : (at + 1) * width, :], 0.0
+            ).astype(BF)
+
+
+def virt_copies(slots, width, virt_hbm, virt, sems):
+    return [
+        pltpu.make_async_copy(
+            virt_hbm.at[0, :, pl.ds(k * width, 2 * width)], virt.at[pair], sems.at[pair]
+        )
+        for pair, k in enumerate(slots[::2])
     ]
-    turned = jnp.concatenate(parts, axis=0).T
-    for at, k in enumerate(slots):
-        live = neighbors_ref[k, me] >= 0
-        virt_t[at * width : (at + 1) * width, :] = jnp.where(
-            live, turned[at * width : (at + 1) * width, :], 0.0
-        ).astype(BF)
-
-
-def product_kernel(slots, width, chunks, neighbors_hbm, virt_hbm, block_hbm, *refs):
-    outs = refs[-7 - len(slots) : -7]
-    neighbors_ref, virt, virt_t, block, neighbors_sem, virt_sem, sems = refs[-7:]
+
+
+def product_kernel(slots, wanted, width, chunks, neighbors_hbm, virt_hbm, block_hbm, *refs):
+    outs = refs[-7 - len(wanted) : -7]
+    neighbors_ref, virt, virt_t, block, neighbors_sem, virt_sems, sems = refs[-7:]
     me = lax.axis_index("tensor")
-    low, count = slots[0], len(slots)
     ri = block.shape[-1]
-    size = block.shape[1] // chunks
+    size = block_hbm.shape[2] // chunks
+    start = min(first for _, first, _ in wanted)
+    stop = max(last for _, _, last in wanted)
 
     def block_copy(c):
-        rows = pl.ds(pl.multiple_of(c * size, size), size)
-        return pltpu.make_async_copy(block_hbm.at[0, :, rows, :], block.at[:, rows, :], sems.at[c])
-
-    virt_copy = pltpu.make_async_copy(
-        virt_hbm.at[0, :, pl.ds(low * width, count * width)], virt, virt_sem
-    )
+        rows = pl.ds(pl.multiple_of((c - start) * size, size), size)
+        source = pl.ds(pl.multiple_of(c * size, size), size)
+        return pltpu.make_async_copy(block_hbm.at[0, :, source, :], block.at[:, rows, :], sems.at[c - start])
+
     neighbors_copy = pltpu.make_async_copy(neighbors_hbm, neighbors_ref, neighbors_sem)
     neighbors_copy.start()
-    virt_copy.start()
-    for c in range(chunks):
+    copies = virt_copies(slots, width, virt_hbm, virt, virt_sems)
+    for copy in copies:
+        copy.start()
+    for c in range(start, stop):
         block_copy(c).start()
     neighbors_copy.wait()
-    virt_copy.wait()
+    for copy in copies:
+        copy.wait()
     masked_turned(slots, width, me, neighbors_ref, virt, virt_t)
 
-    @pl.loop(0, chunks)
-    def _(c):
-        block_copy(c).wait()
-        for pair in range(size // width // 2):
-            base = c * size + 2 * pair * width
-            right = gathered_rows(block, base, 2, width)
-            both = jnp.dot(virt_t[...], right, preferred_element_type=F32).astype(BF)
-            for at in range(count):
-                for half in range(2):
-                    rows = pl.ds(pl.multiple_of(base + half * width, width), width)
-                    outs[at][rows, :] = both[at * width : (at + 1) * width, half * ri : (half + 1) * ri]
-
-
-def products(slots, neighbors, virt, blocks, chunks, after=None, near=False):
+    def run(begin, end, busy):
+        low = min(wanted[at][0] for at in busy) * width
+        high = (max(wanted[at][0] for at in busy) + 1) * width
+
+        @pl.loop(begin, end)
+        def _(c):
+            block_copy(c).wait()
+            for pair in range(size // width // 2):
+                inner = 2 * pair * width
+                right = gathered_rows(block, (c - start) * size + inner, 2, width)
+                both = jnp.dot(virt_t[low:high, :], right, preferred_element_type=F32).astype(BF)
+                for at in busy:
+                    row = wanted[at][0] * width - low
+                    for half in range(2):
+                        base = (c - wanted[at][1]) * size + inner + half * width
+                        rows = pl.ds(pl.multiple_of(base, width), width)
+                        outs[at][rows, :] = both[row : row + width, half * ri : (half + 1) * ri]
+
+    edges = sorted({edge for _, *each in wanted for edge in each})
+    for begin, end in zip(edges, edges[1:]):
+        run(begin, end, [at for at, (_, first, last) in enumerate(wanted) if first <= begin and end <= last])
+
+
+def products(slots, neighbors, virt, blocks, chunks, after=(), near=False, wanted=None):
     pairs, ri = blocks.shape[2:]
     wide = virt.shape[1]
     width = wide // SLOTS
     count = len(slots)
+    wanted = wanted or tuple((at, 0, chunks) for at in range(count))
+    used = max(last for _, _, last in wanted) - min(first for _, first, _ in wanted)
+    shapes = [(pairs // chunks * (last - first), ri) for _, first, last in wanted]
     hbm = pl.BlockSpec(memory_space=pltpu.HBM)
-    after = [] if after is None else [after]
     return pl.pallas_call(
-        functools.partial(product_kernel, slots, width, chunks),
+        functools.partial(product_kernel, slots, wanted, width, chunks),
         in_specs=[hbm, hbm, hbm] + [pl.BlockSpec(memory_space=pl.ANY)] * len(after),
-        out_specs=[pl.BlockSpec(memory_space=pltpu.VMEM)] * count,
-        out_shape=[pltpu.VMEM((pairs, ri), BF) if near else pltpu.HBM((pairs, ri), BF)] * count,
+        out_specs=[pl.BlockSpec(memory_space=pltpu.VMEM)] * len(wanted),
+        out_shape=[(pltpu.VMEM if near else pltpu.HBM)(shape, BF) for shape in shapes],
         scratch_shapes=[
             pltpu.SMEM(neighbors.shape, jnp.int32),
-            pltpu.VMEM((wide, count * width), BF),
+            pltpu.VMEM((count // 2, wide, 2 * width), BF),
             pltpu.VMEM((count * width, wide), BF),
-            pltpu.VMEM((SLOTS, pairs, ri), BF),
+            pltpu.VMEM((SLOTS, pairs // chunks * used, ri), BF),
             pltpu.SemaphoreType.DMA,
-            pltpu.SemaphoreType.DMA,
-            pltpu.SemaphoreType.DMA((chunks,)),
+            pltpu.SemaphoreType.DMA((count // 2,)),
+            pltpu.SemaphoreType.DMA((used,)),
         ],
         compiler_params=pltpu.CompilerParams(vmem_limit_bytes=24 << 20),
         cost_estimate=pl.CostEstimate(flops=1, bytes_accessed=1, transcendentals=0),
@@ -97,12 +121,12 @@
     )(neighbors, virt, blocks, *after)
 
 
-def turned_product_kernel(slots, width, chunks, slab, cuts, me_ref, neighbors_ref, virt_hbm, block_hbm, *refs):
+def turned_product_kernel(slots, width, chunks, slab, cuts, neighbors_hbm, virt_hbm, block_hbm, *refs):
     count = len(slots)
-    outs = refs[-7 - sum(len(each) for each in cuts) : -7]
-    virt, virt_t, block, sides, virt_sem, sems, out_sems = refs[-7:]
-    me = me_ref[0]
-    low = slots[0]
+    pieces = sum(len(each) for each in cuts)
+    outs = refs[-9 - pieces : -9]
+    neighbors_ref, virt, virt_t, block, sides, neighbors_sem, virt_sems, sems, out_sems = refs[-9:]
+    me = lax.axis_index("tensor")
     ri = block.shape[-1]
     size = block.shape[1] // chunks
 
@@ -110,13 +134,16 @@
         rows = pl.ds(pl.multiple_of(c * size, size), size)
         return pltpu.make_async_copy(block_hbm.at[0, :, rows, :], block.at[:, rows, :], sems.at[c])
 
-    virt_copy = pltpu.make_async_copy(
-        virt_hbm.at[0, :, pl.ds(low * width, count * width)], virt, virt_sem
-    )
-    virt_copy.start()
+    neighbors_copy = pltpu.make_async_copy(neighbors_hbm, neighbors_ref, neighbors_sem)
+    neighbors_copy.start()
+    virt_moves = virt_copies(slots, width, virt_hbm, virt, virt_sems)
+    for copy in virt_moves:
+        copy.start()
     for c in range(chunks):
         block_copy(c).start()
-    virt_copy.wait()
+    neighbors_copy.wait()
+    for copy in virt_moves:
+        copy.wait()
     masked_turned(slots, width, me, neighbors_ref, virt, virt_t)
 
     @pl.loop(0, chunks)
@@ -148,31 +175,32 @@
         copy.wait()
 
 
-def turned_products(slots, me, neighbors, virt, blocks, chunks, slab, cuts, after):
+def turned_products(slots, neighbors, virt, blocks, chunks, slab, cuts, after):
     pairs, ri = blocks.shape[2:]
     wide = virt.shape[1]
     width = wide // SLOTS
     count = len(slots)
-    smem = pl.BlockSpec(memory_space=pltpu.SMEM)
     hbm = pl.BlockSpec(memory_space=pltpu.HBM)
     out = pl.pallas_call(
         functools.partial(turned_product_kernel, slots, width, chunks, slab, cuts),
-        in_specs=[smem, smem, hbm, hbm, pl.BlockSpec(memory_space=pl.ANY)],
+        in_specs=[hbm, hbm, hbm, pl.BlockSpec(memory_space=pl.ANY)],
         out_specs=[hbm] * sum(len(each) for each in cuts),
         out_shape=[pltpu.HBM(((last - first) * slab, pairs), BF) for each in cuts for first, last in each],
         scratch_shapes=[
-            pltpu.VMEM((wide, count * width), BF),
+            pltpu.SMEM(neighbors.shape, jnp.int32),
+            pltpu.VMEM((count // 2, wide, 2 * width), BF),
             pltpu.VMEM((count * width, wide), BF),
             pltpu.VMEM((SLOTS, pairs, ri), BF),
             pltpu.VMEM((count, ri, pairs), BF),
             pltpu.SemaphoreType.DMA,
+            pltpu.SemaphoreType.DMA((count // 2,)),
             pltpu.SemaphoreType.DMA((chunks,)),
             pltpu.SemaphoreType.DMA((count * ri // slab,)),
         ],
         compiler_params=pltpu.CompilerParams(vmem_limit_bytes=24 << 20),
         cost_estimate=pl.CostEstimate(flops=1, bytes_accessed=1, transcendentals=0),
         name="turned_products",
-    )(me, neighbors, virt, blocks, after)
+    )(neighbors, virt, blocks, after)
     out = list(out)
     return {k: [out.pop(0) for _ in cuts[at]] for at, k in enumerate(slots)}
 
@@ -228,23 +256,24 @@
     return [each.reshape(pairs, ri) for each in out]
 
 
-def contract_kernel(count, has_start, *refs):
+def contract_kernel(count, begins, has_start, *refs):
     out = refs[2 * count + has_start + (len(refs) - 2 * count - has_start - 1) // 2]
     total = refs[2 * count][...] if has_start else None
-    for left, right in zip(refs[:count], refs[count : 2 * count]):
-        term = lax.dot_general(left[...], right[...], (((0,), (0,)), ((), ())), preferred_element_type=F32)
+    for at, (left, right) in enumerate(zip(refs[:count], refs[count : 2 * count])):
+        rows = pl.ds(begins[at], left.shape[0])
+        term = lax.dot_general(left[...], right[rows, :], (((0,), (0,)), ((), ())), preferred_element_type=F32)
         total = term if total is None else total + term
     out[...] = total
 
 
-def contract(lefts, rights, start=None, passed=()):
-    pairs, ri = rights[0].shape
+def contract(lefts, rights, begins, start=None, passed=()):
+    ri = rights[0].shape[1]
     count = len(lefts)
     starts = [] if start is None else [start]
     vmem = pl.BlockSpec(memory_space=pltpu.VMEM)
     anywhere = pl.BlockSpec(memory_space=pl.ANY)
     return pl.pallas_call(
-        functools.partial(contract_kernel, count, len(starts)),
+        functools.partial(contract_kernel, count, begins, len(starts)),
         in_specs=[vmem] * (2 * count + len(starts)) + [anywhere] * len(passed),
         out_specs=[vmem] + [anywhere] * len(passed),
         out_shape=[pltpu.VMEM((ri, ri), F32)] + [pltpu.HBM(each.shape, each.dtype) for each in passed],
@@ -326,32 +355,47 @@
     three_center = pltpu.with_memory_space_constraint(three_center, pltpu.HBM)
     occ_green = pltpu.with_memory_space_constraint(occ_green, pltpu.HBM)
     virt_green = pltpu.with_memory_space_constraint(virt_green, pltpu.HBM)
-    sides = dict(zip((6, 7), products((6, 7), by_slot, virt_green, three_center, 2, near=True)))
-    arrived = {k: exchange(sides[k], k, devices) for k in (6, 7)}
-    middle = (2, 3, 4, 5)
+    middle, last = (2, 3, 4, 5), (6, 7)
+    pairs = three_center.shape[2]
     slab = 2 * three_center.shape[-1] // devices
     by_owner = devices == 16 and slab == 16
+    cuts = (((3, 8), (0, 3)), ((3, 8), (1, 3), (0, 1))) * 2 if by_owner else (((0, devices // 2),),) * 4
+    begun = products(last, by_slot, virt_green, three_center, 2, near=True, wanted=((0, 0, 1), (1, 0, 1)))
+    begun_in = [exchange(value, k, devices) for k, value in zip(last, begun)]
+    own, *both = products(
+        (0, 1) + last,
+        by_slot,
+        virt_green,
+        three_center,
+        4,
+        begun[:1],
+        wanted=((0, 0, 4), (1, 0, 2), (1, 2, 4), (2, 2, 4), (3, 2, 4)),
+    )
+    other, ended = both[:2], both[2:]
+    ended_in = [exchange(value, k, devices) for k, value in zip(last, ended)]
+    other_in = [exchange(value, 1, devices) for value in other]
     if by_owner:
-        cuts = (((3, 8), (0, 3)), ((3, 8), (1, 3), (0, 1))) * 2
-        pieces = turned_products(
-            middle, me, by_slot, virt_green, three_center, 4, slab, cuts, sides[6]
-        )
+        pieces = turned_products(middle, by_slot, virt_green, three_center, 4, slab, cuts, own)
         latest = pieces[5][0]
     else:
-        sides.update(zip(middle, products(middle, by_slot, virt_green, three_center, 4, sides[6])))
-        for k in middle:
-            arrived[k] = exchange(sides[k], k, devices)
-        latest = sides[5]
-    sides.update(zip((0, 1), products((0, 1), by_slot, virt_green, three_center, 2, latest)))
-    project = projections(me, by_slot, occ_green, three_center, sides[0])
-    arrived[0] = sides[0]
-    arrived[1] = exchange(sides[1], 1, devices)
+        sides = products(middle, by_slot, virt_green, three_center, 4, [own])
+        arrived = {k: exchange(value, k, devices) for k, value in zip(middle, sides)}
+        latest = sides[0]
+    project = projections(me, by_slot, occ_green, three_center, latest)
     first, second = (4, 2), (5, 3)
-    passed = [pieces[k][0] for k in second] if by_owner else []
-    total, *passed = contract([arrived[k] for k in (6, 0)], [project[k] for k in (6, 0)], None, passed)
+    total, *passed = contract(
+        [begun_in[0], own],
+        [project[6], project[0]],
+        (0, 0),
+        None,
+        [pieces[k][0] for k in second] if by_owner else [],
+    )
+    (total,) = contract([begun_in[1]], [project[7]], (0,), total)
+    (total,) = contract(other_in, [project[1]] * 2, (0, pairs // 2), total)
+    (total,) = contract(ended_in, [project[k] for k in last], (pairs // 2,) * 2, total)
     if not by_owner:
-        for group in ((7, 1), first, second):
-            (total,) = contract([arrived[k] for k in group], [project[k] for k in group], total)
+        for group in (first, second):
+            (total,) = contract([arrived[k] for k in group], [project[k] for k in group], (0, 0), total)
         bits = [1 << b for b in reversed(range(devices.bit_length() - 1))]
         return reduce_rows(total, devices, bits)
 
@@ -362,7 +406,6 @@
     second_rights = [project[k] for k in second]
     first_far = send([pieces[k][0] for k in first], first)
     second_far = send(passed, second)
-    (total,) = contract([arrived[k] for k in (7, 1)], [project[k] for k in (7, 1)], total)
     outer, *passed = contract_rows(
         me, first_far, first_rights, (5 * slab,), slab, [("all", 3, total)], [pieces[k][1] for k in first]
     )

time: 106 us -> 103 us (0.972)
  waiting for transfers between devices: 33.3 us -> 25.4 us
  starting transfers between devices: 21.1 us -> 26.2 us
  local copies, waits for them, and re-layouts: 11.2 us -> 13.3 us
  Pallas kernels: 38.7 us -> 37.1 us
    ppermute x18 -> x21, waiting for transfers between devices: 33.3 us -> 25.4 us  [exchange(): return lax.ppermute(value, 'tensor', [(i, i ^ k) for i in range(devices)])]
    ppermute x18 -> x21, starting transfers between devices: 21.1 us -> 26.2 us  [exchange(): return lax.ppermute(value, 'tensor', [(i, i ^ k) for i in range(devices)])]
    unnamed x30 -> x38, local copies, waits for them, and re-layouts: 11.2 us -> 13.3 us
    pallas_call x4 -> x6, Pallas kernels: 14 us -> 13 us  [the longest x2 10.1 us: products(): pl.pallas_call(functools.partial(product_kernel, slots, wanted, width, ch...]
  transfers between devices with their start and end apart: 18 -> 21, of which waited for: 9 -> 8; matrix products, arithmetic and copies ran while one was open for 0% -> 0% of each run, Pallas kernels for 32% -> 33%
where the time goes in v5:
time: 103 us
  Pallas kernels  37.1 us (36%)
  starting transfers between devices  26.2 us (25%)
  waiting for transfers between devices  25.4 us (25%)
  local copies, waits for them, and re-layouts  13.3 us (13%)
    ppermute x21, starting transfers between devices, exchange(): return lax.ppermute(value, 'tensor', [(i, i ^ k) for i in range(devices)])  26.2 us
    ppermute x21, waiting for transfers between devices, exchange(): return lax.ppermute(value, 'tensor', [(i, i ^ k) for i in range(devices)])  25.4 us
    unnamed x38, local copies, waits for them, and re-layouts  13.3 us
    pallas_call x1, Pallas kernels, projections(): pl.pallas_call(functools.partial(project_kernel, width, rows), grid=(step...  11.4 us
    pallas_call x2, Pallas kernels, products(): pl.pallas_call(functools.partial(product_kernel, slots, wanted, width, ch...  10.1 us
    pallas_call x1, Pallas kernels, turned_products(): pl.pallas_call(functools.partial(turned_product_kernel, slots, width, chu...  8.93 us
    pallas_call x5, Pallas kernels, contract_rows(): pl.pallas_call(functools.partial(rows_kernel, count, rows, slab, kinds, l...  3.74 us
    pallas_call x4, Pallas kernels, contract(): pl.pallas_call(functools.partial(contract_kernel, count, begins, len(star...  2.94 us
  transfers between devices with their start and end apart: 21, of which 8 were waited for; matrix products, arithmetic and copies ran while one was open for 0% of the time, Pallas kernels for 33%

profile of v5, /device:TPU:0, one launch (start us, length us, event | category | flops | bytes accessed | tf_op | source)
XLA Modules:
  0.0 102.8 jit_solution(16281494275729654705)
XLA Ops:
  0.0 3.0 %products.2 = (bf16[2048,128]{1,0:T(8,128)(2,1)S(1)}, bf16[2048,128]{1,0:T(8,128)(2,1)S(1)}) custom-call(s32[8,16]{1,0:T(8,128)} %bitcast.27, bf16[1,512,512]{2,1,0:T(8,128)(2,1)} %virt_hbm.5, bf16[1,8,4096,128]{3,2,1,0:T(8,128)(2,1)} %block_ref.1), custom_call_target="tpu_custom_call" | custom-call | flops 1 | bytes 1 | tf_op jit(solution)/shard_map/products/pallas_call | solution.py:104
  3.0 4.0 %collective-permute-start.7 = (bf16[2048,128]{1,0:T(8,128)(2,1)S(1)}, bf16[2048,128]{1,0:T(8,128)(2,1)S(1)}, u32[]{:S(2)}, u32[]{:S(2)}) collective-permute-start(bf16[2048,128]{1,0:T(8,128)(2,1)S(1)} %get-tuple-element.46.refs_0_), channel_id=1, source_target_pairs={{0,6},{1,7},{2,4},{3,5},{4,2},{5,3},{6,0},{7,1},{8,14},{9,15},{10,... | collective-permute-start | bytes 1572872 | tf_op jit(solution)/shard_map/ppermute | solution.py:334
  7.1 7.1 %products.3 = (bf16[4096,128]{1,0:T(8,128)(2,1)}, bf16[2048,128]{1,0:T(8,128)(2,1)}, bf16[2048,128]{1,0:T(8,128)(2,1)}, bf16[2048,128]{1,0:T(8,128)(2,1)}, bf16[2048,128]{1,0:T(8,128)(2,1)}) custom-call(s32[8,16]{1,0:T(8,128)} %bitcast.28, bf16[1,512,512]{2,1,0:T(8,128)(2,1)} %virt_hbm.5, bf16[1,8,4096,128]{3,2,1,0:T(8,128)(2,1)} %block_ref.1, ...), custom_call_target="tpu_custom_call" | custom-call | flops 1 | bytes 1 | tf_op jit(solution)/shard_map/products/pallas_call | solution.py:104
  14.4 1.2 %copy-done = bf16[4096,128]{1,0:T(8,128)(2,1)S(1)} copy-done((bf16[4096,128]{1,0:T(8,128)(2,1)S(1)}, bf16[4096,128]{1,0:T(8,128)(2,1)}, u32[]{:S(2)}) %copy-start) | copy-done | bytes 1048600
  15.6 8.9 %turned_products.1 = (bf16[80,4096]{1,0:T(8,128)(2,1)}, bf16[48,4096]{1,0:T(8,128)(2,1)}, bf16[80,4096]{1,0:T(8,128)(2,1)}, bf16[32,4096]{1,0:T(8,128)(2,1)}, bf...) custom-call(s32[8,16]{1,0:T(8,128)} %bitcast.29, ...), custom_call_target="tpu_custom_call" | custom-call | flops 1 | bytes 1 | tf_op jit(solution)/shard_map/turned_products/pallas_call | solution.py:184
  24.6 2.0 %collective-permute-start = (bf16[80,4096]{1,0:T(8,128)(2,1)}, bf16[80,4096]{1,0:T(8,128)(2,1)}, u32[]{:S(2)}, u32[]{:S(2)}) collective-permute-start(bf16[80,4096]{1,0:T(8,128)(2,1)} %get-tuple-element.48), channel_id=1, source_target_pairs={{0,4},{1,5},{2,6},{3,7},{4,0},{5,1},{6,2},{7,3},{8,12},{9,13},{10,... | collective-permute-start | bytes 1966088 | tf_op jit(solution)/shard_map/ppermute | solution.py:334
  26.5 1.5 %collective-permute-start.1 = (bf16[80,4096]{1,0:T(8,128)(2,1)}, bf16[80,4096]{1,0:T(8,128)(2,1)}, u32[]{:S(2)}, u32[]{:S(2)}) collective-permute-start(bf16[80,4096]{1,0:T(8,128)(2,1)} %get-tuple-element.49), channel_id=1, source_target_pairs={{0,2},{1,3},{2,0},{3,1},{4,6},{5,7},{6,4},{7,5},{8,10},{9,11},{10,... | collective-permute-start | bytes 1966088 | tf_op jit(solution)/shard_map/ppermute | solution.py:334
  28.0 2.6 %collective-permute-done.6.refs_0_ = bf16[2048,128]{1,0:T(8,128)(2,1)S(1)} collective-permute-done((bf16[2048,128]{1,0:T(8,128)(2,1)S(1)}, bf16[2048,128]{1,0:T(8,128)(2,1)S(1)}, u32[]{:S(2)}, u32[]{:S(2)}) %collective-permute-start.6) | collective-permute-done | bytes 524320 | tf_op jit(solution)/shard_map/ppermute | solution.py:334
  31.4 1.2 %collective-permute-start.2 = (bf16[2048,128]{1,0:T(8,128)(2,1)}, bf16[2048,128]{1,0:T(8,128)(2,1)S(1)}, u32[]{:S(2)}, u32[]{:S(2)}) collective-permute-start(bf16[2048,128]{1,0:T(8,128)(2,1)} %get-tuple-element.53), channel_id=1, source_target_pairs={{0,6},{1,7},{2,4},{3,5},{4,2},{5,3},{6,0},{7,1},{8,14},{9,15},{10,... | collective-permute-start | bytes 1572872 | tf_op jit(solution)/shard_map/ppermute | solution.py:334
  32.6 1.7 %collective-permute-start.3 = (bf16[2048,128]{1,0:T(8,128)(2,1)}, bf16[2048,128]{1,0:T(8,128)(2,1)S(1)}, u32[]{:S(2)}, u32[]{:S(2)}) collective-permute-start(bf16[2048,128]{1,0:T(8,128)(2,1)} %get-tuple-element.54), channel_id=1, source_target_pairs={{0,7},{1,6},{2,5},{3,4},{4,3},{5,2},{6,1},{7,0},{8,15},{9,14},{10,... | collective-permute-start | bytes 1572872 | tf_op jit(solution)/shard_map/ppermute | solution.py:334
  34.3 1.1 %copy-done.7 = bf16[80,4096]{1,0:T(8,128)(2,1)S(1)} copy-done((bf16[80,4096]{1,0:T(8,128)(2,1)S(1)}, bf16[80,4096]{1,0:T(8,128)(2,1)}, u32[]{:S(2)}) %copy-start.7) | copy-done | bytes 655384
  35.4 11.4 %projections.1 = (bf16[64,64,128]{2,1,0:T(8,128)(2,1)}, bf16[64,64,128]{2,1,0:T(8,128)(2,1)}, bf16[64,64,128]{2,1,0:T(8,128)(2,1)S(1)}, bf16[64,64,128]{2,1,0:T(...) custom-call(s32[1]{0:T(128)} %bitcast.me_ref, ...), custom_call_target="tpu_custom_call" | custom-call | flops 1 | bytes 1 | tf_op jit(solution)/shard_map/projections/pallas_call | solution.py:239
  47.8 1.0 copy-done.13
  50.7 1.2 %copy-done.2 = bf16[64,64,128]{2,1,0:T(8,128)(2,1)S(1)} copy-done((bf16[64,64,128]{2,1,0:T(8,128)(2,1)S(1)}, bf16[64,64,128]{2,1,0:T(8,128)(2,1)}, u32[]{:S(2)}) %copy-start.2) | copy-done | bytes 1048600
  51.9 1.2 %copy-done.8 = bf16[64,64,128]{2,1,0:T(8,128)(2,1)S(1)} copy-done((bf16[64,64,128]{2,1,0:T(8,128)(2,1)S(1)}, bf16[64,64,128]{2,1,0:T(8,128)(2,1)}, u32[]{:S(2)}) %copy-start.8) | copy-done | bytes 1048600
  53.8 1.5 %copy-done.5 = bf16[64,64,128]{2,1,0:T(8,128)(2,1)S(1)} copy-done((bf16[64,64,128]{2,1,0:T(8,128)(2,1)S(1)}, bf16[64,64,128]{2,1,0:T(8,128)(2,1)}, u32[]{:S(2)}) %copy-start.5) | copy-done | bytes 1048600
  55.3 1.0 %copy-done.10 = bf16[2048,128]{1,0:T(8,128)(2,1)S(1)} copy-done((bf16[2048,128]{1,0:T(8,128)(2,1)S(1)}, bf16[2048,128]{1,0:T(8,128)(2,1)}, u32[]{:S(2)}) %copy-start.10) | copy-done | bytes 524312
  57.0 1.2 %copy-done.4 = bf16[64,64,128]{2,1,0:T(8,128)(2,1)S(1)} copy-done((bf16[64,64,128]{2,1,0:T(8,128)(2,1)S(1)}, bf16[64,64,128]{2,1,0:T(8,128)(2,1)}, u32[]{:S(2)}) %copy-start.4) | copy-done | bytes 1048600
  58.3 1.5 %contract.6.refs_4_ = f32[128,128]{1,0:T(8,128)S(1)} custom-call(bf16[2048,128]{1,0:T(8,128)(2,1)S(1)} %collective-permute-done.4.refs_0_, bf16[2048,128]{1,0:T(8,128)(2,1)} %collective-permute-done.5.refs_1_, bf16[4096,128]{1,0:T(8,128)(2,1)S(1)} %bitcast.12, bf16[4096,128]{1,0:T(8,128)(2,1)S(1)} %bitcast.13, f32[128,128]{1,0:T(8,128)S(1)} %contract.5.refs_4_), custom_call_target="tpu_custom_call" | custom-call | flops 1 | bytes 1 | tf_op jit(solution)/shard_map/contract/pallas_call | solution.py:275
  59.8 2.7 %collective-permute-start.13 = (bf16[80,4096]{1,0:T(8,128)(2,1)}, bf16[80,4096]{1,0:T(8,128)(2,1)S(1)}, u32[]{:S(2)}, u32[]{:S(2)}) collective-permute-start(bf16[80,4096]{1,0:T(8,128)(2,1)} %get-tuple-element.76), channel_id=1, source_target_pairs={{0,3},{1,2},{2,1},{3,0},{4,7},{5,6},{6,5},{7,4},{8,11},{9,10},{10,... | collective-permute-start | bytes 1966088 | tf_op jit(solution)/shard_map/ppermute | solution.py:334
  62.5 4.8 %collective-permute-done.3.refs_1_ = bf16[2048,128]{1,0:T(8,128)(2,1)S(1)} collective-permute-done((bf16[2048,128]{1,0:T(8,128)(2,1)}, bf16[2048,128]{1,0:T(8,128)(2,1)S(1)}, u32[]{:S(2)}, u32[]{:S(2)}) %collective-permute-start.3) | collective-permute-done | bytes 524320 | tf_op jit(solution)/shard_map/ppermute | solution.py:334
  67.8 1.9 %contract_rows.5 = (f32[80,128]{1,0:T(8,128)S(1)}, bf16[48,4096]{1,0:T(8,128)(2,1)}, bf16[48,4096]{1,0:T(8,128)(2,1)}) custom-call(s32[1]{0:T(128)} %bitcast.me_ref, bf16[80,4096]{1,0:T(8,128)(2,1)} %collective-permute-done.refs_0_, bf16[80,4096]{1,0:T(8,128)(2,1)} %collective-permute-done.1.refs_1_, ...), custom_call_target="tpu_custom_call", output_to_operand_aliasing={{1}: (6, {}), {2}: (7, {})} | custom-call | flops 20000000000 | bytes 1 | tf_op jit(solution)/shard_map/contract_rows/pallas_call | solution.py:318
  70.3 1.1 %collective-permute-start.9 = (bf16[48,4096]{1,0:T(8,128)(2,1)}, bf16[48,4096]{1,0:T(8,128)(2,1)S(1)}, u32[]{:S(2)}, u32[]{:S(2)}) collective-permute-start(bf16[48,4096]{1,0:T(8,128)(2,1)} %get-tuple-element.67), channel_id=1, source_target_pairs={{0,2},{1,3},{2,0},{3,1},{4,6},{5,7},{6,4},{7,5},{8,10},{9,11},{10,... | collective-permute-start | bytes 1179656 | tf_op jit(solution)/shard_map/ppermute | solution.py:334
  71.4 9.9 %collective-permute-done.12.refs_0_ = bf16[80,4096]{1,0:T(8,128)(2,1)S(1)} collective-permute-done((bf16[80,4096]{1,0:T(8,128)(2,1)}, bf16[80,4096]{1,0:T(8,128)(2,1)S(1)}, u32[]{:S(2)}, u32[]{:S(2)}) %collective-permute-start.12) | collective-permute-done | bytes 655392 | tf_op jit(solution)/shard_map/ppermute | solution.py:334
  81.9 2.6 %collective-permute-start.14 = (f32[64,128]{1,0:T(8,128)S(1)}, f32[64,128]{1,0:T(8,128)S(1)}, u32[]{:S(2)}, u32[]{:S(2)}) collective-permute-start(f32[64,128]{1,0:T(8,128)S(1)} %get-tuple-element.80), channel_id=1, source_target_pairs={{0,8},{1,9},{2,10},{3,11},{4,12},{5,13},{6,14},{7,15},{8,0},{9,1},... | collective-permute-start | bytes 98312 | tf_op jit(solution)/shard_map/ppermute | solution.py:334
  84.5 1.8 %collective-permute-start.16 = (bf16[32,4096]{1,0:T(8,128)(2,1)}, bf16[32,4096]{1,0:T(8,128)(2,1)S(1)}, u32[]{:S(2)}, u32[]{:S(2)}) collective-permute-start(bf16[32,4096]{1,0:T(8,128)(2,1)} %get-tuple-element.82), channel_id=1, source_target_pairs={{0,5},{1,4},{2,7},{3,6},{4,1},{5,0},{6,3},{7,2},{8,13},{9,12},{10,... | collective-permute-start | bytes 786440 | tf_op jit(solution)/shard_map/ppermute | solution.py:334
  86.8 4.4 %collective-permute-done.8.refs_0_ = bf16[48,4096]{1,0:T(8,128)(2,1)S(1)} collective-permute-done((bf16[48,4096]{1,0:T(8,128)(2,1)}, bf16[48,4096]{1,0:T(8,128)(2,1)S(1)}, u32[]{:S(2)}, u32[]{:S(2)}) %collective-permute-start.8) | collective-permute-done | bytes 393248 | tf_op jit(solution)/shard_map/ppermute | solution.py:334
  91.8 1.1 %collective-permute-start.11 = (bf16[16,4096]{1,0:T(8,128)(2,1)}, bf16[16,4096]{1,0:T(8,128)(2,1)S(1)}, u32[]{:S(2)}, u32[]{:S(2)}) collective-permute-start(bf16[16,4096]{1,0:T(8,128)(2,1)} %get-tuple-element.71), channel_id=1, source_target_pairs={{0,3},{1,2},{2,1},{3,0},{4,7},{5,6},{6,5},{7,4},{8,11},{9,10},{10,... | collective-permute-start | bytes 393224 | tf_op jit(solution)/shard_map/ppermute | solution.py:334
  92.9 2.1 %collective-permute-start.15 = (f32[16,128]{1,0:T(8,128)S(1)}, f32[16,128]{1,0:T(8,128)S(1)}, u32[]{:S(2)}, u32[]{:S(2)}) collective-permute-start(f32[16,128]{1,0:T(8,128)S(1)} %slice_add_fusion), channel_id=1, source_target_pairs={{0,6},{1,7},{2,4},{3,5},{4,2},{5,3},{6,0},{7,1},{8,14},{9,15},{10,... | collective-permute-start | bytes 24584 | tf_op jit(solution)/shard_map/ppermute | solution.py:334
  95.0 1.1 %collective-permute-done.16.refs_0_ = bf16[32,4096]{1,0:T(8,128)(2,1)S(1)} collective-permute-done((bf16[32,4096]{1,0:T(8,128)(2,1)}, bf16[32,4096]{1,0:T(8,128)(2,1)S(1)}, u32[]{:S(2)}, u32[]{:S(2)}) %collective-permute-start.16) | collective-permute-done | bytes 262176 | tf_op jit(solution)/shard_map/ppermute | solution.py:334
  97.0 1.5 %collective-permute-start.19 = (f32[16,128]{1,0:T(8,128)S(1)}, f32[16,128]{1,0:T(8,128)S(1)}, u32[]{:S(2)}, u32[]{:S(2)}) collective-permute-start(f32[16,128]{1,0:T(8,128)S(1)} %get-tuple-element.86), channel_id=1, source_target_pairs={{0,2},{1,3},{2,0},{3,1},{4,6},{5,7},{6,4},{7,5},{8,10},{9,11},{10,... | collective-permute-start | bytes 24584 | tf_op jit(solution)/shard_map/ppermute | solution.py:334
  98.9 1.4 %collective-permute-done.18 = f32[16,128]{1,0:T(8,128)S(1)} collective-permute-done((f32[16,128]{1,0:T(8,128)S(1)}, f32[16,128]{1,0:T(8,128)S(1)}, u32[]{:S(2)}, u32[]{:S(2)}) %collective-permute-start.18) | collective-permute-done | bytes 8224 | tf_op jit(solution)/shard_map/ppermute | solution.py:334
  (65 shorter events, 11.7 us)
Async XLA Ops:
  3.0 25.0 %collective-permute-start.7 = (bf16[2048,128]{1,0:T(8,128)(2,1)S(1)}, bf16[2048,128]{1,0:T(8,128)(2,1)S(1)}, u32[]{:S(2)}, u32[]{:S(2)}) collective-permute-start(bf16[2048,128]{1,0:T(8,128)(2,1)S(1)} %get-tuple-element.46.refs_0_), channel_id=1, source_target_pairs={{0,6},{1,7},{2,4},{3,5},{4,2},{5,3},{6,0},{7,1},{8,14},{9,15},{10,... | collective-permute-start | bytes 1572872 | tf_op jit(solution)/shard_map/ppermute | solution.py:334
  7.1 23.6 %collective-permute-start.6 = (bf16[2048,128]{1,0:T(8,128)(2,1)S(1)}, bf16[2048,128]{1,0:T(8,128)(2,1)S(1)}, u32[]{:S(2)}, u32[]{:S(2)}) collective-permute-start(bf16[2048,128]{1,0:T(8,128)(2,1)S(1)} %get-tuple-element.60), channel_id=1, source_target_pairs={{0,7},{1,6},{2,5},{3,4},{4,3},{5,2},{6,1},{7,0},{8,15},{9,14},{10,... | collective-permute-start | bytes 1572872 | tf_op jit(solution)/shard_map/ppermute | solution.py:334
  14.1 18.5 %collective-permute-start.4 = (bf16[2048,128]{1,0:T(8,128)(2,1)}, bf16[2048,128]{1,0:T(8,128)(2,1)S(1)}, u32[]{:S(2)}, u32[]{:S(2)}) collective-permute-start(bf16[2048,128]{1,0:T(8,128)(2,1)} %get-tuple-element.57), channel_id=1, source_target_pairs={{0,1},{1,0},{2,3},{3,2},{4,5},{5,4},{6,7},{7,6},{8,9},{9,8},{10,11... | collective-permute-start | bytes 1572872 | tf_op jit(solution)/shard_map/ppermute | solution.py:334
  14.4 1.2 %copy-start = (bf16[4096,128]{1,0:T(8,128)(2,1)S(1)}, bf16[4096,128]{1,0:T(8,128)(2,1)}, u32[]{:S(2)}) copy-start(bf16[4096,128]{1,0:T(8,128)(2,1)} %get-tuple-element.47.refs_0_.refs_1_) | copy-start | bytes 3145732
  15.6 35.1 %copy-start.1 = (bf16[4096,128]{1,0:T(8,128)(2,1)S(1)}, bf16[4096,128]{1,0:T(8,128)(2,1)}, u32[]{:S(2)}) copy-start(bf16[4096,128]{1,0:T(8,128)(2,1)} %get-tuple-element.47.refs_0_.refs_1_) | copy-start | bytes 3145732
  24.6 43.2 %collective-permute-start = (bf16[80,4096]{1,0:T(8,128)(2,1)}, bf16[80,4096]{1,0:T(8,128)(2,1)}, u32[]{:S(2)}, u32[]{:S(2)}) collective-permute-start(bf16[80,4096]{1,0:T(8,128)(2,1)} %get-tuple-element.48), channel_id=1, source_target_pairs={{0,4},{1,5},{2,6},{3,7},{4,0},{5,1},{6,2},{7,3},{8,12},{9,13},{10,... | collective-permute-start | bytes 1966088 | tf_op jit(solution)/shard_map/ppermute | solution.py:334
  26.5 41.3 %collective-permute-start.1 = (bf16[80,4096]{1,0:T(8,128)(2,1)}, bf16[80,4096]{1,0:T(8,128)(2,1)}, u32[]{:S(2)}, u32[]{:S(2)}) collective-permute-start(bf16[80,4096]{1,0:T(8,128)(2,1)} %get-tuple-element.49), channel_id=1, source_target_pairs={{0,2},{1,3},{2,0},{3,1},{4,6},{5,7},{6,4},{7,5},{8,10},{9,11},{10,... | collective-permute-start | bytes 1966088 | tf_op jit(solution)/shard_map/ppermute | solution.py:334
  28.0 28.7 %collective-permute-start.5 = (bf16[2048,128]{1,0:T(8,128)(2,1)}, bf16[2048,128]{1,0:T(8,128)(2,1)}, u32[]{:S(2)}, u32[]{:S(2)}) collective-permute-start(bf16[2048,128]{1,0:T(8,128)(2,1)} %get-tuple-element.58), channel_id=1, source_target_pairs={{0,1},{1,0},{2,3},{3,2},{4,5},{5,4},{6,7},{7,6},{8,9},{9,8},{10,11... | collective-permute-start | bytes 1572872 | tf_op jit(solution)/shard_map/ppermute | solution.py:334
  31.4 28.3 %collective-permute-start.2 = (bf16[2048,128]{1,0:T(8,128)(2,1)}, bf16[2048,128]{1,0:T(8,128)(2,1)S(1)}, u32[]{:S(2)}, u32[]{:S(2)}) collective-permute-start(bf16[2048,128]{1,0:T(8,128)(2,1)} %get-tuple-element.53), channel_id=1, source_target_pairs={{0,6},{1,7},{2,4},{3,5},{4,2},{5,3},{6,0},{7,1},{8,14},{9,15},{10,... | collective-permute-start | bytes 1572872 | tf_op jit(solution)/shard_map/ppermute | solution.py:334
  32.6 34.7 %collective-permute-start.3 = (bf16[2048,128]{1,0:T(8,128)(2,1)}, bf16[2048,128]{1,0:T(8,128)(2,1)S(1)}, u32[]{:S(2)}, u32[]{:S(2)}) collective-permute-start(bf16[2048,128]{1,0:T(8,128)(2,1)} %get-tuple-element.54), channel_id=1, source_target_pairs={{0,7},{1,6},{2,5},{3,4},{4,3},{5,2},{6,1},{7,0},{8,15},{9,14},{10,... | collective-permute-start | bytes 1572872 | tf_op jit(solution)/shard_map/ppermute | solution.py:334
  50.7 1.2 %copy-start.2 = (bf16[64,64,128]{2,1,0:T(8,128)(2,1)S(1)}, bf16[64,64,128]{2,1,0:T(8,128)(2,1)}, u32[]{:S(2)}) copy-start(bf16[64,64,128]{2,1,0:T(8,128)(2,1)} %get-tuple-element.55) | copy-start | bytes 3145732
  51.9 1.2 %copy-start.8 = (bf16[64,64,128]{2,1,0:T(8,128)(2,1)S(1)}, bf16[64,64,128]{2,1,0:T(8,128)(2,1)}, u32[]{:S(2)}) copy-start(bf16[64,64,128]{2,1,0:T(8,128)(2,1)} %get-tuple-element.61) | copy-start | bytes 3145732
  53.2 14.1 %copy-start.3 = (bf16[64,64,128]{2,1,0:T(8,128)(2,1)S(1)}, bf16[64,64,128]{2,1,0:T(8,128)(2,1)}, u32[]{:S(2)}) copy-start(bf16[64,64,128]{2,1,0:T(8,128)(2,1)} %get-tuple-element.55) | copy-start | bytes 3145732
  53.2 14.1 %copy-start.6 = (bf16[64,64,128]{2,1,0:T(8,128)(2,1)S(1)}, bf16[64,64,128]{2,1,0:T(8,128)(2,1)}, u32[]{:S(2)}) copy-start(bf16[64,64,128]{2,1,0:T(8,128)(2,1)} %get-tuple-element.56) | copy-start | bytes 3145732
  53.2 14.6 %copy-start.16 = (bf16[64,64,128]{2,1,0:T(8,128)(2,1)S(1)}, bf16[64,64,128]{2,1,0:T(8,128)(2,1)}, u32[]{:S(2)}) copy-start(bf16[64,64,128]{2,1,0:T(8,128)(2,1)} %copy-done.15) | copy-start | bytes 3145732
  53.2 14.7 %copy-start.18 = (bf16[64,64,128]{2,1,0:T(8,128)(2,1)S(1)}, bf16[64,64,128]{2,1,0:T(8,128)(2,1)}, u32[]{:S(2)}) copy-start(bf16[64,64,128]{2,1,0:T(8,128)(2,1)} %copy-done.17) | copy-start | bytes 3145732
  53.8 1.5 %copy-start.5 = (bf16[64,64,128]{2,1,0:T(8,128)(2,1)S(1)}, bf16[64,64,128]{2,1,0:T(8,128)(2,1)}, u32[]{:S(2)}) copy-start(bf16[64,64,128]{2,1,0:T(8,128)(2,1)} %get-tuple-element.56) | copy-start | bytes 3145732
  56.7 24.6 %collective-permute-start.12 = (bf16[80,4096]{1,0:T(8,128)(2,1)}, bf16[80,4096]{1,0:T(8,128)(2,1)S(1)}, u32[]{:S(2)}, u32[]{:S(2)}) collective-permute-start(bf16[80,4096]{1,0:T(8,128)(2,1)} %get-tuple-element.75), channel_id=1, source_target_pairs={{0,5},{1,4},{2,7},{3,6},{4,1},{5,0},{6,3},{7,2},{8,13},{9,12},{10,... | collective-permute-start | bytes 1966088 | tf_op jit(solution)/shard_map/ppermute | solution.py:334
  59.8 21.6 %collective-permute-start.13 = (bf16[80,4096]{1,0:T(8,128)(2,1)}, bf16[80,4096]{1,0:T(8,128)(2,1)S(1)}, u32[]{:S(2)}, u32[]{:S(2)}) collective-permute-start(bf16[80,4096]{1,0:T(8,128)(2,1)} %get-tuple-element.76), channel_id=1, source_target_pairs={{0,3},{1,2},{2,1},{3,0},{4,7},{5,6},{6,5},{7,4},{8,11},{9,10},{10,... | collective-permute-start | bytes 1966088 | tf_op jit(solution)/shard_map/ppermute | solution.py:334
  67.8 13.5 %copy-start.12 = (bf16[64,64,128]{2,1,0:T(8,128)(2,1)S(1)}, bf16[64,64,128]{2,1,0:T(8,128)(2,1)}, u32[]{:S(2)}) copy-start(bf16[64,64,128]{2,1,0:T(8,128)(2,1)} %copy-done.11) | copy-start | bytes 3145732
  67.8 13.5 %copy-start.14 = (bf16[64,64,128]{2,1,0:T(8,128)(2,1)S(1)}, bf16[64,64,128]{2,1,0:T(8,128)(2,1)}, u32[]{:S(2)}) copy-start(bf16[64,64,128]{2,1,0:T(8,128)(2,1)} %copy-done.13) | copy-start | bytes 3145732
  69.8 21.5 %collective-permute-start.8 = (bf16[48,4096]{1,0:T(8,128)(2,1)}, bf16[48,4096]{1,0:T(8,128)(2,1)S(1)}, u32[]{:S(2)}, u32[]{:S(2)}) collective-permute-start(bf16[48,4096]{1,0:T(8,128)(2,1)} %get-tuple-element.66), channel_id=1, source_target_pairs={{0,4},{1,5},{2,6},{3,7},{4,0},{5,1},{6,2},{7,3},{8,12},{9,13},{10,... | collective-permute-start | bytes 1179656 | tf_op jit(solution)/shard_map/ppermute | solution.py:334
  70.3 21.0 %collective-permute-start.9 = (bf16[48,4096]{1,0:T(8,128)(2,1)}, bf16[48,4096]{1,0:T(8,128)(2,1)S(1)}, u32[]{:S(2)}, u32[]{:S(2)}) collective-permute-start(bf16[48,4096]{1,0:T(8,128)(2,1)} %get-tuple-element.67), channel_id=1, source_target_pairs={{0,2},{1,3},{2,0},{3,1},{4,6},{5,7},{6,4},{7,5},{8,10},{9,11},{10,... | collective-permute-start | bytes 1179656 | tf_op jit(solution)/shard_map/ppermute | solution.py:334
  81.9 11.0 %collective-permute-start.14 = (f32[64,128]{1,0:T(8,128)S(1)}, f32[64,128]{1,0:T(8,128)S(1)}, u32[]{:S(2)}, u32[]{:S(2)}) collective-permute-start(f32[64,128]{1,0:T(8,128)S(1)} %get-tuple-element.80), channel_id=1, source_target_pairs={{0,8},{1,9},{2,10},{3,11},{4,12},{5,13},{6,14},{7,15},{8,0},{9,1},... | collective-permute-start | bytes 98312 | tf_op jit(solution)/shard_map/ppermute | solution.py:334
  84.5 11.6 %collective-permute-start.16 = (bf16[32,4096]{1,0:T(8,128)(2,1)}, bf16[32,4096]{1,0:T(8,128)(2,1)S(1)}, u32[]{:S(2)}, u32[]{:S(2)}) collective-permute-start(bf16[32,4096]{1,0:T(8,128)(2,1)} %get-tuple-element.82), channel_id=1, source_target_pairs={{0,5},{1,4},{2,7},{3,6},{4,1},{5,0},{6,3},{7,2},{8,13},{9,12},{10,... | collective-permute-start | bytes 786440 | tf_op jit(solution)/shard_map/ppermute | solution.py:334
  86.4 9.7 %collective-permute-start.17 = (bf16[32,4096]{1,0:T(8,128)(2,1)}, bf16[32,4096]{1,0:T(8,128)(2,1)S(1)}, u32[]{:S(2)}, u32[]{:S(2)}) collective-permute-start(bf16[32,4096]{1,0:T(8,128)(2,1)} %get-tuple-element.83), channel_id=1, source_target_pairs={{0,3},{1,2},{2,1},{3,0},{4,7},{5,6},{6,5},{7,4},{8,11},{9,10},{10,... | collective-permute-start | bytes 786440 | tf_op jit(solution)/shard_map/ppermute | solution.py:334
  91.7 6.7 %collective-permute-start.10 = (bf16[16,4096]{1,0:T(8,128)(2,1)}, bf16[16,4096]{1,0:T(8,128)(2,1)S(1)}, u32[]{:S(2)}, u32[]{:S(2)}) collective-permute-start(bf16[16,4096]{1,0:T(8,128)(2,1)} %get-tuple-element.70), channel_id=1, source_target_pairs={{0,5},{1,4},{2,7},{3,6},{4,1},{5,0},{6,3},{7,2},{8,13},{9,12},{10,... | collective-permute-start | bytes 393224 | tf_op jit(solution)/shard_map/ppermute | solution.py:334
  91.8 6.7 %collective-permute-start.11 = (bf16[16,4096]{1,0:T(8,128)(2,1)}, bf16[16,4096]{1,0:T(8,128)(2,1)S(1)}, u32[]{:S(2)}, u32[]{:S(2)}) collective-permute-start(bf16[16,4096]{1,0:T(8,128)(2,1)} %get-tuple-element.71), channel_id=1, source_target_pairs={{0,3},{1,2},{2,1},{3,0},{4,7},{5,6},{6,5},{7,4},{8,11},{9,10},{10,... | collective-permute-start | bytes 393224 | tf_op jit(solution)/shard_map/ppermute | solution.py:334
  92.9 6.0 %collective-permute-start.15 = (f32[16,128]{1,0:T(8,128)S(1)}, f32[16,128]{1,0:T(8,128)S(1)}, u32[]{:S(2)}, u32[]{:S(2)}) collective-permute-start(f32[16,128]{1,0:T(8,128)S(1)} %slice_add_fusion), channel_id=1, source_target_pairs={{0,6},{1,7},{2,4},{3,5},{4,2},{5,3},{6,0},{7,1},{8,14},{9,15},{10,... | collective-permute-start | bytes 24584 | tf_op jit(solution)/shard_map/ppermute | solution.py:334
  96.5 3.7 %collective-permute-start.18 = (f32[16,128]{1,0:T(8,128)S(1)}, f32[16,128]{1,0:T(8,128)S(1)}, u32[]{:S(2)}, u32[]{:S(2)}) collective-permute-start(f32[16,128]{1,0:T(8,128)S(1)} %get-tuple-element.85), channel_id=1, source_target_pairs={{0,4},{1,5},{2,6},{3,7},{4,0},{5,1},{6,2},{7,3},{8,12},{9,13},{10,... | collective-permute-start | bytes 24584 | tf_op jit(solution)/shard_map/ppermute | solution.py:334
  97.0 3.7 %collective-permute-start.19 = (f32[16,128]{1,0:T(8,128)S(1)}, f32[16,128]{1,0:T(8,128)S(1)}, u32[]{:S(2)}, u32[]{:S(2)}) collective-permute-start(f32[16,128]{1,0:T(8,128)S(1)} %get-tuple-element.86), channel_id=1, source_target_pairs={{0,2},{1,3},{2,0},{3,1},{4,6},{5,7},{6,4},{7,5},{8,10},{9,11},{10,... | collective-permute-start | bytes 24584 | tf_op jit(solution)/shard_map/ppermute | solution.py:334
  100.6 1.6 %collective-permute-start.20 = (f32[8,128]{1,0:T(8,128)S(1)}, f32[8,128]{1,0:T(8,128)S(1)}, u32[]{:S(2)}, u32[]{:S(2)}) collective-permute-start(f32[8,128]{1,0:T(8,128)S(1)} %slice_select_fusion), channel_id=1, source_target_pairs={{0,1},{1,0},{2,3},{3,2},{4,5},{5,4},{6,7},{7,6},{8,9},{9,8},{10,11... | collective-permute-start | bytes 12296 | tf_op jit(solution)/shard_map/ppermute | solution.py:334
  (8 other events, 8.1 us)

commit v6 on v5

--- a/solution.py
+++ b/solution.py
@@ -360,7 +360,7 @@
     slab = 2 * three_center.shape[-1] // devices
     by_owner = devices == 16 and slab == 16
     cuts = (((3, 8), (0, 3)), ((3, 8), (1, 3), (0, 1))) * 2 if by_owner else (((0, devices // 2),),) * 4
-    begun = products(last, by_slot, virt_green, three_center, 2, near=True, wanted=((0, 0, 1), (1, 0, 1)))
+    begun = products(last, by_slot, virt_green, three_center, 8, near=True, wanted=((0, 0, 2), (1, 0, 2)))
     begun_in = [exchange(value, k, devices) for k, value in zip(last, begun)]
     own, *both = products(
         (0, 1) + last,
@@ -369,9 +369,9 @@
         three_center,
         4,
         begun[:1],
-        wanted=((0, 0, 4), (1, 0, 2), (1, 2, 4), (2, 2, 4), (3, 2, 4)),
-    )
-    other, ended = both[:2], both[2:]
+        wanted=((0, 0, 4), (1, 0, 1), (1, 1, 2), (1, 2, 3), (1, 3, 4), (2, 1, 4), (3, 1, 4)),
+    )
+    other, ended = both[:4], both[4:]
     ended_in = [exchange(value, k, devices) for k, value in zip(last, ended)]
     other_in = [exchange(value, 1, devices) for value in other]
     if by_owner:
@@ -391,8 +391,8 @@
         [pieces[k][0] for k in second] if by_owner else [],
     )
     (total,) = contract([begun_in[1]], [project[7]], (0,), total)
-    (total,) = contract(other_in, [project[1]] * 2, (0, pairs // 2), total)
-    (total,) = contract(ended_in, [project[k] for k in last], (pairs // 2,) * 2, total)
+    (total,) = contract(other_in, [project[1]] * 4, [at * pairs // 4 for at in range(4)], total)
+    (total,) = contract(ended_in, [project[k] for k in last], (pairs // 4,) * 2, total)
     if not by_owner:
         for group in (first, second):
             (total,) = contract([arrived[k] for k in group], [project[k] for k in group], (0, 0), total)

time: 103 us -> 102 us (level)
  waiting for transfers between devices: 25.4 us -> 29.3 us
  local copies, waits for them, and re-layouts: 13.3 us -> 9.55 us
  Pallas kernels: 37.1 us -> 35.9 us
    ppermute x21 -> x23, waiting for transfers between devices: 25.4 us -> 29.3 us  [exchange(): return lax.ppermute(value, 'tensor', [(i, i ^ k) for i in range(devices)])]
    unnamed x38 -> x44, local copies, waits for them, and re-layouts: 13.3 us -> 9.55 us
    ppermute x21 -> x23, starting transfers between devices: 26.2 us -> 26.3 us  [exchange(): return lax.ppermute(value, 'tensor', [(i, i ^ k) for i in range(devices)])]
  transfers between devices with their start and end apart: 21 -> 23, of which waited for: 8 -> 10; matrix products, arithmetic and copies ran while one was open for 0% -> 0% of each run, Pallas kernels for 33% -> 33%
where the time goes in v6:
time: 102 us
  Pallas kernels  35.9 us (35%)
  waiting for transfers between devices  29.3 us (29%)
  starting transfers between devices  26.3 us (26%)
  local copies, waits for them, and re-layouts  9.55 us (9%)
    ppermute x23, waiting for transfers between devices, exchange(): return lax.ppermute(value, 'tensor', [(i, i ^ k) for i in range(devices)])  29.3 us
    ppermute x23, starting transfers between devices, exchange(): return lax.ppermute(value, 'tensor', [(i, i ^ k) for i in range(devices)])  26.3 us
    pallas_call x1, Pallas kernels, projections(): pl.pallas_call(functools.partial(project_kernel, width, rows), grid=(step...  11.5 us
    unnamed x44, local copies, waits for them, and re-layouts  9.55 us
    pallas_call x2, Pallas kernels, products(): pl.pallas_call(functools.partial(product_kernel, slots, wanted, width, ch...  9.18 us
    pallas_call x1, Pallas kernels, turned_products(): pl.pallas_call(functools.partial(turned_product_kernel, slots, width, chu...  8.88 us
    pallas_call x5, Pallas kernels, contract_rows(): pl.pallas_call(functools.partial(rows_kernel, count, rows, slab, kinds, l...  3.58 us
    pallas_call x4, Pallas kernels, contract(): pl.pallas_call(functools.partial(contract_kernel, count, begins, len(star...  2.84 us
  transfers between devices with their start and end apart: 23, of which 10 were waited for; matrix products, arithmetic and copies ran while one was open for 0% of the time, Pallas kernels for 33%

profile of v6, /device:TPU:0, one launch (start us, length us, event | category | flops | bytes accessed | tf_op | source)
XLA Modules:
  0.0 101.9 jit_solution(16050406784369160149)
XLA Ops:
  0.0 2.0 %products.2 = (bf16[1024,128]{1,0:T(8,128)(2,1)S(1)}, bf16[1024,128]{1,0:T(8,128)(2,1)S(1)}) custom-call(s32[8,16]{1,0:T(8,128)} %bitcast.29, bf16[1,512,512]{2,1,0:T(8,128)(2,1)} %virt_hbm.5, bf16[1,8,4096,128]{3,2,1,0:T(8,128)(2,1)} %block_ref.1), custom_call_target="tpu_custom_call" | custom-call | flops 1 | bytes 1 | tf_op jit(solution)/shard_map/products/pallas_call | solution.py:104
  2.0 4.0 %collective-permute-start.9 = (bf16[1024,128]{1,0:T(8,128)(2,1)S(1)}, bf16[1024,128]{1,0:T(8,128)(2,1)S(1)}, u32[]{:S(2)}, u32[]{:S(2)}) collective-permute-start(bf16[1024,128]{1,0:T(8,128)(2,1)S(1)} %get-tuple-element.48.refs_0_), channel_id=1, source_target_pairs={{0,6},{1,7},{2,4},{3,5},{4,2},{5,3},{6,0},{7,1},{8,14},{9,15},{10,... | collective-permute-start | bytes 786440 | tf_op jit(solution)/shard_map/ppermute | solution.py:334
  6.1 7.2 %products.3 = (bf16[4096,128]{1,0:T(8,128)(2,1)}, bf16[1024,128]{1,0:T(8,128)(2,1)}, bf16[1024,128]{1,0:T(8,128)(2,1)}, bf16[1024,128]{1,0:T(8,128)(2,1)}, bf16[...) custom-call(s32[8,16]{1,0:T(8,128)} %bitcast.30, bf16[1,512,512]{2,1,0:T(8,128)(2,1)} %virt_hbm.5, ...), custom_call_target="tpu_custom_call" | custom-call | flops 1 | bytes 1 | tf_op jit(solution)/shard_map/products/pallas_call | solution.py:104
  13.8 2.6 %collective-permute-start.2 = (bf16[3072,128]{1,0:T(8,128)(2,1)}, bf16[3072,128]{1,0:T(8,128)(2,1)S(1)}, u32[]{:S(2)}, u32[]{:S(2)}) collective-permute-start(bf16[3072,128]{1,0:T(8,128)(2,1)} %get-tuple-element.55), channel_id=1, source_target_pairs={{0,6},{1,7},{2,4},{3,5},{4,2},{5,3},{6,0},{7,1},{8,14},{9,15},{10,... | collective-permute-start | bytes 2359304 | tf_op jit(solution)/shard_map/ppermute | solution.py:334
  16.5 1.2 %copy-done.1 = bf16[4096,128]{1,0:T(8,128)(2,1)S(1)} copy-done((bf16[4096,128]{1,0:T(8,128)(2,1)S(1)}, bf16[4096,128]{1,0:T(8,128)(2,1)}, u32[]{:S(2)}) %copy-start.1) | copy-done | bytes 1048600
  17.7 8.9 %turned_products.1 = (bf16[80,4096]{1,0:T(8,128)(2,1)}, bf16[48,4096]{1,0:T(8,128)(2,1)}, bf16[80,4096]{1,0:T(8,128)(2,1)}, bf16[32,4096]{1,0:T(8,128)(2,1)}, bf...) custom-call(s32[8,16]{1,0:T(8,128)} %bitcast.31, ...), custom_call_target="tpu_custom_call" | custom-call | flops 1 | bytes 1 | tf_op jit(solution)/shard_map/turned_products/pallas_call | solution.py:184
  26.6 1.7 %collective-permute-start = (bf16[80,4096]{1,0:T(8,128)(2,1)}, bf16[80,4096]{1,0:T(8,128)(2,1)}, u32[]{:S(2)}, u32[]{:S(2)}) collective-permute-start(bf16[80,4096]{1,0:T(8,128)(2,1)} %get-tuple-element.50), channel_id=1, source_target_pairs={{0,4},{1,5},{2,6},{3,7},{4,0},{5,1},{6,2},{7,3},{8,12},{9,13},{10,... | collective-permute-start | bytes 1966088 | tf_op jit(solution)/shard_map/ppermute | solution.py:334
  28.4 1.5 %collective-permute-start.1 = (bf16[80,4096]{1,0:T(8,128)(2,1)}, bf16[80,4096]{1,0:T(8,128)(2,1)}, u32[]{:S(2)}, u32[]{:S(2)}) collective-permute-start(bf16[80,4096]{1,0:T(8,128)(2,1)} %get-tuple-element.51), channel_id=1, source_target_pairs={{0,2},{1,3},{2,0},{3,1},{4,6},{5,7},{6,4},{7,5},{8,10},{9,11},{10,... | collective-permute-start | bytes 1966088 | tf_op jit(solution)/shard_map/ppermute | solution.py:334
  29.9 0.7 copy-done.9
  30.6 1.5 %collective-permute-done.6.refs_2_ = bf16[1024,128]{1,0:T(8,128)(2,1)S(1)} collective-permute-done((bf16[1024,128]{1,0:T(8,128)(2,1)S(1)}, bf16[1024,128]{1,0:T(8,128)(2,1)S(1)}, u32[]{:S(2)}, u32[]{:S(2)}) %collective-permute-start.6) | collective-permute-done | bytes 262176 | tf_op jit(solution)/shard_map/ppermute | solution.py:334
  33.0 1.1 %copy-done.7 = bf16[80,4096]{1,0:T(8,128)(2,1)S(1)} copy-done((bf16[80,4096]{1,0:T(8,128)(2,1)S(1)}, bf16[80,4096]{1,0:T(8,128)(2,1)}, u32[]{:S(2)}) %copy-start.7) | copy-done | bytes 655384
  34.0 11.5 %projections.1 = (bf16[64,64,128]{2,1,0:T(8,128)(2,1)}, bf16[64,64,128]{2,1,0:T(8,128)(2,1)}, bf16[64,64,128]{2,1,0:T(8,128)(2,1)S(1)}, bf16[64,64,128]{2,1,0:T(...) custom-call(s32[1]{0:T(128)} %bitcast.me_ref, ...), custom_call_target="tpu_custom_call" | custom-call | flops 1 | bytes 1 | tf_op jit(solution)/shard_map/projections/pallas_call | solution.py:239
  45.6 2.1 %copy-done.5 = bf16[64,64,128]{2,1,0:T(8,128)(2,1)S(1)} copy-done((bf16[64,64,128]{2,1,0:T(8,128)(2,1)S(1)}, bf16[64,64,128]{2,1,0:T(8,128)(2,1)}, u32[]{:S(2)}) %copy-start.5) | copy-done | bytes 1048600
  47.7 1.2 %copy-done.8 = bf16[64,64,128]{2,1,0:T(8,128)(2,1)S(1)} copy-done((bf16[64,64,128]{2,1,0:T(8,128)(2,1)S(1)}, bf16[64,64,128]{2,1,0:T(8,128)(2,1)}, u32[]{:S(2)}) %copy-start.8) | copy-done | bytes 1048600
  49.5 1.2 %copy-done.3 = bf16[64,64,128]{2,1,0:T(8,128)(2,1)S(1)} copy-done((bf16[64,64,128]{2,1,0:T(8,128)(2,1)S(1)}, bf16[64,64,128]{2,1,0:T(8,128)(2,1)}, u32[]{:S(2)}) %copy-start.3) | copy-done | bytes 1048600
  51.5 1.2 %copy-done = bf16[64,64,128]{2,1,0:T(8,128)(2,1)S(1)} copy-done((bf16[64,64,128]{2,1,0:T(8,128)(2,1)S(1)}, bf16[64,64,128]{2,1,0:T(8,128)(2,1)}, u32[]{:S(2)}) %copy-start) | copy-done | bytes 1048600
  52.7 1.4 %contract.6.refs_4_ = f32[128,128]{1,0:T(8,128)S(1)} custom-call(bf16[1024,128]{1,0:T(8,128)(2,1)S(1)} %collective-permute-done.4.refs_0_, bf16[1024,128]{1,0:T(8,128)(2,1)S(1)} %copy-done.10, bf16[1024,128]{1,0:T(8,128)(2,1)S(1)} %copy-done.12, bf16[1024,128]{1,0:T(8,128)(2,1)} %collective-permute-done.7.refs_3_, bf16[4096,128]{1,0:T(8,128)(2,1)S(1)} %bitcast.10, ...), custom_call_target="tpu_custom_call" | custom-call | flops 1 | bytes 1 | tf_op jit(solution)/shard_map/contract/pallas_call | solution.py:275
  55.0 11.4 %collective-permute-done.refs_0_ = bf16[80,4096]{1,0:T(8,128)(2,1)} collective-permute-done((bf16[80,4096]{1,0:T(8,128)(2,1)}, bf16[80,4096]{1,0:T(8,128)(2,1)}, u32[]{:S(2)}, u32[]{:S(2)}) %collective-permute-start) | collective-permute-done | bytes 655392 | tf_op jit(solution)/shard_map/ppermute | solution.py:334
  66.5 1.8 %contract_rows.5 = (f32[80,128]{1,0:T(8,128)S(1)}, bf16[48,4096]{1,0:T(8,128)(2,1)}, bf16[48,4096]{1,0:T(8,128)(2,1)}) custom-call(s32[1]{0:T(128)} %bitcast.me_ref, bf16[80,4096]{1,0:T(8,128)(2,1)} %collective-permute-done.refs_0_, bf16[80,4096]{1,0:T(8,128)(2,1)} %collective-permute-done.1.refs_1_, ...), custom_call_target="tpu_custom_call", output_to_operand_aliasing={{1}: (6, {}), {2}: (7, {})} | custom-call | flops 20000000000 | bytes 1 | tf_op jit(solution)/shard_map/contract_rows/pallas_call | solution.py:318
  68.3 1.6 %collective-permute-start.10 = (bf16[48,4096]{1,0:T(8,128)(2,1)}, bf16[48,4096]{1,0:T(8,128)(2,1)S(1)}, u32[]{:S(2)}, u32[]{:S(2)}) collective-permute-start(bf16[48,4096]{1,0:T(8,128)(2,1)} %get-tuple-element.70), channel_id=1, source_target_pairs={{0,4},{1,5},{2,6},{3,7},{4,0},{5,1},{6,2},{7,3},{8,12},{9,13},{10,... | collective-permute-start | bytes 1179656 | tf_op jit(solution)/shard_map/ppermute | solution.py:334
  69.9 1.1 %collective-permute-start.11 = (bf16[48,4096]{1,0:T(8,128)(2,1)}, bf16[48,4096]{1,0:T(8,128)(2,1)S(1)}, u32[]{:S(2)}, u32[]{:S(2)}) collective-permute-start(bf16[48,4096]{1,0:T(8,128)(2,1)} %get-tuple-element.71), channel_id=1, source_target_pairs={{0,2},{1,3},{2,0},{3,1},{4,6},{5,7},{6,4},{7,5},{8,10},{9,11},{10,... | collective-permute-start | bytes 1179656 | tf_op jit(solution)/shard_map/ppermute | solution.py:334
  71.0 8.6 %collective-permute-done.14.refs_0_ = bf16[80,4096]{1,0:T(8,128)(2,1)S(1)} collective-permute-done((bf16[80,4096]{1,0:T(8,128)(2,1)}, bf16[80,4096]{1,0:T(8,128)(2,1)S(1)}, u32[]{:S(2)}, u32[]{:S(2)}) %collective-permute-start.14) | collective-permute-done | bytes 655392 | tf_op jit(solution)/shard_map/ppermute | solution.py:334
  80.2 2.8 %collective-permute-start.16 = (f32[64,128]{1,0:T(8,128)S(1)}, f32[64,128]{1,0:T(8,128)S(1)}, u32[]{:S(2)}, u32[]{:S(2)}) collective-permute-start(f32[64,128]{1,0:T(8,128)S(1)} %get-tuple-element.84), channel_id=1, source_target_pairs={{0,8},{1,9},{2,10},{3,11},{4,12},{5,13},{6,14},{7,15},{8,0},{9,1},... | collective-permute-start | bytes 98312 | tf_op jit(solution)/shard_map/ppermute | solution.py:334
  83.0 1.6 %collective-permute-start.18 = (bf16[32,4096]{1,0:T(8,128)(2,1)}, bf16[32,4096]{1,0:T(8,128)(2,1)S(1)}, u32[]{:S(2)}, u32[]{:S(2)}) collective-permute-start(bf16[32,4096]{1,0:T(8,128)(2,1)} %get-tuple-element.86), channel_id=1, source_target_pairs={{0,5},{1,4},{2,7},{3,6},{4,1},{5,0},{6,3},{7,2},{8,13},{9,12},{10,... | collective-permute-start | bytes 786440 | tf_op jit(solution)/shard_map/ppermute | solution.py:334
  84.6 1.2 %collective-permute-start.19 = (bf16[32,4096]{1,0:T(8,128)(2,1)}, bf16[32,4096]{1,0:T(8,128)(2,1)S(1)}, u32[]{:S(2)}, u32[]{:S(2)}) collective-permute-start(bf16[32,4096]{1,0:T(8,128)(2,1)} %get-tuple-element.87), channel_id=1, source_target_pairs={{0,3},{1,2},{2,1},{3,0},{4,7},{5,6},{6,5},{7,4},{8,11},{9,10},{10,... | collective-permute-start | bytes 786440 | tf_op jit(solution)/shard_map/ppermute | solution.py:334
  85.8 2.8 %collective-permute-done.16.refs_5_ = f32[64,128]{1,0:T(8,128)S(1)} collective-permute-done((f32[64,128]{1,0:T(8,128)S(1)}, f32[64,128]{1,0:T(8,128)S(1)}, u32[]{:S(2)}, u32[]{:S(2)}) %collective-permute-start.16) | collective-permute-done | bytes 32800 | tf_op jit(solution)/shard_map/ppermute | solution.py:334
  88.6 3.4 %collective-permute-start.17 = (f32[16,128]{1,0:T(8,128)S(1)}, f32[16,128]{1,0:T(8,128)S(1)}, u32[]{:S(2)}, u32[]{:S(2)}) collective-permute-start(f32[16,128]{1,0:T(8,128)S(1)} %slice_add_fusion), channel_id=1, source_target_pairs={{0,6},{1,7},{2,4},{3,5},{4,2},{5,3},{6,0},{7,1},{8,14},{9,15},{10,... | collective-permute-start | bytes 24584 | tf_op jit(solution)/shard_map/ppermute | solution.py:334
  92.9 1.4 %collective-permute-done.18.refs_0_ = bf16[32,4096]{1,0:T(8,128)(2,1)S(1)} collective-permute-done((bf16[32,4096]{1,0:T(8,128)(2,1)}, bf16[32,4096]{1,0:T(8,128)(2,1)S(1)}, u32[]{:S(2)}, u32[]{:S(2)}) %collective-permute-start.18) | collective-permute-done | bytes 262176 | tf_op jit(solution)/shard_map/ppermute | solution.py:334
  94.8 1.6 %collective-permute-start.20 = (f32[16,128]{1,0:T(8,128)S(1)}, f32[16,128]{1,0:T(8,128)S(1)}, u32[]{:S(2)}, u32[]{:S(2)}) collective-permute-start(f32[16,128]{1,0:T(8,128)S(1)} %get-tuple-element.89), channel_id=1, source_target_pairs={{0,4},{1,5},{2,6},{3,7},{4,0},{5,1},{6,2},{7,3},{8,12},{9,13},{10,... | collective-permute-start | bytes 24584 | tf_op jit(solution)/shard_map/ppermute | solution.py:334
  96.4 1.0 %collective-permute-start.21 = (f32[16,128]{1,0:T(8,128)S(1)}, f32[16,128]{1,0:T(8,128)S(1)}, u32[]{:S(2)}, u32[]{:S(2)}) collective-permute-start(f32[16,128]{1,0:T(8,128)S(1)} %get-tuple-element.90), channel_id=1, source_target_pairs={{0,2},{1,3},{2,0},{3,1},{4,6},{5,7},{6,4},{7,5},{8,10},{9,11},{10,... | collective-permute-start | bytes 24584 | tf_op jit(solution)/shard_map/ppermute | solution.py:334
  98.8 1.3 %collective-permute-done.21 = f32[16,128]{1,0:T(8,128)S(1)} collective-permute-done((f32[16,128]{1,0:T(8,128)S(1)}, f32[16,128]{1,0:T(8,128)S(1)}, u32[]{:S(2)}, u32[]{:S(2)}) %collective-permute-start.21) | collective-permute-done | bytes 8224 | tf_op jit(solution)/shard_map/ppermute | solution.py:334
  100.1 1.2 %collective-permute-done.22 = f32[8,128]{1,0:T(8,128)S(1)} collective-permute-done((f32[8,128]{1,0:T(8,128)S(1)}, f32[8,128]{1,0:T(8,128)S(1)}, u32[]{:S(2)}, u32[]{:S(2)}) %collective-permute-start.22) | collective-permute-done | bytes 4128 | tf_op jit(solution)/shard_map/ppermute | solution.py:334
  (75 shorter events, 7.6 us)
Async XLA Ops:
  2.0 14.4 %collective-permute-start.9 = (bf16[1024,128]{1,0:T(8,128)(2,1)S(1)}, bf16[1024,128]{1,0:T(8,128)(2,1)S(1)}, u32[]{:S(2)}, u32[]{:S(2)}) collective-permute-start(bf16[1024,128]{1,0:T(8,128)(2,1)S(1)} %get-tuple-element.48.refs_0_), channel_id=1, source_target_pairs={{0,6},{1,7},{2,4},{3,5},{4,2},{5,3},{6,0},{7,1},{8,14},{9,15},{10,... | collective-permute-start | bytes 786440 | tf_op jit(solution)/shard_map/ppermute | solution.py:334
  6.0 20.6 %collective-permute-start.8 = (bf16[1024,128]{1,0:T(8,128)(2,1)S(1)}, bf16[1024,128]{1,0:T(8,128)(2,1)S(1)}, u32[]{:S(2)}, u32[]{:S(2)}) collective-permute-start(bf16[1024,128]{1,0:T(8,128)(2,1)S(1)} %get-tuple-element.64), channel_id=1, source_target_pairs={{0,7},{1,6},{2,5},{3,4},{4,3},{5,2},{6,1},{7,0},{8,15},{9,14},{10,... | collective-permute-start | bytes 786440 | tf_op jit(solution)/shard_map/ppermute | solution.py:334
  13.2 15.1 %collective-permute-start.4 = (bf16[1024,128]{1,0:T(8,128)(2,1)}, bf16[1024,128]{1,0:T(8,128)(2,1)S(1)}, u32[]{:S(2)}, u32[]{:S(2)}) collective-permute-start(bf16[1024,128]{1,0:T(8,128)(2,1)} %get-tuple-element.59), channel_id=1, source_target_pairs={{0,1},{1,0},{2,3},{3,2},{4,5},{5,4},{6,7},{7,6},{8,9},{9,8},{10,11... | collective-permute-start | bytes 786440 | tf_op jit(solution)/shard_map/ppermute | solution.py:334
  13.5 16.4 %collective-permute-start.5 = (bf16[1024,128]{1,0:T(8,128)(2,1)}, bf16[1024,128]{1,0:T(8,128)(2,1)S(1)}, u32[]{:S(2)}, u32[]{:S(2)}) collective-permute-start(bf16[1024,128]{1,0:T(8,128)(2,1)} %get-tuple-element.60), channel_id=1, source_target_pairs={{0,1},{1,0},{2,3},{3,2},{4,5},{5,4},{6,7},{7,6},{8,9},{9,8},{10,11... | collective-permute-start | bytes 786440 | tf_op jit(solution)/shard_map/ppermute | solution.py:334
  13.8 40.3 %collective-permute-start.2 = (bf16[3072,128]{1,0:T(8,128)(2,1)}, bf16[3072,128]{1,0:T(8,128)(2,1)S(1)}, u32[]{:S(2)}, u32[]{:S(2)}) collective-permute-start(bf16[3072,128]{1,0:T(8,128)(2,1)} %get-tuple-element.55), channel_id=1, source_target_pairs={{0,6},{1,7},{2,4},{3,5},{4,2},{5,3},{6,0},{7,1},{8,14},{9,15},{10,... | collective-permute-start | bytes 2359304 | tf_op jit(solution)/shard_map/ppermute | solution.py:334
  16.4 38.0 %collective-permute-start.3 = (bf16[3072,128]{1,0:T(8,128)(2,1)}, bf16[3072,128]{1,0:T(8,128)(2,1)S(1)}, u32[]{:S(2)}, u32[]{:S(2)}) collective-permute-start(bf16[3072,128]{1,0:T(8,128)(2,1)} %get-tuple-element.56), channel_id=1, source_target_pairs={{0,7},{1,6},{2,5},{3,4},{4,3},{5,2},{6,1},{7,0},{8,15},{9,14},{10,... | collective-permute-start | bytes 2359304 | tf_op jit(solution)/shard_map/ppermute | solution.py:334
  17.7 12.9 %copy-start.21 = (bf16[1024,128]{1,0:T(8,128)(2,1)S(1)}, bf16[1024,128]{1,0:T(8,128)(2,1)}, u32[]{:S(2)}) copy-start(bf16[1024,128]{1,0:T(8,128)(2,1)} %get-tuple-element.61) | copy-start | bytes 786436
  17.7 27.8 %copy-start.2 = (bf16[4096,128]{1,0:T(8,128)(2,1)S(1)}, bf16[4096,128]{1,0:T(8,128)(2,1)}, u32[]{:S(2)}) copy-start(bf16[4096,128]{1,0:T(8,128)(2,1)} %get-tuple-element.49.refs_0_.refs_1_) | copy-start | bytes 3145732
  26.6 39.8 %collective-permute-start = (bf16[80,4096]{1,0:T(8,128)(2,1)}, bf16[80,4096]{1,0:T(8,128)(2,1)}, u32[]{:S(2)}, u32[]{:S(2)}) collective-permute-start(bf16[80,4096]{1,0:T(8,128)(2,1)} %get-tuple-element.50), channel_id=1, source_target_pairs={{0,4},{1,5},{2,6},{3,7},{4,0},{5,1},{6,2},{7,3},{8,12},{9,13},{10,... | collective-permute-start | bytes 1966088 | tf_op jit(solution)/shard_map/ppermute | solution.py:334
  28.4 38.1 %collective-permute-start.1 = (bf16[80,4096]{1,0:T(8,128)(2,1)}, bf16[80,4096]{1,0:T(8,128)(2,1)}, u32[]{:S(2)}, u32[]{:S(2)}) collective-permute-start(bf16[80,4096]{1,0:T(8,128)(2,1)} %get-tuple-element.51), channel_id=1, source_target_pairs={{0,2},{1,3},{2,0},{3,1},{4,6},{5,7},{6,4},{7,5},{8,10},{9,11},{10,... | collective-permute-start | bytes 1966088 | tf_op jit(solution)/shard_map/ppermute | solution.py:334
  30.6 1.5 %collective-permute-start.6 = (bf16[1024,128]{1,0:T(8,128)(2,1)S(1)}, bf16[1024,128]{1,0:T(8,128)(2,1)S(1)}, u32[]{:S(2)}, u32[]{:S(2)}) collective-permute-start(bf16[1024,128]{1,0:T(8,128)(2,1)S(1)} %copy-done.21), channel_id=1, source_target_pairs={{0,1},{1,0},{2,3},{3,2},{4,5},{5,4},{6,7},{7,6},{8,9},{9,8},{10,11... | collective-permute-start | bytes 786440 | tf_op jit(solution)/shard_map/ppermute | solution.py:334
  32.8 18.2 %collective-permute-start.7 = (bf16[1024,128]{1,0:T(8,128)(2,1)}, bf16[1024,128]{1,0:T(8,128)(2,1)}, u32[]{:S(2)}, u32[]{:S(2)}) collective-permute-start(bf16[1024,128]{1,0:T(8,128)(2,1)} %get-tuple-element.62), channel_id=1, source_target_pairs={{0,1},{1,0},{2,3},{3,2},{4,5},{5,4},{6,7},{7,6},{8,9},{9,8},{10,11... | collective-permute-start | bytes 786440 | tf_op jit(solution)/shard_map/ppermute | solution.py:334
  34.0 17.4 %copy-start.10 = (bf16[1024,128]{1,0:T(8,128)(2,1)S(1)}, bf16[1024,128]{1,0:T(8,128)(2,1)}, u32[]{:S(2)}) copy-start(bf16[1024,128]{1,0:T(8,128)(2,1)} %copy-done.9) | copy-start | bytes 786436
  34.0 17.4 %copy-start.12 = (bf16[1024,128]{1,0:T(8,128)(2,1)S(1)}, bf16[1024,128]{1,0:T(8,128)(2,1)}, u32[]{:S(2)}) copy-start(bf16[1024,128]{1,0:T(8,128)(2,1)} %copy-done.11) | copy-start | bytes 786436
  45.5 22.8 %copy-start.17 = (bf16[64,64,128]{2,1,0:T(8,128)(2,1)}, bf16[64,64,128]{2,1,0:T(8,128)(2,1)S(1)}, u32[]{:S(2)}) copy-start(bf16[64,64,128]{2,1,0:T(8,128)(2,1)S(1)} %get-tuple-element.54) | copy-start | bytes 3145732
  45.5 22.8 %copy-start.19 = (bf16[64,64,128]{2,1,0:T(8,128)(2,1)}, bf16[64,64,128]{2,1,0:T(8,128)(2,1)S(1)}, u32[]{:S(2)}) copy-start(bf16[64,64,128]{2,1,0:T(8,128)(2,1)S(1)} %get-tuple-element.53) | copy-start | bytes 3145732
  45.5 34.2 %copy-start.13 = (bf16[64,64,128]{2,1,0:T(8,128)(2,1)}, bf16[64,64,128]{2,1,0:T(8,128)(2,1)S(1)}, u32[]{:S(2)}) copy-start(bf16[64,64,128]{2,1,0:T(8,128)(2,1)S(1)} %get-tuple-element.77) | copy-start | bytes 3145732
  45.5 34.2 %copy-start.15 = (bf16[64,64,128]{2,1,0:T(8,128)(2,1)}, bf16[64,64,128]{2,1,0:T(8,128)(2,1)S(1)}, u32[]{:S(2)}) copy-start(bf16[64,64,128]{2,1,0:T(8,128)(2,1)S(1)} %get-tuple-element.76) | copy-start | bytes 3145732
  51.0 28.6 %collective-permute-start.14 = (bf16[80,4096]{1,0:T(8,128)(2,1)}, bf16[80,4096]{1,0:T(8,128)(2,1)S(1)}, u32[]{:S(2)}, u32[]{:S(2)}) collective-permute-start(bf16[80,4096]{1,0:T(8,128)(2,1)} %get-tuple-element.79), channel_id=1, source_target_pairs={{0,5},{1,4},{2,7},{3,6},{4,1},{5,0},{6,3},{7,2},{8,13},{9,12},{10,... | collective-permute-start | bytes 1966088 | tf_op jit(solution)/shard_map/ppermute | solution.py:334
  54.1 25.5 %collective-permute-start.15 = (bf16[80,4096]{1,0:T(8,128)(2,1)}, bf16[80,4096]{1,0:T(8,128)(2,1)S(1)}, u32[]{:S(2)}, u32[]{:S(2)}) collective-permute-start(bf16[80,4096]{1,0:T(8,128)(2,1)} %get-tuple-element.80), channel_id=1, source_target_pairs={{0,3},{1,2},{2,1},{3,0},{4,7},{5,6},{6,5},{7,4},{8,11},{9,10},{10,... | collective-permute-start | bytes 1966088 | tf_op jit(solution)/shard_map/ppermute | solution.py:334
  68.3 23.8 %collective-permute-start.10 = (bf16[48,4096]{1,0:T(8,128)(2,1)}, bf16[48,4096]{1,0:T(8,128)(2,1)S(1)}, u32[]{:S(2)}, u32[]{:S(2)}) collective-permute-start(bf16[48,4096]{1,0:T(8,128)(2,1)} %get-tuple-element.70), channel_id=1, source_target_pairs={{0,4},{1,5},{2,6},{3,7},{4,0},{5,1},{6,2},{7,3},{8,12},{9,13},{10,... | collective-permute-start | bytes 1179656 | tf_op jit(solution)/shard_map/ppermute | solution.py:334
  69.9 22.1 %collective-permute-start.11 = (bf16[48,4096]{1,0:T(8,128)(2,1)}, bf16[48,4096]{1,0:T(8,128)(2,1)S(1)}, u32[]{:S(2)}, u32[]{:S(2)}) collective-permute-start(bf16[48,4096]{1,0:T(8,128)(2,1)} %get-tuple-element.71), channel_id=1, source_target_pairs={{0,2},{1,3},{2,0},{3,1},{4,6},{5,7},{6,4},{7,5},{8,10},{9,11},{10,... | collective-permute-start | bytes 1179656 | tf_op jit(solution)/shard_map/ppermute | solution.py:334
  79.7 12.4 %copy-start.20 = (bf16[64,64,128]{2,1,0:T(8,128)(2,1)S(1)}, bf16[64,64,128]{2,1,0:T(8,128)(2,1)}, u32[]{:S(2)}) copy-start(bf16[64,64,128]{2,1,0:T(8,128)(2,1)} %copy-done.19) | copy-start | bytes 3145732
  80.2 8.4 %collective-permute-start.16 = (f32[64,128]{1,0:T(8,128)S(1)}, f32[64,128]{1,0:T(8,128)S(1)}, u32[]{:S(2)}, u32[]{:S(2)}) collective-permute-start(f32[64,128]{1,0:T(8,128)S(1)} %get-tuple-element.84), channel_id=1, source_target_pairs={{0,8},{1,9},{2,10},{3,11},{4,12},{5,13},{6,14},{7,15},{8,0},{9,1},... | collective-permute-start | bytes 98312 | tf_op jit(solution)/shard_map/ppermute | solution.py:334
  83.0 11.4 %collective-permute-start.18 = (bf16[32,4096]{1,0:T(8,128)(2,1)}, bf16[32,4096]{1,0:T(8,128)(2,1)S(1)}, u32[]{:S(2)}, u32[]{:S(2)}) collective-permute-start(bf16[32,4096]{1,0:T(8,128)(2,1)} %get-tuple-element.86), channel_id=1, source_target_pairs={{0,5},{1,4},{2,7},{3,6},{4,1},{5,0},{6,3},{7,2},{8,13},{9,12},{10,... | collective-permute-start | bytes 786440 | tf_op jit(solution)/shard_map/ppermute | solution.py:334
  84.6 9.7 %collective-permute-start.19 = (bf16[32,4096]{1,0:T(8,128)(2,1)}, bf16[32,4096]{1,0:T(8,128)(2,1)S(1)}, u32[]{:S(2)}, u32[]{:S(2)}) collective-permute-start(bf16[32,4096]{1,0:T(8,128)(2,1)} %get-tuple-element.87), channel_id=1, source_target_pairs={{0,3},{1,2},{2,1},{3,0},{4,7},{5,6},{6,5},{7,4},{8,11},{9,10},{10,... | collective-permute-start | bytes 786440 | tf_op jit(solution)/shard_map/ppermute | solution.py:334
  88.6 10.2 %collective-permute-start.17 = (f32[16,128]{1,0:T(8,128)S(1)}, f32[16,128]{1,0:T(8,128)S(1)}, u32[]{:S(2)}, u32[]{:S(2)}) collective-permute-start(f32[16,128]{1,0:T(8,128)S(1)} %slice_add_fusion), channel_id=1, source_target_pairs={{0,6},{1,7},{2,4},{3,5},{4,2},{5,3},{6,0},{7,1},{8,14},{9,15},{10,... | collective-permute-start | bytes 24584 | tf_op jit(solution)/shard_map/ppermute | solution.py:334
  92.5 5.2 %collective-permute-start.12 = (bf16[16,4096]{1,0:T(8,128)(2,1)}, bf16[16,4096]{1,0:T(8,128)(2,1)S(1)}, u32[]{:S(2)}, u32[]{:S(2)}) collective-permute-start(bf16[16,4096]{1,0:T(8,128)(2,1)} %get-tuple-element.74), channel_id=1, source_target_pairs={{0,5},{1,4},{2,7},{3,6},{4,1},{5,0},{6,3},{7,2},{8,13},{9,12},{10,... | collective-permute-start | bytes 393224 | tf_op jit(solution)/shard_map/ppermute | solution.py:334
  92.6 5.8 %collective-permute-start.13 = (bf16[16,4096]{1,0:T(8,128)(2,1)}, bf16[16,4096]{1,0:T(8,128)(2,1)S(1)}, u32[]{:S(2)}, u32[]{:S(2)}) collective-permute-start(bf16[16,4096]{1,0:T(8,128)(2,1)} %get-tuple-element.75), channel_id=1, source_target_pairs={{0,3},{1,2},{2,1},{3,0},{4,7},{5,6},{6,5},{7,4},{8,11},{9,10},{10,... | collective-permute-start | bytes 393224 | tf_op jit(solution)/shard_map/ppermute | solution.py:334
  94.8 4.0 %collective-permute-start.20 = (f32[16,128]{1,0:T(8,128)S(1)}, f32[16,128]{1,0:T(8,128)S(1)}, u32[]{:S(2)}, u32[]{:S(2)}) collective-permute-start(f32[16,128]{1,0:T(8,128)S(1)} %get-tuple-element.89), channel_id=1, source_target_pairs={{0,4},{1,5},{2,6},{3,7},{4,0},{5,1},{6,2},{7,3},{8,12},{9,13},{10,... | collective-permute-start | bytes 24584 | tf_op jit(solution)/shard_map/ppermute | solution.py:334
  96.4 3.7 %collective-permute-start.21 = (f32[16,128]{1,0:T(8,128)S(1)}, f32[16,128]{1,0:T(8,128)S(1)}, u32[]{:S(2)}, u32[]{:S(2)}) collective-permute-start(f32[16,128]{1,0:T(8,128)S(1)} %get-tuple-element.90), channel_id=1, source_target_pairs={{0,2},{1,3},{2,0},{3,1},{4,6},{5,7},{6,4},{7,5},{8,10},{9,11},{10,... | collective-permute-start | bytes 24584 | tf_op jit(solution)/shard_map/ppermute | solution.py:334
  100.1 1.2 %collective-permute-start.22 = (f32[8,128]{1,0:T(8,128)S(1)}, f32[8,128]{1,0:T(8,128)S(1)}, u32[]{:S(2)}, u32[]{:S(2)}) collective-permute-start(f32[8,128]{1,0:T(8,128)S(1)} %slice_select_fusion), channel_id=1, source_target_pairs={{0,1},{1,0},{2,3},{3,2},{4,5},{5,4},{6,7},{7,6},{8,9},{9,8},{10,11... | collective-permute-start | bytes 12296 | tf_op jit(solution)/shard_map/ppermute | solution.py:334
  (13 other events, 40.8 us)

commit v7 on v6

--- a/solution.py
+++ b/solution.py
@@ -423,7 +423,7 @@
     square = contract_rows(
         me, second_mid, second_rights, (slab, slab), slab, [("own", 0, rest), ("own", slab, inner)]
     )
-    square = [exchange(square[at], 2 * (at + 1), devices) for at in (1, 0)]
+    square = [exchange(square[at], 2 * (at + 1), devices) for at in (0, 1)]
     (chip,) = contract_rows(
         me, second_near, second_rights, (slab,), slab, [("own", 0, chip), ("own", 0, inner)]
     )

time: 102 us -> 102 us (level)
  transfers between devices with their start and end apart: 23 -> 23, of which waited for: 10 -> 11; matrix products, arithmetic and copies ran while one was open for 0% -> 0% of each run, Pallas kernels for 33% -> 34%
where the time goes in v7:
time: 102 us; the launch traced here: 101 us
  Pallas kernels  35.9 us (35%)
  waiting for transfers between devices  28.7 us (28%)
  starting transfers between devices  26.3 us (26%)
  local copies, waits for them, and re-layouts  9.55 us (9%)
    ppermute x23, waiting for transfers between devices, exchange(): return lax.ppermute(value, 'tensor', [(i, i ^ k) for i in range(devices)])  28.7 us
    ppermute x23, starting transfers between devices, exchange(): return lax.ppermute(value, 'tensor', [(i, i ^ k) for i in range(devices)])  26.3 us
    pallas_call x1, Pallas kernels, projections(): pl.pallas_call(functools.partial(project_kernel, width, rows), grid=(step...  11.5 us
    unnamed x44, local copies, waits for them, and re-layouts  9.55 us
    pallas_call x2, Pallas kernels, products(): pl.pallas_call(functools.partial(product_kernel, slots, wanted, width, ch...  9.18 us
    pallas_call x1, Pallas kernels, turned_products(): pl.pallas_call(functools.partial(turned_product_kernel, slots, width, chu...  8.88 us
    pallas_call x5, Pallas kernels, contract_rows(): pl.pallas_call(functools.partial(rows_kernel, count, rows, slab, kinds, l...  3.58 us
    pallas_call x4, Pallas kernels, contract(): pl.pallas_call(functools.partial(contract_kernel, count, begins, len(star...  2.84 us
  transfers between devices with their start and end apart: 23, of which 11 were waited for; matrix products, arithmetic and copies ran while one was open for 0% of the time, Pallas kernels for 34%

profile of v7, /device:TPU:0, one launch (start us, length us, event | category | flops | bytes accessed | tf_op | source)
XLA Modules:
  0.0 101.3 jit_solution(432556679583250778)
XLA Ops:
  0.0 2.0 %products.2 = (bf16[1024,128]{1,0:T(8,128)(2,1)S(1)}, bf16[1024,128]{1,0:T(8,128)(2,1)S(1)}) custom-call(s32[8,16]{1,0:T(8,128)} %bitcast.29, bf16[1,512,512]{2,1,0:T(8,128)(2,1)} %virt_hbm.5, bf16[1,8,4096,128]{3,2,1,0:T(8,128)(2,1)} %block_ref.1), custom_call_target="tpu_custom_call" | custom-call | flops 1 | bytes 1 | tf_op jit(solution)/shard_map/products/pallas_call | solution.py:104
  2.0 4.0 %collective-permute-start.9 = (bf16[1024,128]{1,0:T(8,128)(2,1)S(1)}, bf16[1024,128]{1,0:T(8,128)(2,1)S(1)}, u32[]{:S(2)}, u32[]{:S(2)}) collective-permute-start(bf16[1024,128]{1,0:T(8,128)(2,1)S(1)} %get-tuple-element.48.refs_0_), channel_id=1, source_target_pairs={{0,6},{1,7},{2,4},{3,5},{4,2},{5,3},{6,0},{7,1},{8,14},{9,15},{10,... | collective-permute-start | bytes 786440 | tf_op jit(solution)/shard_map/ppermute | solution.py:334
  6.1 7.2 %products.3 = (bf16[4096,128]{1,0:T(8,128)(2,1)}, bf16[1024,128]{1,0:T(8,128)(2,1)}, bf16[1024,128]{1,0:T(8,128)(2,1)}, bf16[1024,128]{1,0:T(8,128)(2,1)}, bf16[...) custom-call(s32[8,16]{1,0:T(8,128)} %bitcast.30, bf16[1,512,512]{2,1,0:T(8,128)(2,1)} %virt_hbm.5, ...), custom_call_target="tpu_custom_call" | custom-call | flops 1 | bytes 1 | tf_op jit(solution)/shard_map/products/pallas_call | solution.py:104
  13.8 2.6 %collective-permute-start.2 = (bf16[3072,128]{1,0:T(8,128)(2,1)}, bf16[3072,128]{1,0:T(8,128)(2,1)S(1)}, u32[]{:S(2)}, u32[]{:S(2)}) collective-permute-start(bf16[3072,128]{1,0:T(8,128)(2,1)} %get-tuple-element.55), channel_id=1, source_target_pairs={{0,6},{1,7},{2,4},{3,5},{4,2},{5,3},{6,0},{7,1},{8,14},{9,15},{10,... | collective-permute-start | bytes 2359304 | tf_op jit(solution)/shard_map/ppermute | solution.py:334
  16.5 1.2 %copy-done.1 = bf16[4096,128]{1,0:T(8,128)(2,1)S(1)} copy-done((bf16[4096,128]{1,0:T(8,128)(2,1)S(1)}, bf16[4096,128]{1,0:T(8,128)(2,1)}, u32[]{:S(2)}) %copy-start.1) | copy-done | bytes 1048600
  17.7 8.9 %turned_products.1 = (bf16[80,4096]{1,0:T(8,128)(2,1)}, bf16[48,4096]{1,0:T(8,128)(2,1)}, bf16[80,4096]{1,0:T(8,128)(2,1)}, bf16[32,4096]{1,0:T(8,128)(2,1)}, bf...) custom-call(s32[8,16]{1,0:T(8,128)} %bitcast.31, ...), custom_call_target="tpu_custom_call" | custom-call | flops 1 | bytes 1 | tf_op jit(solution)/shard_map/turned_products/pallas_call | solution.py:184
  26.6 1.7 %collective-permute-start = (bf16[80,4096]{1,0:T(8,128)(2,1)}, bf16[80,4096]{1,0:T(8,128)(2,1)}, u32[]{:S(2)}, u32[]{:S(2)}) collective-permute-start(bf16[80,4096]{1,0:T(8,128)(2,1)} %get-tuple-element.50), channel_id=1, source_target_pairs={{0,4},{1,5},{2,6},{3,7},{4,0},{5,1},{6,2},{7,3},{8,12},{9,13},{10,... | collective-permute-start | bytes 1966088 | tf_op jit(solution)/shard_map/ppermute | solution.py:334
  28.4 1.5 %collective-permute-start.1 = (bf16[80,4096]{1,0:T(8,128)(2,1)}, bf16[80,4096]{1,0:T(8,128)(2,1)}, u32[]{:S(2)}, u32[]{:S(2)}) collective-permute-start(bf16[80,4096]{1,0:T(8,128)(2,1)} %get-tuple-element.51), channel_id=1, source_target_pairs={{0,2},{1,3},{2,0},{3,1},{4,6},{5,7},{6,4},{7,5},{8,10},{9,11},{10,... | collective-permute-start | bytes 1966088 | tf_op jit(solution)/shard_map/ppermute | solution.py:334
  29.9 0.7 copy-done.9
  30.6 1.5 %collective-permute-done.6.refs_2_ = bf16[1024,128]{1,0:T(8,128)(2,1)S(1)} collective-permute-done((bf16[1024,128]{1,0:T(8,128)(2,1)S(1)}, bf16[1024,128]{1,0:T(8,128)(2,1)S(1)}, u32[]{:S(2)}, u32[]{:S(2)}) %collective-permute-start.6) | collective-permute-done | bytes 262176 | tf_op jit(solution)/shard_map/ppermute | solution.py:334
  32.1 0.7 copy-done.11
  33.0 1.1 %copy-done.7 = bf16[80,4096]{1,0:T(8,128)(2,1)S(1)} copy-done((bf16[80,4096]{1,0:T(8,128)(2,1)S(1)}, bf16[80,4096]{1,0:T(8,128)(2,1)}, u32[]{:S(2)}) %copy-start.7) | copy-done | bytes 655384
  34.0 11.5 %projections.1 = (bf16[64,64,128]{2,1,0:T(8,128)(2,1)}, bf16[64,64,128]{2,1,0:T(8,128)(2,1)}, bf16[64,64,128]{2,1,0:T(8,128)(2,1)S(1)}, bf16[64,64,128]{2,1,0:T(...) custom-call(s32[1]{0:T(128)} %bitcast.me_ref, ...), custom_call_target="tpu_custom_call" | custom-call | flops 1 | bytes 1 | tf_op jit(solution)/shard_map/projections/pallas_call | solution.py:239
  45.6 2.1 %copy-done.5 = bf16[64,64,128]{2,1,0:T(8,128)(2,1)S(1)} copy-done((bf16[64,64,128]{2,1,0:T(8,128)(2,1)S(1)}, bf16[64,64,128]{2,1,0:T(8,128)(2,1)}, u32[]{:S(2)}) %copy-start.5) | copy-done | bytes 1048600
  47.7 1.2 %copy-done.8 = bf16[64,64,128]{2,1,0:T(8,128)(2,1)S(1)} copy-done((bf16[64,64,128]{2,1,0:T(8,128)(2,1)S(1)}, bf16[64,64,128]{2,1,0:T(8,128)(2,1)}, u32[]{:S(2)}) %copy-start.8) | copy-done | bytes 1048600
  49.5 1.2 %copy-done.3 = bf16[64,64,128]{2,1,0:T(8,128)(2,1)S(1)} copy-done((bf16[64,64,128]{2,1,0:T(8,128)(2,1)S(1)}, bf16[64,64,128]{2,1,0:T(8,128)(2,1)}, u32[]{:S(2)}) %copy-start.3) | copy-done | bytes 1048600
  51.5 1.2 %copy-done = bf16[64,64,128]{2,1,0:T(8,128)(2,1)S(1)} copy-done((bf16[64,64,128]{2,1,0:T(8,128)(2,1)S(1)}, bf16[64,64,128]{2,1,0:T(8,128)(2,1)}, u32[]{:S(2)}) %copy-start) | copy-done | bytes 1048600
  52.7 1.4 %contract.6.refs_4_ = f32[128,128]{1,0:T(8,128)S(1)} custom-call(bf16[1024,128]{1,0:T(8,128)(2,1)S(1)} %collective-permute-done.4.refs_0_, bf16[1024,128]{1,0:T(8,128)(2,1)S(1)} %copy-done.10, bf16[1024,128]{1,0:T(8,128)(2,1)S(1)} %copy-done.12, bf16[1024,128]{1,0:T(8,128)(2,1)} %collective-permute-done.7.refs_3_, bf16[4096,128]{1,0:T(8,128)(2,1)S(1)} %bitcast.10, ...), custom_call_target="tpu_custom_call" | custom-call | flops 1 | bytes 1 | tf_op jit(solution)/shard_map/contract/pallas_call | solution.py:275
  55.0 11.4 %collective-permute-done.refs_0_ = bf16[80,4096]{1,0:T(8,128)(2,1)} collective-permute-done((bf16[80,4096]{1,0:T(8,128)(2,1)}, bf16[80,4096]{1,0:T(8,128)(2,1)}, u32[]{:S(2)}, u32[]{:S(2)}) %collective-permute-start) | collective-permute-done | bytes 655392 | tf_op jit(solution)/shard_map/ppermute | solution.py:334
  66.5 1.8 %contract_rows.5 = (f32[80,128]{1,0:T(8,128)S(1)}, bf16[48,4096]{1,0:T(8,128)(2,1)}, bf16[48,4096]{1,0:T(8,128)(2,1)}) custom-call(s32[1]{0:T(128)} %bitcast.me_ref, bf16[80,4096]{1,0:T(8,128)(2,1)} %collective-permute-done.refs_0_, bf16[80,4096]{1,0:T(8,128)(2,1)} %collective-permute-done.1.refs_1_, ...), custom_call_target="tpu_custom_call", output_to_operand_aliasing={{1}: (6, {}), {2}: (7, {})} | custom-call | flops 20000000000 | bytes 1 | tf_op jit(solution)/shard_map/contract_rows/pallas_call | solution.py:318
  68.3 1.6 %collective-permute-start.10 = (bf16[48,4096]{1,0:T(8,128)(2,1)}, bf16[48,4096]{1,0:T(8,128)(2,1)S(1)}, u32[]{:S(2)}, u32[]{:S(2)}) collective-permute-start(bf16[48,4096]{1,0:T(8,128)(2,1)} %get-tuple-element.70), channel_id=1, source_target_pairs={{0,4},{1,5},{2,6},{3,7},{4,0},{5,1},{6,2},{7,3},{8,12},{9,13},{10,... | collective-permute-start | bytes 1179656 | tf_op jit(solution)/shard_map/ppermute | solution.py:334
  69.9 1.1 %collective-permute-start.11 = (bf16[48,4096]{1,0:T(8,128)(2,1)}, bf16[48,4096]{1,0:T(8,128)(2,1)S(1)}, u32[]{:S(2)}, u32[]{:S(2)}) collective-permute-start(bf16[48,4096]{1,0:T(8,128)(2,1)} %get-tuple-element.71), channel_id=1, source_target_pairs={{0,2},{1,3},{2,0},{3,1},{4,6},{5,7},{6,4},{7,5},{8,10},{9,11},{10,... | collective-permute-start | bytes 1179656 | tf_op jit(solution)/shard_map/ppermute | solution.py:334
  71.0 8.6 %collective-permute-done.14.refs_0_ = bf16[80,4096]{1,0:T(8,128)(2,1)S(1)} collective-permute-done((bf16[80,4096]{1,0:T(8,128)(2,1)}, bf16[80,4096]{1,0:T(8,128)(2,1)S(1)}, u32[]{:S(2)}, u32[]{:S(2)}) %collective-permute-start.14) | collective-permute-done | bytes 655392 | tf_op jit(solution)/shard_map/ppermute | solution.py:334
  80.2 2.8 %collective-permute-start.16 = (f32[64,128]{1,0:T(8,128)S(1)}, f32[64,128]{1,0:T(8,128)S(1)}, u32[]{:S(2)}, u32[]{:S(2)}) collective-permute-start(f32[64,128]{1,0:T(8,128)S(1)} %get-tuple-element.84), channel_id=1, source_target_pairs={{0,8},{1,9},{2,10},{3,11},{4,12},{5,13},{6,14},{7,15},{8,0},{9,1},... | collective-permute-start | bytes 98312 | tf_op jit(solution)/shard_map/ppermute | solution.py:334
  83.0 1.6 %collective-permute-start.18 = (bf16[32,4096]{1,0:T(8,128)(2,1)}, bf16[32,4096]{1,0:T(8,128)(2,1)S(1)}, u32[]{:S(2)}, u32[]{:S(2)}) collective-permute-start(bf16[32,4096]{1,0:T(8,128)(2,1)} %get-tuple-element.86), channel_id=1, source_target_pairs={{0,5},{1,4},{2,7},{3,6},{4,1},{5,0},{6,3},{7,2},{8,13},{9,12},{10,... | collective-permute-start | bytes 786440 | tf_op jit(solution)/shard_map/ppermute | solution.py:334
  84.6 1.2 %collective-permute-start.19 = (bf16[32,4096]{1,0:T(8,128)(2,1)}, bf16[32,4096]{1,0:T(8,128)(2,1)S(1)}, u32[]{:S(2)}, u32[]{:S(2)}) collective-permute-start(bf16[32,4096]{1,0:T(8,128)(2,1)} %get-tuple-element.87), channel_id=1, source_target_pairs={{0,3},{1,2},{2,1},{3,0},{4,7},{5,6},{6,5},{7,4},{8,11},{9,10},{10,... | collective-permute-start | bytes 786440 | tf_op jit(solution)/shard_map/ppermute | solution.py:334
  85.8 2.8 %collective-permute-done.16.refs_5_ = f32[64,128]{1,0:T(8,128)S(1)} collective-permute-done((f32[64,128]{1,0:T(8,128)S(1)}, f32[64,128]{1,0:T(8,128)S(1)}, u32[]{:S(2)}, u32[]{:S(2)}) %collective-permute-start.16) | collective-permute-done | bytes 32800 | tf_op jit(solution)/shard_map/ppermute | solution.py:334
  88.6 3.4 %collective-permute-start.17 = (f32[16,128]{1,0:T(8,128)S(1)}, f32[16,128]{1,0:T(8,128)S(1)}, u32[]{:S(2)}, u32[]{:S(2)}) collective-permute-start(f32[16,128]{1,0:T(8,128)S(1)} %slice_add_fusion), channel_id=1, source_target_pairs={{0,6},{1,7},{2,4},{3,5},{4,2},{5,3},{6,0},{7,1},{8,14},{9,15},{10,... | collective-permute-start | bytes 24584 | tf_op jit(solution)/shard_map/ppermute | solution.py:334
  92.9 1.4 %collective-permute-done.18.refs_0_ = bf16[32,4096]{1,0:T(8,128)(2,1)S(1)} collective-permute-done((bf16[32,4096]{1,0:T(8,128)(2,1)}, bf16[32,4096]{1,0:T(8,128)(2,1)S(1)}, u32[]{:S(2)}, u32[]{:S(2)}) %collective-permute-start.18) | collective-permute-done | bytes 262176 | tf_op jit(solution)/shard_map/ppermute | solution.py:334
  94.8 1.1 %collective-permute-start.20 = (f32[16,128]{1,0:T(8,128)S(1)}, f32[16,128]{1,0:T(8,128)S(1)}, u32[]{:S(2)}, u32[]{:S(2)}) collective-permute-start(f32[16,128]{1,0:T(8,128)S(1)} %get-tuple-element.89), channel_id=1, source_target_pairs={{0,2},{1,3},{2,0},{3,1},{4,6},{5,7},{6,4},{7,5},{8,10},{9,11},{10,... | collective-permute-start | bytes 24584 | tf_op jit(solution)/shard_map/ppermute | solution.py:334
  95.9 1.6 %collective-permute-start.21 = (f32[16,128]{1,0:T(8,128)S(1)}, f32[16,128]{1,0:T(8,128)S(1)}, u32[]{:S(2)}, u32[]{:S(2)}) collective-permute-start(f32[16,128]{1,0:T(8,128)S(1)} %get-tuple-element.90), channel_id=1, source_target_pairs={{0,4},{1,5},{2,6},{3,7},{4,0},{5,1},{6,2},{7,3},{8,12},{9,13},{10,... | collective-permute-start | bytes 24584 | tf_op jit(solution)/shard_map/ppermute | solution.py:334
  99.6 1.2 %collective-permute-done.22 = f32[8,128]{1,0:T(8,128)S(1)} collective-permute-done((f32[8,128]{1,0:T(8,128)S(1)}, f32[8,128]{1,0:T(8,128)S(1)}, u32[]{:S(2)}, u32[]{:S(2)}) %collective-permute-start.22) | collective-permute-done | bytes 4128 | tf_op jit(solution)/shard_map/ppermute | solution.py:334
  (75 shorter events, 7.6 us)
Async XLA Ops:
  2.0 14.4 %collective-permute-start.9 = (bf16[1024,128]{1,0:T(8,128)(2,1)S(1)}, bf16[1024,128]{1,0:T(8,128)(2,1)S(1)}, u32[]{:S(2)}, u32[]{:S(2)}) collective-permute-start(bf16[1024,128]{1,0:T(8,128)(2,1)S(1)} %get-tuple-element.48.refs_0_), channel_id=1, source_target_pairs={{0,6},{1,7},{2,4},{3,5},{4,2},{5,3},{6,0},{7,1},{8,14},{9,15},{10,... | collective-permute-start | bytes 786440 | tf_op jit(solution)/shard_map/ppermute | solution.py:334
  6.0 20.6 %collective-permute-start.8 = (bf16[1024,128]{1,0:T(8,128)(2,1)S(1)}, bf16[1024,128]{1,0:T(8,128)(2,1)S(1)}, u32[]{:S(2)}, u32[]{:S(2)}) collective-permute-start(bf16[1024,128]{1,0:T(8,128)(2,1)S(1)} %get-tuple-element.64), channel_id=1, source_target_pairs={{0,7},{1,6},{2,5},{3,4},{4,3},{5,2},{6,1},{7,0},{8,15},{9,14},{10,... | collective-permute-start | bytes 786440 | tf_op jit(solution)/shard_map/ppermute | solution.py:334
  13.2 15.1 %collective-permute-start.4 = (bf16[1024,128]{1,0:T(8,128)(2,1)}, bf16[1024,128]{1,0:T(8,128)(2,1)S(1)}, u32[]{:S(2)}, u32[]{:S(2)}) collective-permute-start(bf16[1024,128]{1,0:T(8,128)(2,1)} %get-tuple-element.59), channel_id=1, source_target_pairs={{0,1},{1,0},{2,3},{3,2},{4,5},{5,4},{6,7},{7,6},{8,9},{9,8},{10,11... | collective-permute-start | bytes 786440 | tf_op jit(solution)/shard_map/ppermute | solution.py:334
  13.5 16.4 %collective-permute-start.5 = (bf16[1024,128]{1,0:T(8,128)(2,1)}, bf16[1024,128]{1,0:T(8,128)(2,1)S(1)}, u32[]{:S(2)}, u32[]{:S(2)}) collective-permute-start(bf16[1024,128]{1,0:T(8,128)(2,1)} %get-tuple-element.60), channel_id=1, source_target_pairs={{0,1},{1,0},{2,3},{3,2},{4,5},{5,4},{6,7},{7,6},{8,9},{9,8},{10,11... | collective-permute-start | bytes 786440 | tf_op jit(solution)/shard_map/ppermute | solution.py:334
  13.8 40.3 %collective-permute-start.2 = (bf16[3072,128]{1,0:T(8,128)(2,1)}, bf16[3072,128]{1,0:T(8,128)(2,1)S(1)}, u32[]{:S(2)}, u32[]{:S(2)}) collective-permute-start(bf16[3072,128]{1,0:T(8,128)(2,1)} %get-tuple-element.55), channel_id=1, source_target_pairs={{0,6},{1,7},{2,4},{3,5},{4,2},{5,3},{6,0},{7,1},{8,14},{9,15},{10,... | collective-permute-start | bytes 2359304 | tf_op jit(solution)/shard_map/ppermute | solution.py:334
  16.4 38.0 %collective-permute-start.3 = (bf16[3072,128]{1,0:T(8,128)(2,1)}, bf16[3072,128]{1,0:T(8,128)(2,1)S(1)}, u32[]{:S(2)}, u32[]{:S(2)}) collective-permute-start(bf16[3072,128]{1,0:T(8,128)(2,1)} %get-tuple-element.56), channel_id=1, source_target_pairs={{0,7},{1,6},{2,5},{3,4},{4,3},{5,2},{6,1},{7,0},{8,15},{9,14},{10,... | collective-permute-start | bytes 2359304 | tf_op jit(solution)/shard_map/ppermute | solution.py:334
  17.7 12.9 %copy-start.21 = (bf16[1024,128]{1,0:T(8,128)(2,1)S(1)}, bf16[1024,128]{1,0:T(8,128)(2,1)}, u32[]{:S(2)}) copy-start(bf16[1024,128]{1,0:T(8,128)(2,1)} %get-tuple-element.61) | copy-start | bytes 786436
  17.7 27.8 %copy-start.2 = (bf16[4096,128]{1,0:T(8,128)(2,1)S(1)}, bf16[4096,128]{1,0:T(8,128)(2,1)}, u32[]{:S(2)}) copy-start(bf16[4096,128]{1,0:T(8,128)(2,1)} %get-tuple-element.49.refs_0_.refs_1_) | copy-start | bytes 3145732
  26.6 39.8 %collective-permute-start = (bf16[80,4096]{1,0:T(8,128)(2,1)}, bf16[80,4096]{1,0:T(8,128)(2,1)}, u32[]{:S(2)}, u32[]{:S(2)}) collective-permute-start(bf16[80,4096]{1,0:T(8,128)(2,1)} %get-tuple-element.50), channel_id=1, source_target_pairs={{0,4},{1,5},{2,6},{3,7},{4,0},{5,1},{6,2},{7,3},{8,12},{9,13},{10,... | collective-permute-start | bytes 1966088 | tf_op jit(solution)/shard_map/ppermute | solution.py:334
  28.4 38.1 %collective-permute-start.1 = (bf16[80,4096]{1,0:T(8,128)(2,1)}, bf16[80,4096]{1,0:T(8,128)(2,1)}, u32[]{:S(2)}, u32[]{:S(2)}) collective-permute-start(bf16[80,4096]{1,0:T(8,128)(2,1)} %get-tuple-element.51), channel_id=1, source_target_pairs={{0,2},{1,3},{2,0},{3,1},{4,6},{5,7},{6,4},{7,5},{8,10},{9,11},{10,... | collective-permute-start | bytes 1966088 | tf_op jit(solution)/shard_map/ppermute | solution.py:334
  30.6 1.5 %collective-permute-start.6 = (bf16[1024,128]{1,0:T(8,128)(2,1)S(1)}, bf16[1024,128]{1,0:T(8,128)(2,1)S(1)}, u32[]{:S(2)}, u32[]{:S(2)}) collective-permute-start(bf16[1024,128]{1,0:T(8,128)(2,1)S(1)} %copy-done.21), channel_id=1, source_target_pairs={{0,1},{1,0},{2,3},{3,2},{4,5},{5,4},{6,7},{7,6},{8,9},{9,8},{10,11... | collective-permute-start | bytes 786440 | tf_op jit(solution)/shard_map/ppermute | solution.py:334
  32.8 18.2 %collective-permute-start.7 = (bf16[1024,128]{1,0:T(8,128)(2,1)}, bf16[1024,128]{1,0:T(8,128)(2,1)}, u32[]{:S(2)}, u32[]{:S(2)}) collective-permute-start(bf16[1024,128]{1,0:T(8,128)(2,1)} %get-tuple-element.62), channel_id=1, source_target_pairs={{0,1},{1,0},{2,3},{3,2},{4,5},{5,4},{6,7},{7,6},{8,9},{9,8},{10,11... | collective-permute-start | bytes 786440 | tf_op jit(solution)/shard_map/ppermute | solution.py:334
  34.0 17.4 %copy-start.10 = (bf16[1024,128]{1,0:T(8,128)(2,1)S(1)}, bf16[1024,128]{1,0:T(8,128)(2,1)}, u32[]{:S(2)}) copy-start(bf16[1024,128]{1,0:T(8,128)(2,1)} %copy-done.9) | copy-start | bytes 786436
  34.0 17.4 %copy-start.12 = (bf16[1024,128]{1,0:T(8,128)(2,1)S(1)}, bf16[1024,128]{1,0:T(8,128)(2,1)}, u32[]{:S(2)}) copy-start(bf16[1024,128]{1,0:T(8,128)(2,1)} %copy-done.11) | copy-start | bytes 786436
  45.5 22.8 %copy-start.17 = (bf16[64,64,128]{2,1,0:T(8,128)(2,1)}, bf16[64,64,128]{2,1,0:T(8,128)(2,1)S(1)}, u32[]{:S(2)}) copy-start(bf16[64,64,128]{2,1,0:T(8,128)(2,1)S(1)} %get-tuple-element.54) | copy-start | bytes 3145732
  45.5 22.8 %copy-start.19 = (bf16[64,64,128]{2,1,0:T(8,128)(2,1)}, bf16[64,64,128]{2,1,0:T(8,128)(2,1)S(1)}, u32[]{:S(2)}) copy-start(bf16[64,64,128]{2,1,0:T(8,128)(2,1)S(1)} %get-tuple-element.53) | copy-start | bytes 3145732
  45.5 34.2 %copy-start.13 = (bf16[64,64,128]{2,1,0:T(8,128)(2,1)}, bf16[64,64,128]{2,1,0:T(8,128)(2,1)S(1)}, u32[]{:S(2)}) copy-start(bf16[64,64,128]{2,1,0:T(8,128)(2,1)S(1)} %get-tuple-element.77) | copy-start | bytes 3145732
  45.5 34.2 %copy-start.15 = (bf16[64,64,128]{2,1,0:T(8,128)(2,1)}, bf16[64,64,128]{2,1,0:T(8,128)(2,1)S(1)}, u32[]{:S(2)}) copy-start(bf16[64,64,128]{2,1,0:T(8,128)(2,1)S(1)} %get-tuple-element.76) | copy-start | bytes 3145732
  51.0 28.6 %collective-permute-start.14 = (bf16[80,4096]{1,0:T(8,128)(2,1)}, bf16[80,4096]{1,0:T(8,128)(2,1)S(1)}, u32[]{:S(2)}, u32[]{:S(2)}) collective-permute-start(bf16[80,4096]{1,0:T(8,128)(2,1)} %get-tuple-element.79), channel_id=1, source_target_pairs={{0,5},{1,4},{2,7},{3,6},{4,1},{5,0},{6,3},{7,2},{8,13},{9,12},{10,... | collective-permute-start | bytes 1966088 | tf_op jit(solution)/shard_map/ppermute | solution.py:334
  54.1 25.5 %collective-permute-start.15 = (bf16[80,4096]{1,0:T(8,128)(2,1)}, bf16[80,4096]{1,0:T(8,128)(2,1)S(1)}, u32[]{:S(2)}, u32[]{:S(2)}) collective-permute-start(bf16[80,4096]{1,0:T(8,128)(2,1)} %get-tuple-element.80), channel_id=1, source_target_pairs={{0,3},{1,2},{2,1},{3,0},{4,7},{5,6},{6,5},{7,4},{8,11},{9,10},{10,... | collective-permute-start | bytes 1966088 | tf_op jit(solution)/shard_map/ppermute | solution.py:334
  68.3 23.8 %collective-permute-start.10 = (bf16[48,4096]{1,0:T(8,128)(2,1)}, bf16[48,4096]{1,0:T(8,128)(2,1)S(1)}, u32[]{:S(2)}, u32[]{:S(2)}) collective-permute-start(bf16[48,4096]{1,0:T(8,128)(2,1)} %get-tuple-element.70), channel_id=1, source_target_pairs={{0,4},{1,5},{2,6},{3,7},{4,0},{5,1},{6,2},{7,3},{8,12},{9,13},{10,... | collective-permute-start | bytes 1179656 | tf_op jit(solution)/shard_map/ppermute | solution.py:334
  69.9 22.1 %collective-permute-start.11 = (bf16[48,4096]{1,0:T(8,128)(2,1)}, bf16[48,4096]{1,0:T(8,128)(2,1)S(1)}, u32[]{:S(2)}, u32[]{:S(2)}) collective-permute-start(bf16[48,4096]{1,0:T(8,128)(2,1)} %get-tuple-element.71), channel_id=1, source_target_pairs={{0,2},{1,3},{2,0},{3,1},{4,6},{5,7},{6,4},{7,5},{8,10},{9,11},{10,... | collective-permute-start | bytes 1179656 | tf_op jit(solution)/shard_map/ppermute | solution.py:334
  79.7 12.4 %copy-start.20 = (bf16[64,64,128]{2,1,0:T(8,128)(2,1)S(1)}, bf16[64,64,128]{2,1,0:T(8,128)(2,1)}, u32[]{:S(2)}) copy-start(bf16[64,64,128]{2,1,0:T(8,128)(2,1)} %copy-done.19) | copy-start | bytes 3145732
  80.2 8.4 %collective-permute-start.16 = (f32[64,128]{1,0:T(8,128)S(1)}, f32[64,128]{1,0:T(8,128)S(1)}, u32[]{:S(2)}, u32[]{:S(2)}) collective-permute-start(f32[64,128]{1,0:T(8,128)S(1)} %get-tuple-element.84), channel_id=1, source_target_pairs={{0,8},{1,9},{2,10},{3,11},{4,12},{5,13},{6,14},{7,15},{8,0},{9,1},... | collective-permute-start | bytes 98312 | tf_op jit(solution)/shard_map/ppermute | solution.py:334
  83.0 11.4 %collective-permute-start.18 = (bf16[32,4096]{1,0:T(8,128)(2,1)}, bf16[32,4096]{1,0:T(8,128)(2,1)S(1)}, u32[]{:S(2)}, u32[]{:S(2)}) collective-permute-start(bf16[32,4096]{1,0:T(8,128)(2,1)} %get-tuple-element.86), channel_id=1, source_target_pairs={{0,5},{1,4},{2,7},{3,6},{4,1},{5,0},{6,3},{7,2},{8,13},{9,12},{10,... | collective-permute-start | bytes 786440 | tf_op jit(solution)/shard_map/ppermute | solution.py:334
  84.6 9.7 %collective-permute-start.19 = (bf16[32,4096]{1,0:T(8,128)(2,1)}, bf16[32,4096]{1,0:T(8,128)(2,1)S(1)}, u32[]{:S(2)}, u32[]{:S(2)}) collective-permute-start(bf16[32,4096]{1,0:T(8,128)(2,1)} %get-tuple-element.87), channel_id=1, source_target_pairs={{0,3},{1,2},{2,1},{3,0},{4,7},{5,6},{6,5},{7,4},{8,11},{9,10},{10,... | collective-permute-start | bytes 786440 | tf_op jit(solution)/shard_map/ppermute | solution.py:334
  88.6 10.2 %collective-permute-start.17 = (f32[16,128]{1,0:T(8,128)S(1)}, f32[16,128]{1,0:T(8,128)S(1)}, u32[]{:S(2)}, u32[]{:S(2)}) collective-permute-start(f32[16,128]{1,0:T(8,128)S(1)} %slice_add_fusion), channel_id=1, source_target_pairs={{0,6},{1,7},{2,4},{3,5},{4,2},{5,3},{6,0},{7,1},{8,14},{9,15},{10,... | collective-permute-start | bytes 24584 | tf_op jit(solution)/shard_map/ppermute | solution.py:334
  92.5 5.2 %collective-permute-start.12 = (bf16[16,4096]{1,0:T(8,128)(2,1)}, bf16[16,4096]{1,0:T(8,128)(2,1)S(1)}, u32[]{:S(2)}, u32[]{:S(2)}) collective-permute-start(bf16[16,4096]{1,0:T(8,128)(2,1)} %get-tuple-element.74), channel_id=1, source_target_pairs={{0,5},{1,4},{2,7},{3,6},{4,1},{5,0},{6,3},{7,2},{8,13},{9,12},{10,... | collective-permute-start | bytes 393224 | tf_op jit(solution)/shard_map/ppermute | solution.py:334
  92.6 5.8 %collective-permute-start.13 = (bf16[16,4096]{1,0:T(8,128)(2,1)}, bf16[16,4096]{1,0:T(8,128)(2,1)S(1)}, u32[]{:S(2)}, u32[]{:S(2)}) collective-permute-start(bf16[16,4096]{1,0:T(8,128)(2,1)} %get-tuple-element.75), channel_id=1, source_target_pairs={{0,3},{1,2},{2,1},{3,0},{4,7},{5,6},{6,5},{7,4},{8,11},{9,10},{10,... | collective-permute-start | bytes 393224 | tf_op jit(solution)/shard_map/ppermute | solution.py:334
  94.8 4.1 %collective-permute-start.20 = (f32[16,128]{1,0:T(8,128)S(1)}, f32[16,128]{1,0:T(8,128)S(1)}, u32[]{:S(2)}, u32[]{:S(2)}) collective-permute-start(f32[16,128]{1,0:T(8,128)S(1)} %get-tuple-element.89), channel_id=1, source_target_pairs={{0,2},{1,3},{2,0},{3,1},{4,6},{5,7},{6,4},{7,5},{8,10},{9,11},{10,... | collective-permute-start | bytes 24584 | tf_op jit(solution)/shard_map/ppermute | solution.py:334
  95.9 3.7 %collective-permute-start.21 = (f32[16,128]{1,0:T(8,128)S(1)}, f32[16,128]{1,0:T(8,128)S(1)}, u32[]{:S(2)}, u32[]{:S(2)}) collective-permute-start(f32[16,128]{1,0:T(8,128)S(1)} %get-tuple-element.90), channel_id=1, source_target_pairs={{0,4},{1,5},{2,6},{3,7},{4,0},{5,1},{6,2},{7,3},{8,12},{9,13},{10,... | collective-permute-start | bytes 24584 | tf_op jit(solution)/shard_map/ppermute | solution.py:334
  99.5 1.2 %collective-permute-start.22 = (f32[8,128]{1,0:T(8,128)S(1)}, f32[8,128]{1,0:T(8,128)S(1)}, u32[]{:S(2)}, u32[]{:S(2)}) collective-permute-start(f32[8,128]{1,0:T(8,128)S(1)} %slice_select_fusion), channel_id=1, source_target_pairs={{0,1},{1,0},{2,3},{3,2},{4,5},{5,4},{6,7},{7,6},{8,9},{9,8},{10,11... | collective-permute-start | bytes 12296 | tf_op jit(solution)/shard_map/ppermute | solution.py:334
  (13 other events, 40.8 us)

commit v8 on v7

--- a/solution.py
+++ b/solution.py
@@ -419,7 +419,10 @@
         me, first_own, first_rights, (slab, 2 * slab), slab, [("all", 0, total)], [pieces[k][2] for k in second]
     )
     second_near = send(passed, second)
-    across = exchange(across + inner[3 * slab :], 6, devices)
+    (across,) = contract_rows(
+        me, [], [], (slab,), slab, [("own", 0, across), ("own", 3 * slab, inner)], (), [rest]
+    )
+    across = exchange(across, 6, devices)
     square = contract_rows(
         me, second_mid, second_rights, (slab, slab), slab, [("own", 0, rest), ("own", slab, inner)]
     )

time: 102 us -> 102 us (level)
  waiting for transfers between devices: 28.7 us -> 21.1 us
  local copies, waits for them, and re-layouts: 9.55 us -> 16.5 us
  Pallas kernels: 35.9 us -> 37.2 us
    ppermute x23, waiting for transfers between devices: 28.7 us -> 21.1 us  [exchange(): return lax.ppermute(value, 'tensor', [(i, i ^ k) for i in range(devices)])]
    unnamed x44 -> x52, local copies, waits for them, and re-layouts: 9.55 us -> 16.5 us
    pallas_call x4, Pallas kernels: 2.84 us -> 3.98 us  [contract(): pl.pallas_call(functools.partial(contract_kernel, count, begins, len(star...]
    pallas_call x5 -> x6, Pallas kernels: 3.58 us -> 3.72 us  [contract_rows(): pl.pallas_call(functools.partial(rows_kernel, count, rows, slab, kinds, l...]
  transfers between devices with their start and end apart: 23 -> 23, of which waited for: 11 -> 10; matrix products, arithmetic and copies ran while one was open for 0% -> 0% of each run, Pallas kernels for 34% -> 35%
where the time goes in v8:
time: 102 us; the launch traced here: 101 us
  Pallas kernels  37.2 us (36%)
  starting transfers between devices  25.8 us (25%)
  waiting for transfers between devices  21.1 us (21%)
  local copies, waits for them, and re-layouts  16.5 us (16%)
    ppermute x23, starting transfers between devices, exchange(): return lax.ppermute(value, 'tensor', [(i, i ^ k) for i in range(devices)])  25.8 us
    ppermute x23, waiting for transfers between devices, exchange(): return lax.ppermute(value, 'tensor', [(i, i ^ k) for i in range(devices)])  21.1 us
    unnamed x52, local copies, waits for them, and re-layouts  16.5 us
    pallas_call x1, Pallas kernels, projections(): pl.pallas_call(functools.partial(project_kernel, width, rows), grid=(step...  11.4 us
    pallas_call x2, Pallas kernels, products(): pl.pallas_call(functools.partial(product_kernel, slots, wanted, width, ch...  9.15 us
    pallas_call x1, Pallas kernels, turned_products(): pl.pallas_call(functools.partial(turned_product_kernel, slots, width, chu...  8.92 us
    pallas_call x4, Pallas kernels, contract(): pl.pallas_call(functools.partial(contract_kernel, count, begins, len(star...  3.98 us
    pallas_call x6, Pallas kernels, contract_rows(): pl.pallas_call(functools.partial(rows_kernel, count, rows, slab, kinds, l...  3.72 us
  transfers between devices with their start and end apart: 23, of which 10 were waited for; matrix products, arithmetic and copies ran while one was open for 0% of the time, Pallas kernels for 35%

profile of v8, /device:TPU:0, one launch (start us, length us, event | category | flops | bytes accessed | tf_op | source)
XLA Modules:
  0.0 101.4 jit_solution(15280041284073023281)
XLA Ops:
  0.0 2.0 %products.2 = (bf16[1024,128]{1,0:T(8,128)(2,1)S(1)}, bf16[1024,128]{1,0:T(8,128)(2,1)S(1)}) custom-call(s32[8,16]{1,0:T(8,128)} %bitcast.29, bf16[1,512,512]{2,1,0:T(8,128)(2,1)} %virt_hbm.5, bf16[1,8,4096,128]{3,2,1,0:T(8,128)(2,1)} %block_ref.1), custom_call_target="tpu_custom_call" | custom-call | flops 1 | bytes 1 | tf_op jit(solution)/shard_map/products/pallas_call | solution.py:104
  2.0 4.0 %collective-permute-start.9 = (bf16[1024,128]{1,0:T(8,128)(2,1)S(1)}, bf16[1024,128]{1,0:T(8,128)(2,1)S(1)}, u32[]{:S(2)}, u32[]{:S(2)}) collective-permute-start(bf16[1024,128]{1,0:T(8,128)(2,1)S(1)} %get-tuple-element.48.refs_0_), channel_id=1, source_target_pairs={{0,6},{1,7},{2,4},{3,5},{4,2},{5,3},{6,0},{7,1},{8,14},{9,15},{10,... | collective-permute-start | bytes 786440 | tf_op jit(solution)/shard_map/ppermute | solution.py:334
  6.1 7.2 %products.3 = (bf16[4096,128]{1,0:T(8,128)(2,1)}, bf16[1024,128]{1,0:T(8,128)(2,1)}, bf16[1024,128]{1,0:T(8,128)(2,1)}, bf16[1024,128]{1,0:T(8,128)(2,1)}, bf16[...) custom-call(s32[8,16]{1,0:T(8,128)} %bitcast.30, bf16[1,512,512]{2,1,0:T(8,128)(2,1)} %virt_hbm.5, ...), custom_call_target="tpu_custom_call" | custom-call | flops 1 | bytes 1 | tf_op jit(solution)/shard_map/products/pallas_call | solution.py:104
  13.8 2.6 %collective-permute-start.2 = (bf16[3072,128]{1,0:T(8,128)(2,1)}, bf16[3072,128]{1,0:T(8,128)(2,1)S(1)}, u32[]{:S(2)}, u32[]{:S(2)}) collective-permute-start(bf16[3072,128]{1,0:T(8,128)(2,1)} %get-tuple-element.55), channel_id=1, source_target_pairs={{0,6},{1,7},{2,4},{3,5},{4,2},{5,3},{6,0},{7,1},{8,14},{9,15},{10,... | collective-permute-start | bytes 2359304 | tf_op jit(solution)/shard_map/ppermute | solution.py:334
  16.5 1.2 %copy-done.1 = bf16[4096,128]{1,0:T(8,128)(2,1)S(1)} copy-done((bf16[4096,128]{1,0:T(8,128)(2,1)S(1)}, bf16[4096,128]{1,0:T(8,128)(2,1)}, u32[]{:S(2)}) %copy-start.1) | copy-done | bytes 1048600
  17.7 8.9 %turned_products.1 = (bf16[80,4096]{1,0:T(8,128)(2,1)}, bf16[48,4096]{1,0:T(8,128)(2,1)}, bf16[80,4096]{1,0:T(8,128)(2,1)}, bf16[32,4096]{1,0:T(8,128)(2,1)}, bf...) custom-call(s32[8,16]{1,0:T(8,128)} %bitcast.31, ...), custom_call_target="tpu_custom_call" | custom-call | flops 1 | bytes 1 | tf_op jit(solution)/shard_map/turned_products/pallas_call | solution.py:184
  26.6 1.7 %collective-permute-start = (bf16[80,4096]{1,0:T(8,128)(2,1)}, bf16[80,4096]{1,0:T(8,128)(2,1)}, u32[]{:S(2)}, u32[]{:S(2)}) collective-permute-start(bf16[80,4096]{1,0:T(8,128)(2,1)} %get-tuple-element.50), channel_id=1, source_target_pairs={{0,4},{1,5},{2,6},{3,7},{4,0},{5,1},{6,2},{7,3},{8,12},{9,13},{10,... | collective-permute-start | bytes 1966088 | tf_op jit(solution)/shard_map/ppermute | solution.py:334
  29.1 1.5 %collective-permute-start.1 = (bf16[80,4096]{1,0:T(8,128)(2,1)}, bf16[80,4096]{1,0:T(8,128)(2,1)}, u32[]{:S(2)}, u32[]{:S(2)}) collective-permute-start(bf16[80,4096]{1,0:T(8,128)(2,1)} %get-tuple-element.51), channel_id=1, source_target_pairs={{0,2},{1,3},{2,0},{3,1},{4,6},{5,7},{6,4},{7,5},{8,10},{9,11},{10,... | collective-permute-start | bytes 1966088 | tf_op jit(solution)/shard_map/ppermute | solution.py:334
  31.3 1.5 %collective-permute-done.6.refs_2_ = bf16[1024,128]{1,0:T(8,128)(2,1)S(1)} collective-permute-done((bf16[1024,128]{1,0:T(8,128)(2,1)S(1)}, bf16[1024,128]{1,0:T(8,128)(2,1)S(1)}, u32[]{:S(2)}, u32[]{:S(2)}) %collective-permute-start.6) | collective-permute-done | bytes 262176 | tf_op jit(solution)/shard_map/ppermute | solution.py:334
  33.7 1.1 %copy-done.7 = bf16[80,4096]{1,0:T(8,128)(2,1)S(1)} copy-done((bf16[80,4096]{1,0:T(8,128)(2,1)S(1)}, bf16[80,4096]{1,0:T(8,128)(2,1)}, u32[]{:S(2)}) %copy-start.7) | copy-done | bytes 655384
  34.8 11.4 %projections.1 = (bf16[64,64,128]{2,1,0:T(8,128)(2,1)}, bf16[64,64,128]{2,1,0:T(8,128)(2,1)}, bf16[64,64,128]{2,1,0:T(8,128)(2,1)S(1)}, bf16[64,64,128]{2,1,0:T(...) custom-call(s32[1]{0:T(128)} %bitcast.me_ref, ...), custom_call_target="tpu_custom_call" | custom-call | flops 1 | bytes 1 | tf_op jit(solution)/shard_map/projections/pallas_call | solution.py:239
  50.1 1.3 %copy-done.5 = bf16[64,64,128]{2,1,0:T(8,128)(2,1)S(1)} copy-done((bf16[64,64,128]{2,1,0:T(8,128)(2,1)S(1)}, bf16[64,64,128]{2,1,0:T(8,128)(2,1)}, u32[]{:S(2)}) %copy-start.5) | copy-done | bytes 1048600
  51.5 1.2 %copy-done.8 = bf16[64,64,128]{2,1,0:T(8,128)(2,1)S(1)} copy-done((bf16[64,64,128]{2,1,0:T(8,128)(2,1)S(1)}, bf16[64,64,128]{2,1,0:T(8,128)(2,1)}, u32[]{:S(2)}) %copy-start.8) | copy-done | bytes 1048600
  53.2 1.5 %copy-done.3 = bf16[64,64,128]{2,1,0:T(8,128)(2,1)S(1)} copy-done((bf16[64,64,128]{2,1,0:T(8,128)(2,1)S(1)}, bf16[64,64,128]{2,1,0:T(8,128)(2,1)}, u32[]{:S(2)}) %copy-start.3) | copy-done | bytes 1048600
  55.5 1.2 %copy-done = bf16[64,64,128]{2,1,0:T(8,128)(2,1)S(1)} copy-done((bf16[64,64,128]{2,1,0:T(8,128)(2,1)S(1)}, bf16[64,64,128]{2,1,0:T(8,128)(2,1)}, u32[]{:S(2)}) %copy-start) | copy-done | bytes 1048600
  59.6 1.4 %contract.6.refs_4_ = f32[128,128]{1,0:T(8,128)S(1)} custom-call(bf16[1024,128]{1,0:T(8,128)(2,1)S(1)} %copy-done.10, bf16[1024,128]{1,0:T(8,128)(2,1)S(1)} %copy-done.12, bf16[1024,128]{1,0:T(8,128)(2,1)S(1)} %copy-done.14, bf16[1024,128]{1,0:T(8,128)(2,1)} %collective-permute-done.7.refs_3_, bf16[4096,128]{1,0:T(8,128)(2,1)S(1)} %bitcast.10, ...), custom_call_target="tpu_custom_call" | custom-call | flops 1 | bytes 1 | tf_op jit(solution)/shard_map/contract/pallas_call | solution.py:275
  61.3 1.7 %contract.7.refs_4_ = f32[128,128]{1,0:T(8,128)S(1)} custom-call(bf16[3072,128]{1,0:T(8,128)(2,1)S(1)} %collective-permute-done.2.refs_0_, bf16[3072,128]{1,0:T(8,128)(2,1)} %collective-permute-done.3.refs_1_, bf16[4096,128]{1,0:T(8,128)(2,1)S(1)} %bitcast.17, bf16[4096,128]{1,0:T(8,128)(2,1)S(1)} %bitcast.15, f32[128,128]{1,0:T(8,128)S(1)} %contract.6.refs_4_), custom_call_target="tpu_custom_call" | custom-call | flops 1 | bytes 1 | tf_op jit(solution)/shard_map/contract/pallas_call | solution.py:275
  63.0 3.4 %collective-permute-done.refs_0_ = bf16[80,4096]{1,0:T(8,128)(2,1)} collective-permute-done((bf16[80,4096]{1,0:T(8,128)(2,1)}, bf16[80,4096]{1,0:T(8,128)(2,1)}, u32[]{:S(2)}, u32[]{:S(2)}) %collective-permute-start) | collective-permute-done | bytes 655392 | tf_op jit(solution)/shard_map/ppermute | solution.py:334
  66.5 1.9 %contract_rows.6 = (f32[80,128]{1,0:T(8,128)S(1)}, bf16[48,4096]{1,0:T(8,128)(2,1)}, bf16[48,4096]{1,0:T(8,128)(2,1)}) custom-call(s32[1]{0:T(128)} %bitcast.me_ref, bf16[80,4096]{1,0:T(8,128)(2,1)} %collective-permute-done.refs_0_, bf16[80,4096]{1,0:T(8,128)(2,1)} %collective-permute-done.1.refs_1_, ...), custom_call_target="tpu_custom_call", output_to_operand_aliasing={{1}: (6, {}), {2}: (7, {})} | custom-call | flops 20000000000 | bytes 1 | tf_op jit(solution)/shard_map/contract_rows/pallas_call | solution.py:318
  68.4 1.6 %collective-permute-start.10 = (bf16[48,4096]{1,0:T(8,128)(2,1)}, bf16[48,4096]{1,0:T(8,128)(2,1)S(1)}, u32[]{:S(2)}, u32[]{:S(2)}) collective-permute-start(bf16[48,4096]{1,0:T(8,128)(2,1)} %get-tuple-element.70), channel_id=1, source_target_pairs={{0,4},{1,5},{2,6},{3,7},{4,0},{5,1},{6,2},{7,3},{8,12},{9,13},{10,... | collective-permute-start | bytes 1179656 | tf_op jit(solution)/shard_map/ppermute | solution.py:334
  70.0 1.1 %collective-permute-start.11 = (bf16[48,4096]{1,0:T(8,128)(2,1)}, bf16[48,4096]{1,0:T(8,128)(2,1)S(1)}, u32[]{:S(2)}, u32[]{:S(2)}) collective-permute-start(bf16[48,4096]{1,0:T(8,128)(2,1)} %get-tuple-element.71), channel_id=1, source_target_pairs={{0,2},{1,3},{2,0},{3,1},{4,6},{5,7},{6,4},{7,5},{8,10},{9,11},{10,... | collective-permute-start | bytes 1179656 | tf_op jit(solution)/shard_map/ppermute | solution.py:334
  71.1 8.5 %collective-permute-done.14.refs_0_ = bf16[80,4096]{1,0:T(8,128)(2,1)S(1)} collective-permute-done((bf16[80,4096]{1,0:T(8,128)(2,1)}, bf16[80,4096]{1,0:T(8,128)(2,1)S(1)}, u32[]{:S(2)}, u32[]{:S(2)}) %collective-permute-start.14) | collective-permute-done | bytes 655392 | tf_op jit(solution)/shard_map/ppermute | solution.py:334
  80.2 2.8 %collective-permute-start.16 = (f32[64,128]{1,0:T(8,128)S(1)}, f32[64,128]{1,0:T(8,128)S(1)}, u32[]{:S(2)}, u32[]{:S(2)}) collective-permute-start(f32[64,128]{1,0:T(8,128)S(1)} %get-tuple-element.84), channel_id=1, source_target_pairs={{0,8},{1,9},{2,10},{3,11},{4,12},{5,13},{6,14},{7,15},{8,0},{9,1},... | collective-permute-start | bytes 98312 | tf_op jit(solution)/shard_map/ppermute | solution.py:334
  82.9 1.6 %collective-permute-start.18 = (bf16[32,4096]{1,0:T(8,128)(2,1)}, bf16[32,4096]{1,0:T(8,128)(2,1)S(1)}, u32[]{:S(2)}, u32[]{:S(2)}) collective-permute-start(bf16[32,4096]{1,0:T(8,128)(2,1)} %get-tuple-element.87), channel_id=1, source_target_pairs={{0,5},{1,4},{2,7},{3,6},{4,1},{5,0},{6,3},{7,2},{8,13},{9,12},{10,... | collective-permute-start | bytes 786440 | tf_op jit(solution)/shard_map/ppermute | solution.py:334
  84.6 1.2 %collective-permute-start.19 = (bf16[32,4096]{1,0:T(8,128)(2,1)}, bf16[32,4096]{1,0:T(8,128)(2,1)S(1)}, u32[]{:S(2)}, u32[]{:S(2)}) collective-permute-start(bf16[32,4096]{1,0:T(8,128)(2,1)} %get-tuple-element.88), channel_id=1, source_target_pairs={{0,3},{1,2},{2,1},{3,0},{4,7},{5,6},{6,5},{7,4},{8,11},{9,10},{10,... | collective-permute-start | bytes 786440 | tf_op jit(solution)/shard_map/ppermute | solution.py:334
  85.8 3.7 %collective-permute-done.10.refs_0_ = bf16[48,4096]{1,0:T(8,128)(2,1)S(1)} collective-permute-done((bf16[48,4096]{1,0:T(8,128)(2,1)}, bf16[48,4096]{1,0:T(8,128)(2,1)S(1)}, u32[]{:S(2)}, u32[]{:S(2)}) %collective-permute-start.10) | collective-permute-done | bytes 393248 | tf_op jit(solution)/shard_map/ppermute | solution.py:334
  90.0 2.1 %collective-permute-start.17 = (f32[16,128]{1,0:T(8,128)S(1)}, f32[16,128]{1,0:T(8,128)S(1)}, u32[]{:S(2)}, u32[]{:S(2)}) collective-permute-start(f32[16,128]{1,0:T(8,128)S(1)} %contract_rows.10), channel_id=1, source_target_pairs={{0,6},{1,7},{2,4},{3,5},{4,2},{5,3},{6,0},{7,1},{8,14},{9,15},{10,... | collective-permute-start | bytes 24584 | tf_op jit(solution)/shard_map/ppermute | solution.py:334
  92.1 1.2 %collective-permute-start.13 = (bf16[16,4096]{1,0:T(8,128)(2,1)S(1)}, bf16[16,4096]{1,0:T(8,128)(2,1)S(1)}, u32[]{:S(2)}, u32[]{:S(2)}) collective-permute-start(bf16[16,4096]{1,0:T(8,128)(2,1)S(1)} %copy-done.24), channel_id=1, source_target_pairs={{0,3},{1,2},{2,1},{3,0},{4,7},{5,6},{6,5},{7,4},{8,11},{9,10},{10,... | collective-permute-start | bytes 393224 | tf_op jit(solution)/shard_map/ppermute | solution.py:334
  93.3 1.0 %collective-permute-done.18.refs_0_ = bf16[32,4096]{1,0:T(8,128)(2,1)S(1)} collective-permute-done((bf16[32,4096]{1,0:T(8,128)(2,1)}, bf16[32,4096]{1,0:T(8,128)(2,1)S(1)}, u32[]{:S(2)}, u32[]{:S(2)}) %collective-permute-start.18) | collective-permute-done | bytes 262176 | tf_op jit(solution)/shard_map/ppermute | solution.py:334
  94.8 1.1 %collective-permute-start.20 = (f32[16,128]{1,0:T(8,128)S(1)}, f32[16,128]{1,0:T(8,128)S(1)}, u32[]{:S(2)}, u32[]{:S(2)}) collective-permute-start(f32[16,128]{1,0:T(8,128)S(1)} %get-tuple-element.89), channel_id=1, source_target_pairs={{0,2},{1,3},{2,0},{3,1},{4,6},{5,7},{6,4},{7,5},{8,10},{9,11},{10,... | collective-permute-start | bytes 24584 | tf_op jit(solution)/shard_map/ppermute | solution.py:334
  95.9 1.6 %collective-permute-start.21 = (f32[16,128]{1,0:T(8,128)S(1)}, f32[16,128]{1,0:T(8,128)S(1)}, u32[]{:S(2)}, u32[]{:S(2)}) collective-permute-start(f32[16,128]{1,0:T(8,128)S(1)} %get-tuple-element.90), channel_id=1, source_target_pairs={{0,4},{1,5},{2,6},{3,7},{4,0},{5,1},{6,2},{7,3},{8,12},{9,13},{10,... | collective-permute-start | bytes 24584 | tf_op jit(solution)/shard_map/ppermute | solution.py:334
  99.6 1.2 %collective-permute-done.22 = f32[8,128]{1,0:T(8,128)S(1)} collective-permute-done((f32[8,128]{1,0:T(8,128)S(1)}, f32[8,128]{1,0:T(8,128)S(1)}, u32[]{:S(2)}, u32[]{:S(2)}) %collective-permute-start.22) | collective-permute-done | bytes 4128 | tf_op jit(solution)/shard_map/ppermute | solution.py:334
  (83 shorter events, 15.5 us)
Async XLA Ops:
  2.0 14.4 %collective-permute-start.9 = (bf16[1024,128]{1,0:T(8,128)(2,1)S(1)}, bf16[1024,128]{1,0:T(8,128)(2,1)S(1)}, u32[]{:S(2)}, u32[]{:S(2)}) collective-permute-start(bf16[1024,128]{1,0:T(8,128)(2,1)S(1)} %get-tuple-element.48.refs_0_), channel_id=1, source_target_pairs={{0,6},{1,7},{2,4},{3,5},{4,2},{5,3},{6,0},{7,1},{8,14},{9,15},{10,... | collective-permute-start | bytes 786440 | tf_op jit(solution)/shard_map/ppermute | solution.py:334
  6.0 20.6 %collective-permute-start.8 = (bf16[1024,128]{1,0:T(8,128)(2,1)S(1)}, bf16[1024,128]{1,0:T(8,128)(2,1)S(1)}, u32[]{:S(2)}, u32[]{:S(2)}) collective-permute-start(bf16[1024,128]{1,0:T(8,128)(2,1)S(1)} %get-tuple-element.64), channel_id=1, source_target_pairs={{0,7},{1,6},{2,5},{3,4},{4,3},{5,2},{6,1},{7,0},{8,15},{9,14},{10,... | collective-permute-start | bytes 786440 | tf_op jit(solution)/shard_map/ppermute | solution.py:334
  13.2 15.2 %collective-permute-start.4 = (bf16[1024,128]{1,0:T(8,128)(2,1)}, bf16[1024,128]{1,0:T(8,128)(2,1)S(1)}, u32[]{:S(2)}, u32[]{:S(2)}) collective-permute-start(bf16[1024,128]{1,0:T(8,128)(2,1)} %get-tuple-element.59), channel_id=1, source_target_pairs={{0,1},{1,0},{2,3},{3,2},{4,5},{5,4},{6,7},{7,6},{8,9},{9,8},{10,11... | collective-permute-start | bytes 786440 | tf_op jit(solution)/shard_map/ppermute | solution.py:334
  13.5 17.1 %collective-permute-start.5 = (bf16[1024,128]{1,0:T(8,128)(2,1)}, bf16[1024,128]{1,0:T(8,128)(2,1)S(1)}, u32[]{:S(2)}, u32[]{:S(2)}) collective-permute-start(bf16[1024,128]{1,0:T(8,128)(2,1)} %get-tuple-element.60), channel_id=1, source_target_pairs={{0,1},{1,0},{2,3},{3,2},{4,5},{5,4},{6,7},{7,6},{8,9},{9,8},{10,11... | collective-permute-start | bytes 786440 | tf_op jit(solution)/shard_map/ppermute | solution.py:334
  13.8 47.2 %collective-permute-start.2 = (bf16[3072,128]{1,0:T(8,128)(2,1)}, bf16[3072,128]{1,0:T(8,128)(2,1)S(1)}, u32[]{:S(2)}, u32[]{:S(2)}) collective-permute-start(bf16[3072,128]{1,0:T(8,128)(2,1)} %get-tuple-element.55), channel_id=1, source_target_pairs={{0,6},{1,7},{2,4},{3,5},{4,2},{5,3},{6,0},{7,1},{8,14},{9,15},{10,... | collective-permute-start | bytes 2359304 | tf_op jit(solution)/shard_map/ppermute | solution.py:334
  16.4 44.9 %collective-permute-start.3 = (bf16[3072,128]{1,0:T(8,128)(2,1)}, bf16[3072,128]{1,0:T(8,128)(2,1)}, u32[]{:S(2)}, u32[]{:S(2)}) collective-permute-start(bf16[3072,128]{1,0:T(8,128)(2,1)} %get-tuple-element.56), channel_id=1, source_target_pairs={{0,7},{1,6},{2,5},{3,4},{4,3},{5,2},{6,1},{7,0},{8,15},{9,14},{10,... | collective-permute-start | bytes 2359304 | tf_op jit(solution)/shard_map/ppermute | solution.py:334
  17.7 13.6 %copy-start.23 = (bf16[1024,128]{1,0:T(8,128)(2,1)S(1)}, bf16[1024,128]{1,0:T(8,128)(2,1)}, u32[]{:S(2)}) copy-start(bf16[1024,128]{1,0:T(8,128)(2,1)} %get-tuple-element.61) | copy-start | bytes 786436
  17.7 32.4 %copy-start.2 = (bf16[4096,128]{1,0:T(8,128)(2,1)S(1)}, bf16[4096,128]{1,0:T(8,128)(2,1)}, u32[]{:S(2)}) copy-start(bf16[4096,128]{1,0:T(8,128)(2,1)} %get-tuple-element.49.refs_0_.refs_1_) | copy-start | bytes 3145732
  26.6 39.8 %collective-permute-start = (bf16[80,4096]{1,0:T(8,128)(2,1)}, bf16[80,4096]{1,0:T(8,128)(2,1)}, u32[]{:S(2)}, u32[]{:S(2)}) collective-permute-start(bf16[80,4096]{1,0:T(8,128)(2,1)} %get-tuple-element.50), channel_id=1, source_target_pairs={{0,4},{1,5},{2,6},{3,7},{4,0},{5,1},{6,2},{7,3},{8,12},{9,13},{10,... | collective-permute-start | bytes 1966088 | tf_op jit(solution)/shard_map/ppermute | solution.py:334
  29.1 37.3 %collective-permute-start.1 = (bf16[80,4096]{1,0:T(8,128)(2,1)}, bf16[80,4096]{1,0:T(8,128)(2,1)}, u32[]{:S(2)}, u32[]{:S(2)}) collective-permute-start(bf16[80,4096]{1,0:T(8,128)(2,1)} %get-tuple-element.51), channel_id=1, source_target_pairs={{0,2},{1,3},{2,0},{3,1},{4,6},{5,7},{6,4},{7,5},{8,10},{9,11},{10,... | collective-permute-start | bytes 1966088 | tf_op jit(solution)/shard_map/ppermute | solution.py:334
  31.3 1.5 %collective-permute-start.6 = (bf16[1024,128]{1,0:T(8,128)(2,1)S(1)}, bf16[1024,128]{1,0:T(8,128)(2,1)S(1)}, u32[]{:S(2)}, u32[]{:S(2)}) collective-permute-start(bf16[1024,128]{1,0:T(8,128)(2,1)S(1)} %copy-done.23), channel_id=1, source_target_pairs={{0,1},{1,0},{2,3},{3,2},{4,5},{5,4},{6,7},{7,6},{8,9},{9,8},{10,11... | collective-permute-start | bytes 786440 | tf_op jit(solution)/shard_map/ppermute | solution.py:334
  33.5 21.5 %collective-permute-start.7 = (bf16[1024,128]{1,0:T(8,128)(2,1)}, bf16[1024,128]{1,0:T(8,128)(2,1)}, u32[]{:S(2)}, u32[]{:S(2)}) collective-permute-start(bf16[1024,128]{1,0:T(8,128)(2,1)} %get-tuple-element.62), channel_id=1, source_target_pairs={{0,1},{1,0},{2,3},{3,2},{4,5},{5,4},{6,7},{7,6},{8,9},{9,8},{10,11... | collective-permute-start | bytes 786440 | tf_op jit(solution)/shard_map/ppermute | solution.py:334
  50.1 11.2 %copy-start.4 = (bf16[64,64,128]{2,1,0:T(8,128)(2,1)S(1)}, bf16[64,64,128]{2,1,0:T(8,128)(2,1)}, u32[]{:S(2)}) copy-start(bf16[64,64,128]{2,1,0:T(8,128)(2,1)} %get-tuple-element.58) | copy-start | bytes 3145732
  52.7 8.6 %copy-start.6 = (bf16[64,64,128]{2,1,0:T(8,128)(2,1)S(1)}, bf16[64,64,128]{2,1,0:T(8,128)(2,1)}, u32[]{:S(2)}) copy-start(bf16[64,64,128]{2,1,0:T(8,128)(2,1)} %get-tuple-element.57) | copy-start | bytes 3145732
  52.7 13.7 %copy-start.20 = (bf16[64,64,128]{2,1,0:T(8,128)(2,1)S(1)}, bf16[64,64,128]{2,1,0:T(8,128)(2,1)}, u32[]{:S(2)}) copy-start(bf16[64,64,128]{2,1,0:T(8,128)(2,1)} %copy-done.19) | copy-start | bytes 3145732
  52.7 13.7 %copy-start.22 = (bf16[64,64,128]{2,1,0:T(8,128)(2,1)S(1)}, bf16[64,64,128]{2,1,0:T(8,128)(2,1)}, u32[]{:S(2)}) copy-start(bf16[64,64,128]{2,1,0:T(8,128)(2,1)} %copy-done.21) | copy-start | bytes 3145732
  55.0 24.6 %collective-permute-start.14 = (bf16[80,4096]{1,0:T(8,128)(2,1)}, bf16[80,4096]{1,0:T(8,128)(2,1)S(1)}, u32[]{:S(2)}, u32[]{:S(2)}) collective-permute-start(bf16[80,4096]{1,0:T(8,128)(2,1)} %get-tuple-element.79), channel_id=1, source_target_pairs={{0,5},{1,4},{2,7},{3,6},{4,1},{5,0},{6,3},{7,2},{8,13},{9,12},{10,... | collective-permute-start | bytes 1966088 | tf_op jit(solution)/shard_map/ppermute | solution.py:334
  61.0 18.6 %collective-permute-start.15 = (bf16[80,4096]{1,0:T(8,128)(2,1)}, bf16[80,4096]{1,0:T(8,128)(2,1)S(1)}, u32[]{:S(2)}, u32[]{:S(2)}) collective-permute-start(bf16[80,4096]{1,0:T(8,128)(2,1)} %get-tuple-element.80), channel_id=1, source_target_pairs={{0,3},{1,2},{2,1},{3,0},{4,7},{5,6},{6,5},{7,4},{8,11},{9,10},{10,... | collective-permute-start | bytes 1966088 | tf_op jit(solution)/shard_map/ppermute | solution.py:334
  66.4 13.3 %copy-start.16 = (bf16[64,64,128]{2,1,0:T(8,128)(2,1)S(1)}, bf16[64,64,128]{2,1,0:T(8,128)(2,1)}, u32[]{:S(2)}) copy-start(bf16[64,64,128]{2,1,0:T(8,128)(2,1)} %copy-done.15) | copy-start | bytes 3145732
  66.4 13.2 %copy-start.18 = (bf16[64,64,128]{2,1,0:T(8,128)(2,1)S(1)}, bf16[64,64,128]{2,1,0:T(8,128)(2,1)}, u32[]{:S(2)}) copy-start(bf16[64,64,128]{2,1,0:T(8,128)(2,1)} %copy-done.17) | copy-start | bytes 3145732
  68.4 21.1 %collective-permute-start.10 = (bf16[48,4096]{1,0:T(8,128)(2,1)}, bf16[48,4096]{1,0:T(8,128)(2,1)S(1)}, u32[]{:S(2)}, u32[]{:S(2)}) collective-permute-start(bf16[48,4096]{1,0:T(8,128)(2,1)} %get-tuple-element.70), channel_id=1, source_target_pairs={{0,4},{1,5},{2,6},{3,7},{4,0},{5,1},{6,2},{7,3},{8,12},{9,13},{10,... | collective-permute-start | bytes 1179656 | tf_op jit(solution)/shard_map/ppermute | solution.py:334
  70.0 19.5 %collective-permute-start.11 = (bf16[48,4096]{1,0:T(8,128)(2,1)}, bf16[48,4096]{1,0:T(8,128)(2,1)S(1)}, u32[]{:S(2)}, u32[]{:S(2)}) collective-permute-start(bf16[48,4096]{1,0:T(8,128)(2,1)} %get-tuple-element.71), channel_id=1, source_target_pairs={{0,2},{1,3},{2,0},{3,1},{4,6},{5,7},{6,4},{7,5},{8,10},{9,11},{10,... | collective-permute-start | bytes 1179656 | tf_op jit(solution)/shard_map/ppermute | solution.py:334
  80.2 9.8 %collective-permute-start.16 = (f32[64,128]{1,0:T(8,128)S(1)}, f32[64,128]{1,0:T(8,128)S(1)}, u32[]{:S(2)}, u32[]{:S(2)}) collective-permute-start(f32[64,128]{1,0:T(8,128)S(1)} %get-tuple-element.84), channel_id=1, source_target_pairs={{0,8},{1,9},{2,10},{3,11},{4,12},{5,13},{6,14},{7,15},{8,0},{9,1},... | collective-permute-start | bytes 98312 | tf_op jit(solution)/shard_map/ppermute | solution.py:334
  82.9 11.4 %collective-permute-start.18 = (bf16[32,4096]{1,0:T(8,128)(2,1)}, bf16[32,4096]{1,0:T(8,128)(2,1)S(1)}, u32[]{:S(2)}, u32[]{:S(2)}) collective-permute-start(bf16[32,4096]{1,0:T(8,128)(2,1)} %get-tuple-element.87), channel_id=1, source_target_pairs={{0,5},{1,4},{2,7},{3,6},{4,1},{5,0},{6,3},{7,2},{8,13},{9,12},{10,... | collective-permute-start | bytes 786440 | tf_op jit(solution)/shard_map/ppermute | solution.py:334
  84.6 9.8 %collective-permute-start.19 = (bf16[32,4096]{1,0:T(8,128)(2,1)}, bf16[32,4096]{1,0:T(8,128)(2,1)S(1)}, u32[]{:S(2)}, u32[]{:S(2)}) collective-permute-start(bf16[32,4096]{1,0:T(8,128)(2,1)} %get-tuple-element.88), channel_id=1, source_target_pairs={{0,3},{1,2},{2,1},{3,0},{4,7},{5,6},{6,5},{7,4},{8,11},{9,10},{10,... | collective-permute-start | bytes 786440 | tf_op jit(solution)/shard_map/ppermute | solution.py:334
  90.0 2.1 %copy-start.25 = (bf16[16,4096]{1,0:T(8,128)(2,1)S(1)}, bf16[16,4096]{1,0:T(8,128)(2,1)}, u32[]{:S(2)}) copy-start(bf16[16,4096]{1,0:T(8,128)(2,1)} %get-tuple-element.74) | copy-start | bytes 393220
  90.0 8.1 %collective-permute-start.17 = (f32[16,128]{1,0:T(8,128)S(1)}, f32[16,128]{1,0:T(8,128)S(1)}, u32[]{:S(2)}, u32[]{:S(2)}) collective-permute-start(f32[16,128]{1,0:T(8,128)S(1)} %contract_rows.10), channel_id=1, source_target_pairs={{0,6},{1,7},{2,4},{3,5},{4,2},{5,3},{6,0},{7,1},{8,14},{9,15},{10,... | collective-permute-start | bytes 24584 | tf_op jit(solution)/shard_map/ppermute | solution.py:334
  92.1 5.6 %collective-permute-start.12 = (bf16[16,4096]{1,0:T(8,128)(2,1)S(1)}, bf16[16,4096]{1,0:T(8,128)(2,1)S(1)}, u32[]{:S(2)}, u32[]{:S(2)}) collective-permute-start(bf16[16,4096]{1,0:T(8,128)(2,1)S(1)} %copy-done.25), channel_id=1, source_target_pairs={{0,5},{1,4},{2,7},{3,6},{4,1},{5,0},{6,3},{7,2},{8,13},{9,12},{10,... | collective-permute-start | bytes 393224 | tf_op jit(solution)/shard_map/ppermute | solution.py:334
  92.1 5.6 %collective-permute-start.13 = (bf16[16,4096]{1,0:T(8,128)(2,1)S(1)}, bf16[16,4096]{1,0:T(8,128)(2,1)S(1)}, u32[]{:S(2)}, u32[]{:S(2)}) collective-permute-start(bf16[16,4096]{1,0:T(8,128)(2,1)S(1)} %copy-done.24), channel_id=1, source_target_pairs={{0,3},{1,2},{2,1},{3,0},{4,7},{5,6},{6,5},{7,4},{8,11},{9,10},{10,... | collective-permute-start | bytes 393224 | tf_op jit(solution)/shard_map/ppermute | solution.py:334
  94.8 3.7 %collective-permute-start.20 = (f32[16,128]{1,0:T(8,128)S(1)}, f32[16,128]{1,0:T(8,128)S(1)}, u32[]{:S(2)}, u32[]{:S(2)}) collective-permute-start(f32[16,128]{1,0:T(8,128)S(1)} %get-tuple-element.89), channel_id=1, source_target_pairs={{0,2},{1,3},{2,0},{3,1},{4,6},{5,7},{6,4},{7,5},{8,10},{9,11},{10,... | collective-permute-start | bytes 24584 | tf_op jit(solution)/shard_map/ppermute | solution.py:334
  95.9 3.7 %collective-permute-start.21 = (f32[16,128]{1,0:T(8,128)S(1)}, f32[16,128]{1,0:T(8,128)S(1)}, u32[]{:S(2)}, u32[]{:S(2)}) collective-permute-start(f32[16,128]{1,0:T(8,128)S(1)} %get-tuple-element.90), channel_id=1, source_target_pairs={{0,4},{1,5},{2,6},{3,7},{4,0},{5,1},{6,2},{7,3},{8,12},{9,13},{10,... | collective-permute-start | bytes 24584 | tf_op jit(solution)/shard_map/ppermute | solution.py:334
  99.5 1.2 %collective-permute-start.22 = (f32[8,128]{1,0:T(8,128)S(1)}, f32[8,128]{1,0:T(8,128)S(1)}, u32[]{:S(2)}, u32[]{:S(2)}) collective-permute-start(f32[8,128]{1,0:T(8,128)S(1)} %slice_select_fusion), channel_id=1, source_target_pairs={{0,1},{1,0},{2,3},{3,2},{4,5},{5,4},{6,7},{7,6},{8,9},{9,8},{10,11... | collective-permute-start | bytes 12296 | tf_op jit(solution)/shard_map/ppermute | solution.py:334
  (17 other events, 18.6 us)
